TPU v7x, 32 devices: a whole 2x2x4 slice. The times are simulated.
32 devices in a mesh: groups: 2 (over y), seq: 4 (over z), tp: 4 (over x, core).
Axes of the slice: x: 2, y: 2, z: 4, core: 2. Of those that a mesh axis runs over, the one named last changes fastest.
Arguments:
- query: bfloat16 [4096, 2048], P(('groups', 'seq'), 'tp'), parts along dimension 0, may hold values from -64 to 64
- key_head_rows: bfloat16 [4096, 512], P(('groups', 'seq'), 'tp'), parts along dimension 0, may hold values from -64 to 64
- value_head_rows: bfloat16 [4096, 512], P(('groups', 'seq'), 'tp'), parts along dimension 0, may hold values from -6 to 6
- output_gradient: bfloat16 [4096, 2048], P(('groups', 'seq'), 'tp'), parts along dimension 0, may hold values from -16 to 16
- doc_blocks: int32 [32, 8], P(('groups', 'seq')), parts along dimension 0, may hold values from 0 to 13, as said below
- w_query: bfloat16 [4096, 2048], P(None, 'tp'), may hold values from -0.5 to 0.5
- key_weight: bfloat16 [4096, 512], P(None, 'tp'), may hold values from -0.5 to 0.5
- value_weight: bfloat16 [4096, 512], P(None, 'tp'), may hold values from -0.5 to 0.5
Outputs:
- input_grad: bfloat16 [4096, 4096], P(('groups', 'seq'), 'tp'), parts along dimension 0
There are 2 independent parts, one for each index of `groups`. A program takes and returns all parts, laid end to end along the dimension named above; an argument that names none is the same for every part. Nothing has to cross between parts.
Inputs may be any that keep to these rules, and one draw needn't show every extreme that they name: `doc_blocks`: row b holds max(b - o, 0) for 8 distinct offsets o of 2 to 12; every row b that starts a shard of 512 positions uses the offset 12, and the last row uses the offset 2.
All inputs are finite; a program needn't handle non-finite values.
Results may differ from a plain program's by a relative error of at most 0.014.
Values may be sent and summed in bfloat16 or wider, within the bound.
No kernel may reach another device: no remote copies, remote signals or barrier semaphores. Data moves between devices by JAX's collectives and lax.ppermute only.
A program may use at most 128 MiB of HBM per device.

v0:
```python
import jax
import jax.numpy as jnp
from jax import lax
from jax.sharding import PartitionSpec as P

HEAD_WIDTH = 128
BLOCK_POSITIONS = 128
LISTED_COUNT = 8


def shifted(block, axis, distance):
    devices = range(lax.axis_size(axis))
    route = [(i - distance, i) for i in devices if i - distance in devices]
    return lax.ppermute(block, axis, route)


def body(
    query,
    key_head_rows,
    value_head_rows,
    output_gradient,
    doc_blocks,
    w_query,
    key_weight,
    value_weight,
):
    tok_rows = query.shape[0]
    heads_here = query.shape[1] // HEAD_WIDTH
    kv_here = key_head_rows.shape[1] // HEAD_WIDTH
    group_width = heads_here // kv_here
    blocks_here = tok_rows // BLOCK_POSITIONS
    listed_slot_count = LISTED_COUNT + 2
    reach_dev = min(8, lax.axis_size("seq") - 1)
    window_blocks = (reach_dev + 1) * blocks_here
    seq_place = lax.axis_index("seq")
    score_scale = HEAD_WIDTH ** (-0.5)
    key_value = jnp.stack([key_head_rows, value_head_rows])
    pieces = []
    for distance in range(reach_dev, 0, -1):
        pieces.append(shifted(key_value, "seq", distance))
    pieces.append(key_value)
    window = jnp.concatenate(pieces, axis=1)
    window = window.reshape(2, window_blocks, BLOCK_POSITIONS, kv_here, HEAD_WIDTH)
    offsets = jnp.arange(BLOCK_POSITIONS, dtype=jnp.int32)
    query_ids = seq_place * blocks_here + jnp.arange(blocks_here, dtype=jnp.int32)
    earlier = jnp.arange(LISTED_COUNT)[:, None] > jnp.arange(LISTED_COUNT)[None, :]
    repeated = jnp.any((doc_blocks[:, :, None] == doc_blocks[:, None, :]) & earlier[None], axis=2)
    listed_ok = (doc_blocks <= query_ids[:, None] - 2) & jnp.logical_not(repeated)
    slot_ids = jnp.concatenate([query_ids[:, None] - 1, query_ids[:, None], doc_blocks], axis=1)
    slot_ok = jnp.concatenate([query_ids[:, None] >= 1, query_ids[:, None] >= 0, listed_ok], axis=1)
    local_ids = jnp.clip(slot_ids - (seq_place - reach_dev) * blocks_here, 0, window_blocks - 1)
    fetched = jnp.take(window, local_ids.reshape(-1), axis=1).reshape(
        2, blocks_here, listed_slot_count * BLOCK_POSITIONS, kv_here, HEAD_WIDTH
    )
    key_block = fetched[0]
    value_block = fetched[1]
    query_pos = query_ids[:, None] * BLOCK_POSITIONS + offsets[None, :]
    key_pos = (slot_ids[:, :, None] * BLOCK_POSITIONS + offsets[None, None, :]).reshape(
        blocks_here, listed_slot_count * BLOCK_POSITIONS
    )
    in_reach = (key_pos[:, None, :] <= query_pos[:, :, None]) & (
        query_pos[:, :, None] - key_pos[:, None, :] < BLOCK_POSITIONS
    )
    far_slot = jnp.repeat(jnp.arange(listed_slot_count) >= 2, BLOCK_POSITIONS)
    allowed = jnp.repeat(slot_ok, BLOCK_POSITIONS, axis=1)[:, None, :] & (
        far_slot[None, None, :] | in_reach
    )
    allowed = allowed[:, None, None]
    query_block = query.reshape(blocks_here, BLOCK_POSITIONS, kv_here, group_width, HEAD_WIDTH)
    grad_block = output_gradient.reshape(
        blocks_here, BLOCK_POSITIONS, kv_here, group_width, HEAD_WIDTH
    )
    scores = (
        jnp.einsum("bqhgd,bkhd->bhgqk", query_block, key_block, preferred_element_type=jnp.float32)
        * score_scale
    )
    scores = jnp.where(allowed, scores, -jnp.inf)
    row_max = jnp.max(scores, axis=-1, keepdims=True)
    weights = jnp.where(allowed, jnp.exp(scores - row_max), 0.0)
    probability = weights / jnp.sum(weights, axis=-1, keepdims=True)
    prob_half = probability.astype(jnp.bfloat16)
    attended = jnp.einsum(
        "bhgqk,bkhd->bqhgd", prob_half, value_block, preferred_element_type=jnp.float32
    )
    row_delta = jnp.sum(grad_block.astype(jnp.float32) * attended, axis=-1)
    prob_grad = jnp.einsum(
        "bqhgd,bkhd->bhgqk", grad_block, value_block, preferred_element_type=jnp.float32
    )
    score_grad = probability * (prob_grad - jnp.transpose(row_delta, (0, 2, 3, 1))[..., None])
    score_half = score_grad.astype(jnp.bfloat16)
    query_grad = (
        jnp.einsum("bhgqk,bkhd->bqhgd", score_half, key_block, preferred_element_type=jnp.float32)
        * score_scale
    )
    key_gradient = (
        jnp.einsum("bhgqk,bqhgd->bkhd", score_half, query_block, preferred_element_type=jnp.float32)
        * score_scale
    )
    value_gradient = jnp.einsum(
        "bhgqk,bqhgd->bkhd", prob_half, grad_block, preferred_element_type=jnp.float32
    )
    feature_count = BLOCK_POSITIONS * kv_here * HEAD_WIDTH
    slot_grads = jnp.stack(
        [
            key_gradient.reshape(blocks_here, listed_slot_count, feature_count),
            value_gradient.reshape(blocks_here, listed_slot_count, feature_count),
        ],
        axis=2,
    )
    slot_grads = slot_grads.reshape(blocks_here * listed_slot_count, 2 * feature_count)
    window_grads = (
        jnp.zeros((window_blocks, 2 * feature_count), jnp.float32)
        .at[local_ids.reshape(-1)]
        .add(slot_grads)
    )
    window_grads = window_grads.reshape(reach_dev + 1, blocks_here, 2, feature_count)
    returned = window_grads[reach_dev]
    for distance in range(1, reach_dev + 1):
        returned = returned + shifted(
            window_grads[reach_dev - distance].astype(jnp.bfloat16), "seq", -distance
        ).astype(jnp.float32)
    key_gradient_sum = returned[:, 0].reshape(tok_rows, kv_here * HEAD_WIDTH).astype(jnp.bfloat16)
    value_gradient_sum = returned[:, 1].reshape(tok_rows, kv_here * HEAD_WIDTH).astype(jnp.bfloat16)
    query_sum = query_grad.astype(jnp.bfloat16).reshape(tok_rows, heads_here * HEAD_WIDTH)
    contract = (((1,), (1,)), ((), ()))
    grad_term = lax.dot_general(query_sum, w_query, contract, preferred_element_type=jnp.float32)
    grad_term = grad_term + lax.dot_general(
        key_gradient_sum, key_weight, contract, preferred_element_type=jnp.float32
    )
    grad_term = grad_term + lax.dot_general(
        value_gradient_sum, value_weight, contract, preferred_element_type=jnp.float32
    )
    input_grad = lax.psum_scatter(
        grad_term.astype(jnp.bfloat16), "tp", scatter_dimension=1, tiled=True
    )
    return input_grad


def solution(mesh):
    in_specs = (
        P(("groups", "seq"), "tp"),
        P(("groups", "seq"), "tp"),
        P(("groups", "seq"), "tp"),
        P(("groups", "seq"), "tp"),
        P(("groups", "seq"), None),
        P(None, "tp"),
        P(None, "tp"),
        P(None, "tp"),
    )
    out_specs = P(("groups", "seq"), "tp")
    return jax.shard_map(body, mesh=mesh, in_specs=in_specs, out_specs=out_specs, check_vma=False)
```

profile of v0, /device:TPU:0, one launch (start us, length us, event | category | flops | bytes accessed | tf_op | source)
XLA Modules:
  0.0 186.1 jit_solution(2233959382489369433)
XLA Ops:
  8.3 5.6 %collective-permute-start.2 = (bf16[2,512,128]{2,1,0:T(8,128)(2,1)}, bf16[2,512,128]{2,1,0:T(8,128)(2,1)}, u32[]{:S(2)}, u32[]{:S(2)}) collective-permute-start(bf16[2,512,128]{2,1,0:T(8,128)(2,1)} %pad_maximum_fusion.1), channel_id=1, source_target_pairs={{0,4},{4,8},{8,12},{1,5},{5,9},{9,13},{2,6},{6,10},{10,14},{3,7},{... | collective-permute-start | bytes 786440 | tf_op jit(solution)/shard_map/ppermute | solution.py:14
  14.0 4.5 %collective-permute-start.1 = (bf16[2,512,128]{2,1,0:T(8,128)(2,1)}, bf16[2,512,128]{2,1,0:T(8,128)(2,1)}, u32[]{:S(2)}, u32[]{:S(2)}) collective-permute-start(bf16[2,512,128]{2,1,0:T(8,128)(2,1)} %pad_maximum_fusion.1), channel_id=1, source_target_pairs={{0,8},{4,12},{1,9},{5,13},{2,10},{6,14},{3,11},{7,15},{16,24},{20,... | collective-permute-start | bytes 786440 | tf_op jit(solution)/shard_map/ppermute | solution.py:14
  18.5 2.0 %collective-permute-start = (bf16[2,512,128]{2,1,0:T(8,128)(2,1)}, bf16[2,512,128]{2,1,0:T(8,128)(2,1)}, u32[]{:S(2)}, u32[]{:S(2)}) collective-permute-start(bf16[2,512,128]{2,1,0:T(8,128)(2,1)} %pad_maximum_fusion.1), channel_id=1, source_target_pairs={{0,12},{1,13},{2,14},{3,15},{16,28},{17,29},{18,30},{19,31}} | collective-permute-start | bytes 786440 | tf_op jit(solution)/shard_map/ppermute | solution.py:14
  23.5 2.2 %fusion.28 = pred[4,128,1280]{1,2,0:T(8,128)(4,1)S(1)} fusion(s32[4,128]{1,0:T(4,128)S(1)} %iota_add_fusion, s32[4,1280]{1,0:T(4,128)S(1)} %bitcast_add_fusion, pred[1280]{0:T(1024)(128)(4,1)S(1)} %broadcast_bitcast_fusion.2, pred[4,1280]{1,0:T(4,128)(4,1)S(1)} %bitcast.187), kind=kLoop, calls=%fused_computation.29 | loop fusion | flops 3932160 | bytes 684288 | tf_op jit(solution)/shard_map/and | solution.py:65
  25.8 2.0 %reshape.265 = bf16[4,128,4,128]{3,2,1,0:T(4,128)(2,1)} reshape(bf16[512,512]{1,0:T(8,128)(2,1)} %param.11) | data formatting | bytes 1048576 | tf_op jit(solution)/shard_map/reshape.22
  32.9 2.6 %gather_fusion = bf16[40,2,128,128]{3,2,1,0:T(8,128)(2,1)} fusion(bf16[2,16,128,128]{3,2,1,0:T(8,128)(2,1)S(1)} %bitcast.172, s32[1024]{0:T(1024)S(1)} %pad_clamp_fusion), kind=kCustom, calls=%fused_computation | custom fusion | bytes 5243040 | tf_op jit(solution)/shard_map/jit(_take)/gather | solution.py:52
  35.5 2.0 %bitcast_select_fusion.1 = bf16[2,40,128,1,128]{4,2,0,1,3:T(8,128)(2,1)S(1)} fusion(bf16[40,2,128,128]{3,2,1,0:T(8,128)(2,1)} %gather_fusion, pred[40]{0:T(512)(128)(4,1)S(1)} %compare_and_fusion), kind=kLoop, calls=%fused_computation.25 | loop fusion | flops 1310720 | bytes 5242920 | tf_op jit(solution)/shard_map/jit(_take)/select_n | solution.py:52
  39.2 2.6 %fusion.4 = f32[4,4,128]{2,1,0:T(4,128)S(1)} fusion(f32[4,1280,128,4]{2,1,3,0:T(8,128)S(1)} %get-tuple-element.15, f32[4,4,128]{2,1,0:T(4,128)S(1)} %get-tuple-element.14, pred[4,128,1280]{1,2,0:T(8,128)(4,1)S(1)} %fusion.28), kind=kLoop, calls=%fused_computation.11 | loop fusion | flops 13105152 | bytes 11157504 | tf_op jit(solution)/shard_map/reduce_sum | solution.py:80
  41.8 4.5 %fusion.14 = f32[4,1280,1,128]{3,1,0,2:T(8,128)} fusion(bf16[4,128,4,128]{3,2,1,0:T(4,128)(2,1)S(1)} %copy-done.4, f32[4,4,128]{2,1,0:T(4,128)S(1)} %fusion.4, f32[4,4,128]{2,1,0:T(4,128)S(1)} %get-tuple-element.14, f32[4,1280,128,4]{2,1,3,0:T(8,128)S(1)} %get-tuple-element.15, pred[4,128,1280]{1,2,0:T(8,128)(4,1)S(1)} %fusion.28), kind=kOutput, calls=%fused_computation.21 | convolution fusion | flops 686817280 | bytes 14303232 | tf_op jit(solution)/shard_map/bhgqk,bqhgd->bkhd/dot_general | solution.py:99
  46.3 3.3 %fusion.44 = f32[4,128,4]{1,2,0:T(4,128)S(1)} fusion(f32[4,128,1,4,128]{1,4,3,0,2:T(8,128)S(1)} %copy-done.2, bf16[4,1280,128,1]{2,1,3,0:T(8,128)(2,1)S(1)} %bitcast.178, f32[4,4,128]{2,1,0:T(4,128)S(1)} %fusion.4, f32[4,4,128]{2,1,0:T(4,128)S(1)} %get-tuple-element.14, f32[4,1280,128,4]{2,1,3,0:T(8,128)S(1)} %get-tuple-element.15, ...), kind=kOutput, calls=%fused_computation.35 | convolution fusion | flops 687339520 | bytes 13524992 | tf_op jit(solution)/shard_map/bhgqk,bkhd->bqhgd/dot_general | solution.py:82
  49.6 4.2 %fusion.1 = bf16[4,1,4,128,1280]{3,4,2,0,1:T(8,128)(2,1)S(1)} fusion(bf16[4,1280,128,1]{2,1,3,0:T(8,128)(2,1)S(1)} %bitcast.179, f32[4,4,128]{2,1,0:T(4,128)S(1)} %bitcast.188, f32[4,4,128]{2,1,0:T(4,128)S(1)} %fusion.4, f32[4,4,128]{2,1,0:T(4,128)S(1)} %get-tuple-element.14, f32[4,1280,128,4]{2,1,3,0:T(8,128)S(1)} %get-tuple-element.15, ...), kind=kOutput, calls=%fused_computation.4 | convolution fusion | flops 692060160 | bytes 18243584 | tf_op jit(solution)/shard_map/bqhgd,bkhd->bhgqk/dot_general | solution.py:86
  54.8 3.1 %fusion.23 = f32[4,1280,1,128]{3,1,0,2:T(8,128)} fusion(bf16[4,1,4,128,1280]{3,4,2,0,1:T(8,128)(2,1)S(1)} %fusion.1, bf16[4,128,4,128]{3,2,1,0:T(4,128)(2,1)S(1)} %reshape.263), kind=kOutput, calls=%fused_computation.24 | convolution fusion | flops 671744000 | bytes 8388608 | tf_op jit(solution)/shard_map/bhgqk,bqhgd->bkhd/dot_general | solution.py:96
  58.9 3.5 %stack_reshape.6 = f32[4,10,1,16384]{3,1,0,2:T(8,128)} reshape(f32[4,1280,1,128]{3,1,0,2:T(8,128)} %fusion.23) | data formatting | bytes 5242880 | tf_op jit(solution)/shard_map/stack;reshape | solution.py:103
  62.4 3.5 %stack_reshape.7 = f32[4,10,1,16384]{3,1,0,2:T(8,128)} reshape(f32[4,1280,1,128]{3,1,0,2:T(8,128)} %fusion.14) | data formatting | bytes 5242880 | tf_op jit(solution)/shard_map/stack;reshape | solution.py:103
  66.0 7.5 %pad_maximum_fusion = f32[4,10,2,16384]{3,1,0,2:T(8,128)} fusion(f32[4,10,1,16384]{3,1,0,2:T(8,128)} %stack_reshape.7, f32[4,10,1,16384]{3,1,0,2:T(8,128)} %stack_reshape.6), kind=kLoop, calls=%fused_computation.8 | loop fusion | flops 1310720 | bytes 10485760 | tf_op jit(solution)/shard_map/stack | solution.py:103
  73.5 7.4 %copy.38 = f32[4,10,2,16384]{3,2,1,0:T(2,128)S(1)} copy(f32[4,10,2,16384]{3,1,0,2:T(8,128)} %pad_maximum_fusion) | data formatting | bytes 10485760 | tf_op jit(solution)/shard_map/stack | solution.py:103
  80.9 5.3 %copy.54 = f32[5,8,2,16384]{3,1,2,0:T(8,128)} copy(f32[5,8,2,16384]{3,2,1,0:T(2,128)S(1)} %bitcast.171) | data formatting | bytes 10485760
  86.2 8.8 %scatter_custom_fusion = f32[16,32768]{1,0:T(8,128)S(1)} fusion(s32[40]{0:T(128)S(1)} %fusion.60, f32[40,32768]{1,0:T(8,128)} %bitcast.175, f32[]{:T(128)} %constant.54.clone.1), kind=kCustom, calls=%fused_computation.37 | custom fusion | flops 1310720 | bytes 2097664 | tf_op jit(solution)/shard_map/scatter-add | solution.py:114
  99.5 6.7 %fusion.49 = f32[512,4096]{1,0:T(8,128)} fusion(bf16[4096,512]{1,0:T(8,128)(2,1)S(1)} %copy-done.1, bf16[64,8,4,128]{3,2,1,0:T(4,128)(2,1)} %bitcast.176), kind=kOutput, calls=%fused_computation.39 | convolution fusion | flops 2147483648 | bytes 13107200 | tf_op jit(solution)/shard_map/dot_general | solution.py:126
  106.3 6.5 %collective-permute-done.5 = bf16[4,2,16384]{2,0,1:T(4,128)(2,1)S(1)} collective-permute-done((bf16[4,2,16384]{2,0,1:T(4,128)(2,1)S(1)}, bf16[4,2,16384]{2,0,1:T(4,128)(2,1)S(1)}, u32[]{:S(2)}, u32[]{:S(2)}) %collective-permute-start.5) | collective-permute-done | bytes 262176 | tf_op jit(solution)/shard_map/ppermute | solution.py:14
  112.8 2.3 %collective-permute-done.3 = bf16[4,2,16384]{2,0,1:T(4,128)(2,1)S(1)} collective-permute-done((bf16[4,2,16384]{2,0,1:T(4,128)(2,1)S(1)}, bf16[4,2,16384]{2,0,1:T(4,128)(2,1)S(1)}, u32[]{:S(2)}, u32[]{:S(2)}) %collective-permute-start.3) | collective-permute-done | bytes 262176 | tf_op jit(solution)/shard_map/ppermute | solution.py:14
  115.1 12.4 %collective-permute-done.4 = bf16[4,2,16384]{2,0,1:T(4,128)(2,1)S(1)} collective-permute-done((bf16[4,2,16384]{2,0,1:T(4,128)(2,1)S(1)}, bf16[4,2,16384]{2,0,1:T(4,128)(2,1)S(1)}, u32[]{:S(2)}, u32[]{:S(2)}) %collective-permute-start.4) | collective-permute-done | bytes 262176 | tf_op jit(solution)/shard_map/ppermute | solution.py:14
  129.5 6.8 %add_convert_fusion = bf16[512,4096]{1,0:T(8,128)(2,1)} fusion(f32[512,4096]{1,0:T(8,128)} %fusion.49, f32[512,4096]{1,0:T(8,128)S(1)} %fusion.68, bf16[512,128]{1,0:T(8,128)(2,1)S(1)} %convert_element_type.75, bf16[4096,128]{1,0:T(8,128)(2,1)S(1)} %copy-done.3), kind=kOutput, calls=%fused_computation.9 | convolution fusion | flops 543162368 | bytes 22151168 | tf_op jit(solution)/shard_map/dot_general | solution.py:130
  136.4 42.9 %reduce-scatter.2.cloned.1.call-done = bf16[512,1024]{1,0:T(8,128)(2,1)} async-done(((bf16[512,4096]{1,0:T(8,128)(2,1)}), bf16[512,1024]{1,0:T(8,128)(2,1)}) %reduce-scatter.2.cloned.1.call-update) | async-done | bytes 1048592 | tf_op jit(solution)/shard_map/reduce_scatter | solution.py:133
  (60 shorter events, 20.3 us)
Async XLA Ops:
  6.5 121.7 %copy-start = (bf16[4096,128]{1,0:T(8,128)(2,1)S(1)}, bf16[4096,128]{1,0:T(8,128)(2,1)}, u32[]{:S(2)}) copy-start(bf16[4096,128]{1,0:T(8,128)(2,1)} %param.14) | copy-start | bytes 3145732
  6.5 25.2 %copy-start.5 = (bf16[512,128]{1,0:T(8,128)(2,1)S(1)}, bf16[512,128]{1,0:T(8,128)(2,1)}, u32[]{:S(2)}) copy-start(bf16[512,128]{1,0:T(8,128)(2,1)} %param.10) | copy-start | bytes 393220
  6.5 25.2 %copy-start.6 = (bf16[512,128]{1,0:T(8,128)(2,1)S(1)}, bf16[512,128]{1,0:T(8,128)(2,1)}, u32[]{:S(2)}) copy-start(bf16[512,128]{1,0:T(8,128)(2,1)} %param.9) | copy-start | bytes 393220
  6.5 172.7 %reduce-scatter.2.cloned.1.call-start = ((), (), s32[]{:S(2)}) async-start(), calls=%async_computation.1 | async-start | bytes 5242880 | tf_op jit(solution)/shard_map/reduce_scatter | solution.py:133
  8.3 23.3 %collective-permute-start.2 = (bf16[2,512,128]{2,1,0:T(8,128)(2,1)}, bf16[2,512,128]{2,1,0:T(8,128)(2,1)}, u32[]{:S(2)}, u32[]{:S(2)}) collective-permute-start(bf16[2,512,128]{2,1,0:T(8,128)(2,1)} %pad_maximum_fusion.1), channel_id=1, source_target_pairs={{0,4},{4,8},{8,12},{1,5},{5,9},{9,13},{2,6},{6,10},{10,14},{3,7},{... | collective-permute-start | bytes 786440 | tf_op jit(solution)/shard_map/ppermute | solution.py:14
  14.0 17.7 %collective-permute-start.1 = (bf16[2,512,128]{2,1,0:T(8,128)(2,1)}, bf16[2,512,128]{2,1,0:T(8,128)(2,1)}, u32[]{:S(2)}, u32[]{:S(2)}) collective-permute-start(bf16[2,512,128]{2,1,0:T(8,128)(2,1)} %pad_maximum_fusion.1), channel_id=1, source_target_pairs={{0,8},{4,12},{1,9},{5,13},{2,10},{6,14},{3,11},{7,15},{16,24},{20,... | collective-permute-start | bytes 786440 | tf_op jit(solution)/shard_map/ppermute | solution.py:14
  18.5 13.2 %collective-permute-start = (bf16[2,512,128]{2,1,0:T(8,128)(2,1)}, bf16[2,512,128]{2,1,0:T(8,128)(2,1)}, u32[]{:S(2)}, u32[]{:S(2)}) collective-permute-start(bf16[2,512,128]{2,1,0:T(8,128)(2,1)} %pad_maximum_fusion.1), channel_id=1, source_target_pairs={{0,12},{1,13},{2,14},{3,15},{16,28},{17,29},{18,30},{19,31}} | collective-permute-start | bytes 786440 | tf_op jit(solution)/shard_map/ppermute | solution.py:14
  39.2 2.6 %copy-start.4 = (bf16[4,128,4,128]{3,2,1,0:T(4,128)(2,1)S(1)}, bf16[4,128,4,128]{3,2,1,0:T(4,128)(2,1)}, u32[]{:S(2)}) copy-start(bf16[4,128,4,128]{3,2,1,0:T(4,128)(2,1)} %reshape.265) | copy-start | bytes 1572868
  41.8 4.5 %copy-start.2 = (f32[4,128,1,4,128]{1,4,3,0,2:T(8,128)S(1)}, f32[4,128,1,4,128]{1,4,3,0,2:T(8,128)}, u32[]{:S(2)}) copy-start(f32[4,128,1,4,128]{1,4,3,0,2:T(8,128)} %copy.32) | copy-start | bytes 3145732
  95.0 4.5 %copy-start.1 = (bf16[4096,512]{1,0:T(8,128)(2,1)S(1)}, bf16[4096,512]{1,0:T(8,128)(2,1)}, u32[]{:S(2)}) copy-start(bf16[4096,512]{1,0:T(8,128)(2,1)} %param.13) | copy-start | bytes 12582916
  95.4 17.4 %collective-permute-start.5 = (bf16[4,2,16384]{2,0,1:T(4,128)(2,1)S(1)}, bf16[4,2,16384]{2,0,1:T(4,128)(2,1)S(1)}, u32[]{:S(2)}, u32[]{:S(2)}) collective-permute-start(bf16[4,2,16384]{2,0,1:T(4,128)(2,1)S(1)} %bitcast.186), channel_id=1, source_target_pairs={{12,0},{13,1},{14,2},{15,3},{28,16},{29,17},{30,18},{31,19}} | collective-permute-start | bytes 786440 | tf_op jit(solution)/shard_map/ppermute | solution.py:14
  96.9 18.2 %collective-permute-start.3 = (bf16[4,2,16384]{2,0,1:T(4,128)(2,1)S(1)}, bf16[4,2,16384]{2,0,1:T(4,128)(2,1)S(1)}, u32[]{:S(2)}, u32[]{:S(2)}) collective-permute-start(bf16[4,2,16384]{2,0,1:T(4,128)(2,1)S(1)} %bitcast.185), channel_id=1, source_target_pairs={{4,0},{8,4},{12,8},{5,1},{9,5},{13,9},{6,2},{10,6},{14,10},{7,3},{... | collective-permute-start | bytes 786440 | tf_op jit(solution)/shard_map/ppermute | solution.py:14
  98.2 29.3 %collective-permute-start.4 = (bf16[4,2,16384]{2,0,1:T(4,128)(2,1)S(1)}, bf16[4,2,16384]{2,0,1:T(4,128)(2,1)S(1)}, u32[]{:S(2)}, u32[]{:S(2)}) collective-permute-start(bf16[4,2,16384]{2,0,1:T(4,128)(2,1)S(1)} %bitcast.184), channel_id=1, source_target_pairs={{8,0},{12,4},{9,1},{13,5},{10,2},{14,6},{11,3},{15,7},{24,16},{28,... | collective-permute-start | bytes 786440 | tf_op jit(solution)/shard_map/ppermute | solution.py:14
  128.2 1.3 copy-start.3
Sparse Core Ops, SparseCore 0:
  136.5 42.7 reduce-scatter.1
where the time goes:
time: 187 us; the launch traced here: 186 us
  waiting for transfers between devices  64.1 us (34%)
  matrix products  32.3 us (17%)
  local copies, waits for them, and re-layouts  30.6 us (16%)
  other arithmetic  29.2 us (16%)
  starting transfers between devices  16.3 us (9%)
  between operations  13.7 us (7%)
    reduce_scatter x1, waiting for transfers between devices, body(): lax.psum_scatter(grad_term.astype(jnp.bfloat16), 'tp', scatter_dimension=...  42.9 us
    ppermute x6, waiting for transfers between devices, shifted(): return lax.ppermute(block, axis, route)  21.2 us
    ppermute x6, starting transfers between devices, shifted(): return lax.ppermute(block, axis, route)  16.3 us
    another operation x3, local copies, waits for them, and re-layouts, body(): jnp.stack([key_gradient.reshape(blocks_here, listed_slot_count, feature_c...  14.5 us
    scatter-add x1, other arithmetic, body(): window_grads = jnp.zeros((window_blocks, 2 * feature_count), jnp.float32)...  8.81 us
    another operation x1, other arithmetic, body(): jnp.stack([key_gradient.reshape(blocks_here, listed_slot_count, feature_c...  7.51 us
    dot_general x1, matrix products, body(): lax.dot_general(value_gradient_sum, value_weight, contract, preferred_ele...  6.83 us
    dot_general x1, matrix products, body(): lax.dot_general(query_sum, w_query, contract, preferred_element_type=jnp....  6.66 us
  transfers between devices with their start and end apart: 7, of which 4 were waited for; matrix products, arithmetic and copies ran while one was open for 10% of the time, Pallas kernels for 0%

commit v1 on v0

v1 whole, which is shorter than its diff:
```python
import functools

import jax
import jax.numpy as jnp
from jax import lax
from jax.experimental import pallas as pl
from jax.experimental.pallas import tpu as pltpu
from jax.sharding import PartitionSpec as P

HEAD_WIDTH = 128
BLOCK = 128
SCALE = HEAD_WIDTH ** (-0.5)
SCALE_LOG2 = SCALE * 1.4426950408889634
LOWEST = -1e30
NT = (((1,), (1,)), ((), ()))


def shifted(block, axis, distance):
    devices = range(lax.axis_size(axis))
    route = [(i - distance, i) for i in devices if i - distance in devices]
    return lax.ppermute(block, axis, route)


def swapped(block, axis, bits):
    return lax.ppermute(block, axis, [(i, i ^ bits) for i in range(lax.axis_size(axis))])


def key_range(distance, i, blocks, reach):
    if distance == 0:
        return 0, i + 1
    if distance == reach:
        return i, blocks
    return 0, blocks


def lane_range(distance, j, blocks, reach):
    if distance == 0:
        return j, blocks
    if distance == reach:
        return 0, j + 1
    return 0, blocks


def stack_heads(rows_ref, stack_ref, blocks, heads):
    for i in range(blocks):
        for h in range(heads):
            at = (i * heads + h) * BLOCK
            stack_ref[at : at + BLOCK, :] = rows_ref[
                i * BLOCK : (i + 1) * BLOCK, h * HEAD_WIDTH : (h + 1) * HEAD_WIDTH
            ]


def band_keep(offset, lanes):
    key_at = lax.broadcasted_iota(jnp.int32, (BLOCK, lanes), 0)
    query_at = lax.broadcasted_iota(jnp.int32, (BLOCK, lanes), 1) % BLOCK
    return key_at <= query_at if offset == 0 else key_at > query_at


def fold(tile, op):
    rows = tile.shape[0]
    total = tile[0:8]
    for at in range(8, rows, 8):
        total = op(total, tile[at : at + 8])
    return total


def tiles_of(distances, i, blocks, reach):
    return [
        (c, d, j)
        for c, d in enumerate(distances)
        for j in range(*key_range(d, i, blocks, reach))
    ]


def score_pass(i, distances, blocks, reach, flag_ref, key_refs, value_refs, query_i, grad_i, s_ref, g_ref):
    rows = blocks * BLOCK
    top = None
    for c, d in enumerate(distances):
        low, high = key_range(d, i, blocks, reach)
        span = slice(low * BLOCK, high * BLOCK)
        at = slice(c * rows + low * BLOCK, c * rows + high * BLOCK)
        s_ref[at, :] = lax.dot_general(key_refs[c][span, :], query_i, NT, preferred_element_type=jnp.float32)
        g_ref[at, :] = lax.dot_general(value_refs[c][span, :], grad_i, NT, preferred_element_type=jnp.float32)
    for c, d, j in tiles_of(distances, i, blocks, reach):
        at = slice(c * rows + j * BLOCK, c * rows + (j + 1) * BLOCK)
        offset = d * blocks + i - j
        tile = s_ref[at, :]
        if offset < 2:
            tile = jnp.where(band_keep(offset, tile.shape[1]), tile, LOWEST)
            s_ref[at, :] = tile
        part = fold(tile, jnp.maximum)
        if offset > 0:
            part = jnp.where(flag_ref[i, d * blocks + j] != 0, part, LOWEST)
        top = part if top is None else jnp.maximum(top, part)
    return jnp.max(top, axis=0, keepdims=True)


def shift_of(flag_ref, i, d, j, blocks, base):
    if d * blocks + i - j == 0:
        return base
    return jnp.where(flag_ref[i, d * blocks + j] != 0, base, -LOWEST)


def weight_pass(i, distances, blocks, reach, flag_ref, s_ref, g_ref, base, keep):
    rows = blocks * BLOCK
    total = dot_total = None
    for c, d, j in tiles_of(distances, i, blocks, reach):
        at = slice(c * rows + j * BLOCK, c * rows + (j + 1) * BLOCK)
        weights = jnp.exp2(s_ref[at, :] * SCALE_LOG2 - shift_of(flag_ref, i, d, j, blocks, base))
        if keep:
            s_ref[at, :] = weights
        part = fold(weights, jnp.add)
        dot_part = fold(weights * g_ref[at, :], jnp.add)
        total = part if total is None else total + part
        dot_total = dot_part if dot_total is None else dot_total + dot_part
    return jnp.sum(total, axis=0, keepdims=True), jnp.sum(dot_total, axis=0, keepdims=True)


def key_value_sums(c, d, blocks, reach, lanes, p_ref, ds_ref, query_stack, grad_stack, out_ref):
    rows = blocks * BLOCK
    for j in range(blocks):
        low, high = lane_range(d, j, blocks, reach)
        at = slice(c * rows + j * BLOCK, c * rows + (j + 1) * BLOCK)
        span = slice(low * lanes, high * lanes)
        out = slice(j * BLOCK, (j + 1) * BLOCK)
        key_sum = jnp.dot(ds_ref[at, span], query_stack[span, :], preferred_element_type=jnp.float32)
        out_ref[0, out, :] = (key_sum * SCALE).astype(out_ref.dtype)
        value_sum = jnp.dot(p_ref[at, span], grad_stack[span, :], preferred_element_type=jnp.float32)
        out_ref[1, out, :] = value_sum.astype(out_ref.dtype)


def query_sum(i, distances, blocks, reach, lanes, key_turned, ds_ref):
    rows = blocks * BLOCK
    total = None
    for c, d in enumerate(distances):
        low, high = key_range(d, i, blocks, reach)
        at = slice(c * rows + low * BLOCK, c * rows + high * BLOCK)
        part = jnp.dot(
            key_turned[:, at], ds_ref[at, i * lanes : (i + 1) * lanes], preferred_element_type=jnp.float32
        )
        total = part if total is None else total + part
    return total


def near_stats_kernel(blocks, reach, heads, flag_ref, query_ref, grad_ref, k0, v0, kv1, m_ref, l_ref, r_ref, qs, gs, s_ref, g_ref):
    lanes = heads * BLOCK
    stack_heads(query_ref, qs, blocks, heads)
    stack_heads(grad_ref, gs, blocks, heads)
    for i in range(blocks):
        span = slice(i * lanes, (i + 1) * lanes)
        s_i, g_i = s_ref.at[i % 2], g_ref.at[i % 2]
        top = score_pass(
            i, (0, 1), blocks, reach, flag_ref, (k0, kv1.at[0]), (v0, kv1.at[1]), qs[span, :], gs[span, :], s_i, g_i
        )
        total, dot_total = weight_pass(
            i, (0, 1), blocks, reach, flag_ref, s_i, g_i, top * SCALE_LOG2, False
        )
        m_ref[i : i + 1, :] = top
        l_ref[i : i + 1, :] = total
        r_ref[i : i + 1, :] = dot_total


def gradients(i, distances, blocks, reach, lanes, s_i, g_i, p_ref, ds_ref, inverse, delta):
    rows = blocks * BLOCK
    span = slice(i * lanes, (i + 1) * lanes)
    for c, d, j in tiles_of(distances, i, blocks, reach):
        at = slice(c * rows + j * BLOCK, c * rows + (j + 1) * BLOCK)
        probability = s_i[at, :] * inverse
        p_ref[at, span] = probability.astype(jnp.bfloat16)
        ds_ref[at, span] = (probability * (g_i[at, :] - delta)).astype(jnp.bfloat16)


def far_kernel(blocks, reach, heads, distances, *refs):
    count = len(distances)
    flag_ref, query_ref, grad_ref, m_ref, l_ref, r_ref = refs[:6]
    kv_refs = refs[6 : 6 + count]
    stat_ref, part_ref = refs[6 + count : 8 + count]
    out_refs = refs[8 + count : 8 + 2 * count]
    qs, gs, kt, s_ref, g_ref, p_ref, ds_ref = refs[8 + 2 * count :]
    lanes = heads * BLOCK
    rows = blocks * BLOCK
    stack_heads(query_ref, qs, blocks, heads)
    stack_heads(grad_ref, gs, blocks, heads)
    keys = [r.at[0] for r in kv_refs]
    values = [r.at[1] for r in kv_refs]
    for c in range(count):
        kt[:, c * rows : (c + 1) * rows] = keys[c][...].T
    for i in range(blocks):
        span = slice(i * lanes, (i + 1) * lanes)
        s_i, g_i = s_ref.at[i % 2], g_ref.at[i % 2]
        top = score_pass(
            i, distances, blocks, reach, flag_ref, keys, values, qs[span, :], gs[span, :], s_i, g_i
        )
        before = m_ref[i : i + 1, :]
        top = jnp.maximum(top, before)
        base = top * SCALE_LOG2
        total, dot_total = weight_pass(i, distances, blocks, reach, flag_ref, s_i, g_i, base, True)
        fade = jnp.exp2(before * SCALE_LOG2 - base)
        total = total + l_ref[i : i + 1, :] * fade
        dot_total = dot_total + r_ref[i : i + 1, :] * fade
        inverse = 1.0 / total
        delta = dot_total * inverse
        stat_ref[0, i : i + 1, :] = base
        stat_ref[1, i : i + 1, :] = inverse
        stat_ref[2, i : i + 1, :] = delta
        gradients(i, distances, blocks, reach, lanes, s_i, g_i, p_ref, ds_ref, inverse, delta)
    for c, d in enumerate(distances):
        key_value_sums(c, d, blocks, reach, lanes, p_ref, ds_ref, qs, gs, out_refs[c])
    for i in range(blocks):
        part_ref[i] = query_sum(i, distances, blocks, reach, lanes, kt, ds_ref)


def near_kernel(blocks, reach, heads, far, flag_ref, query_ref, grad_ref, k0, v0, kv1, stat_ref, *refs):
    part_ref, refs = (refs[0], refs[1:]) if far else (None, refs)
    out0_ref, out1_ref, dq_ref, qs, gs, kt, s_ref, g_ref, p_ref, ds_ref = refs
    lanes = heads * BLOCK
    rows = blocks * BLOCK
    distances = (0, 1)
    stack_heads(query_ref, qs, blocks, heads)
    stack_heads(grad_ref, gs, blocks, heads)
    keys, values = (k0, kv1.at[0]), (v0, kv1.at[1])
    for c in range(2):
        kt[:, c * rows : (c + 1) * rows] = keys[c][...].T
    for i in range(blocks):
        span = slice(i * lanes, (i + 1) * lanes)
        s_i, g_i = s_ref.at[i % 2], g_ref.at[i % 2]
        score_pass(
            i, distances, blocks, reach, flag_ref, keys, values, qs[span, :], gs[span, :], s_i, g_i
        )
        base = stat_ref[0, i : i + 1, :]
        weight_pass(i, distances, blocks, reach, flag_ref, s_i, g_i, base, True)
        inverse = stat_ref[1, i : i + 1, :]
        delta = stat_ref[2, i : i + 1, :]
        gradients(i, distances, blocks, reach, lanes, s_i, g_i, p_ref, ds_ref, inverse, delta)
    key_value_sums(1, 1, blocks, reach, lanes, p_ref, ds_ref, qs, gs, out1_ref)
    for i in range(blocks):
        total = query_sum(i, distances, blocks, reach, lanes, kt, ds_ref)
        if far:
            total = total + part_ref[i]
        total = total * SCALE
        for h in range(heads):
            dq_ref[i * BLOCK : (i + 1) * BLOCK, h * HEAD_WIDTH : (h + 1) * HEAD_WIDTH] = (
                total[:, h * BLOCK : (h + 1) * BLOCK].T.astype(dq_ref.dtype)
            )
    key_value_sums(0, 0, blocks, reach, lanes, p_ref, ds_ref, qs, gs, out0_ref)


def kernel_call(kernel, flags, arrays, outs, scratch, flops):
    size = sum(a.size * a.dtype.itemsize for a in arrays) + sum(a.size * a.dtype.itemsize for a in outs)
    held = sum(functools.reduce(lambda a, b: a * b, s.shape) * jnp.dtype(s.dtype).itemsize for s in scratch)
    return pl.pallas_call(
        kernel,
        out_shape=outs,
        in_specs=[pl.BlockSpec(memory_space=pltpu.SMEM)] + [pl.BlockSpec(memory_space=pltpu.VMEM)] * len(arrays),
        out_specs=[pl.BlockSpec(memory_space=pltpu.VMEM)] * len(outs),
        scratch_shapes=scratch,
        compiler_params=pltpu.CompilerParams(vmem_limit_bytes=int(held + 2 * size + (12 << 20))),
        cost_estimate=pl.CostEstimate(flops=flops, bytes_accessed=size, transcendentals=0),
    )(flags, *arrays)


def attention_flags(doc_blocks, blocks, reach, place):
    query_ids = place * blocks + jnp.arange(blocks, dtype=jnp.int32)
    column = jnp.arange((reach + 1) * blocks, dtype=jnp.int32)
    key_ids = (place - column // blocks) * blocks + column % blocks
    behind = query_ids[:, None] - key_ids[None, :]
    listed = jnp.any(doc_blocks[:, :, None] == key_ids[None, None, :], axis=1)
    allowed = (key_ids[None, :] >= 0) & ((behind == 0) | (behind == 1) | ((behind >= 2) & listed))
    return allowed.astype(jnp.int32)


def weight_pieces(w, rows_out, tp_place, group_place, group_count, bits):
    share = rows_out // group_count
    peer = tp_place ^ bits
    return lax.dynamic_slice_in_dim(w, peer * rows_out + group_place * share, share, axis=0)


def gathered_rows(piece, group_count, group_place):
    share = piece.shape[0]
    whole = jnp.zeros((share * group_count, piece.shape[1]), piece.dtype)
    whole = lax.dynamic_update_slice_in_dim(whole, piece, group_place * share, axis=0)
    for step in range(1, group_count):
        route = [(i, (i + step) % group_count) for i in range(group_count)]
        other = lax.ppermute(piece, "groups", route)
        source = lax.rem(group_place - step + group_count, group_count)
        whole = lax.dynamic_update_slice_in_dim(whole, other, source * share, axis=0)
    return whole


def body(query, key_head_rows, value_head_rows, output_gradient, doc_blocks, w_query, key_weight, value_weight):
    rows = query.shape[0]
    blocks = rows // BLOCK
    heads = query.shape[1] // key_head_rows.shape[1]
    lanes = heads * BLOCK
    reach = min(8, lax.axis_size("seq") - 1)
    place = lax.axis_index("seq")
    tp_count = lax.axis_size("tp")
    tp_place = lax.axis_index("tp")
    group_count = lax.axis_size("groups")
    group_place = lax.axis_index("groups")
    rows_out = w_query.shape[0] // tp_count
    bf16, f32 = jnp.bfloat16, jnp.float32

    key_value = jnp.stack([key_head_rows, value_head_rows])
    window = {1: shifted(key_value, "seq", 1)}
    if reach > 1:
        window[reach] = shifted(key_value, "seq", reach)
    for d in range(2, reach):
        window[d] = shifted(window[d - 1], "seq", 1)
    far = tuple(range(reach, 1, -1))

    flags = attention_flags(doc_blocks, blocks, reach, place)

    def scratch(count, gradient):
        shapes = [
            pltpu.VMEM((blocks * lanes, HEAD_WIDTH), bf16),
            pltpu.VMEM((blocks * lanes, HEAD_WIDTH), bf16),
        ]
        if gradient:
            shapes.append(pltpu.VMEM((HEAD_WIDTH, count * rows), bf16))
        shapes += [pltpu.VMEM((2, count * rows, lanes), f32)] * 2
        if gradient:
            shapes += [pltpu.VMEM((count * rows, blocks * lanes), bf16)] * 2
        return shapes

    unit = 2 * rows * blocks * lanes * HEAD_WIDTH
    near_in = [query, output_gradient, key_head_rows, value_head_rows, window[1]]
    stats = [jax.ShapeDtypeStruct((blocks, lanes), f32)] * 3
    top, total, dot_total = kernel_call(
        functools.partial(near_stats_kernel, blocks, reach, heads),
        flags, near_in, stats, scratch(2, False), 4 * unit,
    )
    grads = {}
    kv_shape = (2, rows, HEAD_WIDTH)
    if far:
        stat, part, *far_grads = kernel_call(
            functools.partial(far_kernel, blocks, reach, heads, far),
            flags,
            [query, output_gradient, top, total, dot_total] + [window[d] for d in far],
            [
                jax.ShapeDtypeStruct((3, blocks, lanes), f32),
                jax.ShapeDtypeStruct((blocks, HEAD_WIDTH, lanes), f32),
            ]
            + [jax.ShapeDtypeStruct(kv_shape, bf16)] * len(far),
            scratch(len(far), True),
            5 * len(far) * unit,
        )
        grads = dict(zip(far, far_grads))
        near_extra = [stat, part]
    else:
        near_extra = [jnp.stack([top * SCALE_LOG2, 1.0 / total, dot_total / total])]
    own, grads[1], query_grad = kernel_call(
        functools.partial(near_kernel, blocks, reach, heads, bool(far)),
        flags,
        near_in + near_extra,
        [
            jax.ShapeDtypeStruct(kv_shape, f32),
            jax.ShapeDtypeStruct(kv_shape, f32),
            jax.ShapeDtypeStruct(query.shape, bf16),
        ],
        scratch(2, True),
        10 * unit,
    )

    if far:
        own = own + shifted(grads[reach], "seq", -reach).astype(f32)
        passed = None
        for d in range(reach - 1, 0, -1):
            sent = grads[d] if passed is None else (grads[d].astype(f32) + passed.astype(f32))
            passed = shifted(sent.astype(bf16), "seq", -1)
    else:
        passed = shifted(grads[1].astype(bf16), "seq", -1)
    key_value_grad = (own + passed.astype(f32)).astype(bf16)
    key_value_grad = jnp.concatenate([key_value_grad[0], key_value_grad[1]], axis=1)

    kv_weight = jnp.concatenate([key_weight, value_weight], axis=1)
    own_rows = lambda w: lax.dynamic_slice_in_dim(w, tp_place * rows_out, rows_out, axis=0)
    w_q = {0: own_rows(w_query)}
    w_kv = {0: own_rows(kv_weight)}
    for bits in range(1, tp_count):
        if bits == 1:
            w_q[bits] = swapped(weight_pieces(w_query, rows_out, tp_place, 0, 1, bits), "tp", bits)
            w_kv[bits] = swapped(weight_pieces(kv_weight, rows_out, tp_place, 0, 1, bits), "tp", bits)
        else:
            piece = weight_pieces(w_query, rows_out, tp_place, group_place, group_count, bits)
            w_q[bits] = gathered_rows(swapped(piece, "tp", bits), group_count, group_place)
            piece = weight_pieces(kv_weight, rows_out, tp_place, group_place, group_count, bits)
            w_kv[bits] = gathered_rows(swapped(piece, "tp", bits), group_count, group_place)

    def gathered(block):
        pieces = {0: block, 1: swapped(block, "tp", 1)}
        for bits in range(2, tp_count, 2):
            pieces[bits] = swapped(block, "tp", bits)
            pieces[bits + 1] = swapped(pieces[bits], "tp", 1)
        return pieces

    q_pieces = gathered(query_grad)
    kv_pieces = gathered(key_value_grad)
    result = None
    for pieces, weights in ((q_pieces, w_q), (kv_pieces, w_kv)):
        for bits in range(tp_count):
            part = lax.dot_general(pieces[bits], weights[bits], NT, preferred_element_type=f32)
            result = part if result is None else result + part
    return result.astype(bf16)


def solution(mesh):
    in_specs = (
        P(("groups", "seq"), "tp"),
        P(("groups", "seq"), "tp"),
        P(("groups", "seq"), "tp"),
        P(("groups", "seq"), "tp"),
        P(("groups", "seq"), None),
        P(None, "tp"),
        P(None, "tp"),
        P(None, "tp"),
    )
    out_specs = P(("groups", "seq"), "tp")
    return jax.shard_map(body, mesh=mesh, in_specs=in_specs, out_specs=out_specs, check_vma=False)
```

time: 187 us -> 110 us (0.59)
  other arithmetic: 29.2 us -> 2.05 us
  matrix products: 32.3 us -> 7.65 us
  local copies, waits for them, and re-layouts: 30.6 us -> 8.52 us
  Pallas kernels: 0 us -> 16 us
  between operations: 13.7 us -> 0.49 us
  waiting for transfers between devices: 64.1 us -> 52.1 us
  starting transfers between devices: 16.3 us -> 23 us
    reduce_scatter x1 -> x0, waiting for transfers between devices: 42.9 us -> none  [body(): lax.psum_scatter(grad_term.astype(jnp.bfloat16), 'tp', scatter_dimension=...]
    ppermute x0 -> x16, waiting for transfers between devices: none -> 37.9 us  [the longest x4 21.6 us: gathered_rows(): other = lax.ppermute(piece, 'groups', route)]
    dot_general x9 -> x8, matrix products: 32.3 us -> 7.65 us  [body(): lax.dot_general(pieces[bits], weights[bits], NT, preferred_element_type=f32)]
    another operation x5 -> x4, local copies, waits for them, and re-layouts: 17.6 us -> 0.22 us  [the longest x3 14.5 us: body(): jnp.stack([key_gradient.reshape(blocks_here, listed_slot_count, feature_c...]
    pallas_call x0 -> x3, Pallas kernels: none -> 16 us  [kernel_call(): pl.pallas_call(kernel, out_shape=outs, in_specs=[pl.BlockSpec(memory_spac...]
    ppermute x0 -> x16, starting transfers between devices: none -> 9.55 us  [the longest x12 6.59 us: swapped(): lax.ppermute(block, axis, [(i, i ^ bits) for i in range(lax.axis_size(axi...]
    scatter-add x1 -> x0, other arithmetic: 8.81 us -> none  [body(): window_grads = jnp.zeros((window_blocks, 2 * feature_count), jnp.float32)...]
    another operation x3 -> x0, other arithmetic: 7.87 us -> none  [the longest x1 7.51 us: body(): jnp.stack([key_gradient.reshape(blocks_here, listed_slot_count, feature_c...]
  transfers between devices with their start and end apart: 7 -> 22, of which waited for: 4 -> 9; matrix products, arithmetic and copies ran while one was open for 10% -> 13% of each run, Pallas kernels for 0% -> 15%
where the time goes in v1:
time: 110 us
  waiting for transfers between devices  52.1 us (47%)
  starting transfers between devices  23 us (21%)
  Pallas kernels  16 us (15%)
  local copies, waits for them, and re-layouts  8.52 us (8%)
  matrix products  7.65 us (7%)
  other arithmetic  2.05 us (2%)
    ppermute x4, waiting for transfers between devices, gathered_rows(): other = lax.ppermute(piece, 'groups', route)  21.6 us
    ppermute x12, waiting for transfers between devices, swapped(): lax.ppermute(block, axis, [(i, i ^ bits) for i in range(lax.axis_size(axi...  16.2 us
    pallas_call x3, Pallas kernels, kernel_call(): pl.pallas_call(kernel, out_shape=outs, in_specs=[pl.BlockSpec(memory_spac...  16 us
    ppermute x6, waiting for transfers between devices, shifted(): return lax.ppermute(block, axis, route)  14.2 us
    ppermute x6, starting transfers between devices, shifted(): return lax.ppermute(block, axis, route)  13.4 us
    dot_general x8, matrix products, body(): lax.dot_general(pieces[bits], weights[bits], NT, preferred_element_type=f32)  7.65 us
    ppermute x12, starting transfers between devices, swapped(): lax.ppermute(block, axis, [(i, i ^ bits) for i in range(lax.axis_size(axi...  6.59 us
    dynamic_slice x4, local copies, waits for them, and re-layouts, weight_pieces(): lax.dynamic_slice_in_dim(w, peer * rows_out + group_place * share, share,...  4.61 us
  transfers between devices with their start and end apart: 22, of which 9 were waited for; matrix products, arithmetic and copies ran while one was open for 13% of the time, Pallas kernels for 15%

profile of v1, /device:TPU:0, one launch (start us, length us, event | category | flops | bytes accessed | tf_op | source)
XLA Modules:
  0.0 109.8 jit_solution(6292184795039744022)
XLA Ops:
  0.0 1.7 %pad_maximum_fusion = bf16[2,512,128]{2,1,0:T(8,128)(2,1)} fusion(bf16[1,512,128]{2,1,0:T(8,128)(2,1)} %bitcast.20, bf16[1,512,128]{2,1,0:T(8,128)(2,1)} %bitcast.19), kind=kLoop, calls=%fused_computation.7 | loop fusion | flops 131072 | bytes 524288 | tf_op jit(solution)/shard_map/stack | solution.py:304
  1.7 7.0 %collective-permute-start.1 = (bf16[2,512,128]{2,1,0:T(8,128)(2,1)}, bf16[2,512,128]{2,1,0:T(8,128)(2,1)S(1)}, u32[]{:S(2)}, u32[]{:S(2)}) collective-permute-start(bf16[2,512,128]{2,1,0:T(8,128)(2,1)} %pad_maximum_fusion), channel_id=1, source_target_pairs={{0,12},{1,13},{2,14},{3,15},{16,28},{17,29},{18,30},{19,31}} | collective-permute-start | bytes 786440 | tf_op jit(solution)/shard_map/ppermute | solution.py:21
  8.7 1.3 %collective-permute-start = (bf16[2,512,128]{2,1,0:T(8,128)(2,1)}, bf16[2,512,128]{2,1,0:T(8,128)(2,1)S(1)}, u32[]{:S(2)}, u32[]{:S(2)}) collective-permute-start(bf16[2,512,128]{2,1,0:T(8,128)(2,1)} %pad_maximum_fusion), channel_id=1, source_target_pairs={{0,4},{4,8},{8,12},{1,5},{5,9},{9,13},{2,6},{6,10},{10,14},{3,7},{... | collective-permute-start | bytes 786440 | tf_op jit(solution)/shard_map/ppermute | solution.py:21
  10.0 2.4 %constant_dynamic-slice_fusion.4 = (bf16[512,512]{1,0:T(8,128)(2,1)}, bf16[512,512]{1,0:T(8,128)(2,1)}) fusion(bf16[4096,512]{1,0:T(8,128)(2,1)} %param.13, s32[]{:T(128)S(6)} %select_n.66, s32[]{:T(128)S(6)} %select_n.69), kind=kLoop, calls=%fused_computation.27 | loop fusion | bytes 2097160 | tf_op jit(solution)/shard_map/dynamic_slice | solution.py:275
  12.4 1.5 %collective-permute-start.6 = (bf16[512,512]{1,0:T(8,128)(2,1)}, bf16[512,512]{1,0:T(8,128)(2,1)}, u32[]{:S(2)}, u32[]{:S(2)}) collective-permute-start(bf16[512,512]{1,0:T(8,128)(2,1)} %get-tuple-element.25), channel_id=1, source_target_pairs={{0,2},{1,3},{2,0},{3,1},{4,6},{5,7},{6,4},{7,5},{8,10},{9,11},{10,... | collective-permute-start | bytes 1572872 | tf_op jit(solution)/shard_map/ppermute | solution.py:25
  16.4 1.4 %constant_dynamic-slice_fusion.5 = bf16[1024,512]{1,0:T(8,128)(2,1)S(1)} fusion(bf16[4096,512]{1,0:T(8,128)(2,1)} %param.13, s32[]{:T(128)S(6)} %select_n.65), kind=kLoop, calls=%fused_computation.28 | loop fusion | bytes 2097156 | tf_op jit(solution)/shard_map/dynamic_slice | solution.py:275
  17.8 2.4 %collective-permute-done.kv1 = bf16[2,512,128]{2,1,0:T(8,128)(2,1)S(1)} collective-permute-done((bf16[2,512,128]{2,1,0:T(8,128)(2,1)}, bf16[2,512,128]{2,1,0:T(8,128)(2,1)S(1)}, u32[]{:S(2)}, u32[]{:S(2)}) %collective-permute-start) | collective-permute-done | bytes 262176 | tf_op jit(solution)/shard_map/ppermute | solution.py:21
  20.3 11.9 %collective-permute-done.20 = bf16[512,256]{1,0:T(8,128)(2,1)} collective-permute-done((bf16[512,256]{1,0:T(8,128)(2,1)}, bf16[512,256]{1,0:T(8,128)(2,1)}, u32[]{:S(2)}, u32[]{:S(2)}) %collective-permute-start.20) | collective-permute-done | bytes 262176 | tf_op jit(solution)/shard_map/ppermute | solution.py:25
  32.2 1.3 %collective-permute-start.2 = (bf16[2,512,128]{2,1,0:T(8,128)(2,1)S(1)}, bf16[2,512,128]{2,1,0:T(8,128)(2,1)S(1)}, u32[]{:S(2)}, u32[]{:S(2)}) collective-permute-start(bf16[2,512,128]{2,1,0:T(8,128)(2,1)S(1)} %collective-permute-done.kv1), channel_id=1, source_target_pairs={{0,4},{4,8},{8,12},{1,5},{5,9},{9,13},{2,6},{6,10},{10,14},{3,7},{... | collective-permute-start | bytes 786440 | tf_op jit(solution)/shard_map/ppermute | solution.py:21
  34.5 4.3 %collective-permute-done.17 = bf16[512,256]{1,0:T(8,128)(2,1)} collective-permute-done((bf16[512,256]{1,0:T(8,128)(2,1)S(1)}, bf16[512,256]{1,0:T(8,128)(2,1)}, u32[]{:S(2)}, u32[]{:S(2)}) %collective-permute-start.17) | collective-permute-done | bytes 262176 | tf_op jit(solution)/shard_map/ppermute | solution.py:25
  38.8 1.5 %collective-permute-start.21 = (bf16[512,256]{1,0:T(8,128)(2,1)}, bf16[512,256]{1,0:T(8,128)(2,1)S(1)}, u32[]{:S(2)}, u32[]{:S(2)}) collective-permute-start(bf16[512,256]{1,0:T(8,128)(2,1)} %collective-permute-done.20), channel_id=1, source_target_pairs={{0,16},{16,0},{1,17},{17,1},{2,18},{18,2},{3,19},{19,3},{4,20},{20... | collective-permute-start | bytes 786440 | tf_op jit(solution)/shard_map/ppermute | solution.py:284
  41.4 3.5 %shard_map.82 = (f32[4,512]{1,0:T(4,128)S(1)}, f32[4,512]{1,0:T(4,128)S(1)}, f32[4,512]{1,0:T(4,128)S(1)}) custom-call(s32[4,16]{1,0:T(4,128)S(1)} %fusion.10.flag_ref.refs_0_, bf16[512,512]{1,0:T(8,128)(2,1)S(1)} %copy-done.2, bf16[512,512]{1,0:T(8,128)(2,1)S(1)} %copy-done.3, bf16[512,128]{1,0:T(8,128)(2,1)S(1)} %copy-done, ...), custom_call_target="tpu_custom_call" | custom-call | flops 1073741824 | bytes 1597440 | tf_op jit(solution)/shard_map/pallas_call | solution.py:251
  45.5 7.0 %shard_map.83 = (f32[3,4,512]{2,1,0:T(4,128)S(1)}, f32[4,128,512]{2,1,0:T(8,128)S(1)}, bf16[2,512,128]{2,1,0:T(8,128)(2,1)S(1)}, bf16[2,512,128]{2,1,0:T(8,128)(2,1)S(1)}) custom-call(s32[4,16]{1,0:T(4,128)S(1)} %fusion.10.flag_ref.refs_0_, bf16[512,512]{1,0:T(8,128)(2,1)S(1)} %copy-done.2, bf16[512,512]{1,0:T(8,128)(2,1)S(1)} %copy-done.3, ...), custom_call_target="tpu_custom_call" | custom-call | flops 2684354560 | bytes 3194880 | tf_op jit(solution)/shard_map/pallas_call | solution.py:251
  53.1 5.5 %shard_map.84 = (f32[2,512,128]{2,1,0:T(8,128)S(1)}, f32[2,512,128]{2,1,0:T(8,128)S(1)}, bf16[512,512]{1,0:T(8,128)(2,1)S(1)}) custom-call(s32[4,16]{1,0:T(4,128)S(1)} %fusion.10.flag_ref.refs_0_, bf16[512,512]{1,0:T(8,128)(2,1)S(1)} %copy-done.2, bf16[512,512]{1,0:T(8,128)(2,1)S(1)} %copy-done.3, bf16[512,128]{1,0:T(8,128)(2,1)S(1)} %copy-done, ...), custom_call_target="tpu_custom_call" | custom-call | flops 2684354560 | bytes 4218880 | tf_op jit(solution)/shard_map/pallas_call | solution.py:251
  58.6 2.5 %collective-permute-done.18 = bf16[512,256]{1,0:T(8,128)(2,1)S(1)} collective-permute-done((bf16[512,256]{1,0:T(8,128)(2,1)}, bf16[512,256]{1,0:T(8,128)(2,1)S(1)}, u32[]{:S(2)}, u32[]{:S(2)}) %collective-permute-start.18) | collective-permute-done | bytes 262176 | tf_op jit(solution)/shard_map/ppermute | solution.py:284
  64.9 1.5 %collective-permute-start.5 = (bf16[512,512]{1,0:T(8,128)(2,1)S(1)}, bf16[512,512]{1,0:T(8,128)(2,1)S(1)}, u32[]{:S(2)}, u32[]{:S(2)}) collective-permute-start(bf16[512,512]{1,0:T(8,128)(2,1)S(1)} %get-tuple-element.20), channel_id=1, source_target_pairs={{0,2},{1,3},{2,0},{3,1},{4,6},{5,7},{6,4},{7,5},{8,10},{9,11},{10,... | collective-permute-start | bytes 1572872 | tf_op jit(solution)/shard_map/ppermute | solution.py:25
  66.6 5.7 %collective-permute-done.12 = bf16[2,512,128]{2,1,0:T(8,128)(2,1)S(1)} collective-permute-done((bf16[2,512,128]{2,1,0:T(8,128)(2,1)S(1)}, bf16[2,512,128]{2,1,0:T(8,128)(2,1)S(1)}, u32[]{:S(2)}, u32[]{:S(2)}) %collective-permute-start.12) | collective-permute-done | bytes 262176 | tf_op jit(solution)/shard_map/ppermute | solution.py:21
  73.6 2.0 %fusion = f32[512,1024]{1,0:T(8,128)S(1)} fusion(bf16[512,512]{1,0:T(8,128)(2,1)S(1)} %get-tuple-element.20, bf16[4096,512]{1,0:T(8,128)(2,1)} %param.13, s32[]{:T(128)S(6)} %select_n.64), kind=kOutput, calls=%fused_computation.1 | convolution fusion | flops 536870912 | bytes 3670020 | tf_op jit(solution)/shard_map/dot_general | solution.py:402
  75.6 2.3 %collective-permute-done.11 = bf16[2,512,128]{2,1,0:T(8,128)(2,1)S(1)} collective-permute-done((bf16[2,512,128]{2,1,0:T(8,128)(2,1)S(1)}, bf16[2,512,128]{2,1,0:T(8,128)(2,1)S(1)}, u32[]{:S(2)}, u32[]{:S(2)}) %collective-permute-start.11) | collective-permute-done | bytes 262176 | tf_op jit(solution)/shard_map/ppermute | solution.py:21
  77.8 3.9 %collective-permute-done.13 = bf16[2,512,128]{2,1,0:T(8,128)(2,1)S(1)} collective-permute-done((bf16[2,512,128]{2,1,0:T(8,128)(2,1)S(1)}, bf16[2,512,128]{2,1,0:T(8,128)(2,1)S(1)}, u32[]{:S(2)}, u32[]{:S(2)}) %collective-permute-start.13) | collective-permute-done | bytes 262176 | tf_op jit(solution)/shard_map/ppermute | solution.py:21
  82.4 11.8 %collective-permute-done.7 = bf16[512,512]{1,0:T(8,128)(2,1)S(1)} collective-permute-done((bf16[512,512]{1,0:T(8,128)(2,1)}, bf16[512,512]{1,0:T(8,128)(2,1)S(1)}, u32[]{:S(2)}, u32[]{:S(2)}) %collective-permute-start.7) | collective-permute-done | bytes 524320 | tf_op jit(solution)/shard_map/ppermute | solution.py:284
  95.5 1.6 %collective-permute-start.16 = (bf16[512,256]{1,0:T(8,128)(2,1)S(1)}, bf16[512,256]{1,0:T(8,128)(2,1)S(1)}, u32[]{:S(2)}, u32[]{:S(2)}) collective-permute-start(bf16[512,256]{1,0:T(8,128)(2,1)S(1)} %pad_maximum_fusion.1), channel_id=1, source_target_pairs={{0,2},{1,3},{2,0},{3,1},{4,6},{5,7},{6,4},{7,5},{8,10},{9,11},{10,... | collective-permute-start | bytes 786440 | tf_op jit(solution)/shard_map/ppermute | solution.py:25
  98.1 7.4 %collective-permute-done.10 = bf16[512,512]{1,0:T(8,128)(2,1)S(1)} collective-permute-done((bf16[512,512]{1,0:T(8,128)(2,1)S(1)}, bf16[512,512]{1,0:T(8,128)(2,1)S(1)}, u32[]{:S(2)}, u32[]{:S(2)}) %collective-permute-start.10) | collective-permute-done | bytes 524320 | tf_op jit(solution)/shard_map/ppermute | solution.py:284
  107.8 2.0 %add_convert_fusion = bf16[512,1024]{1,0:T(8,128)(2,1)} fusion(f32[512,1024]{1,0:T(8,128)S(1)} %fusion.18, f32[512,1024]{1,0:T(8,128)S(1)} %fusion.17, f32[512,1024]{1,0:T(8,128)S(1)} %fusion.2, f32[512,1024]{1,0:T(8,128)S(1)} %fusion.16, f32[512,1024]{1,0:T(8,128)S(1)} %fusion.15, f32[512,1024]{1,0:T(8,128)S(1)} %fusion, f32[512,1024]{1,0:T(8,128)S(1)} %fusion.14, ...), kind=kOutput, calls=%fused_computation | convolution fusion | flops 272629760 | bytes 16515072 | tf_op jit(solution)/shard_map/dot_general | solution.py:402
  (75 shorter events, 16.0 us)
Async XLA Ops:
  1.7 43.2 %collective-permute-start.1 = (bf16[2,512,128]{2,1,0:T(8,128)(2,1)}, bf16[2,512,128]{2,1,0:T(8,128)(2,1)S(1)}, u32[]{:S(2)}, u32[]{:S(2)}) collective-permute-start(bf16[2,512,128]{2,1,0:T(8,128)(2,1)} %pad_maximum_fusion), channel_id=1, source_target_pairs={{0,12},{1,13},{2,14},{3,15},{16,28},{17,29},{18,30},{19,31}} | collective-permute-start | bytes 786440 | tf_op jit(solution)/shard_map/ppermute | solution.py:21
  8.7 11.5 %collective-permute-start = (bf16[2,512,128]{2,1,0:T(8,128)(2,1)}, bf16[2,512,128]{2,1,0:T(8,128)(2,1)S(1)}, u32[]{:S(2)}, u32[]{:S(2)}) collective-permute-start(bf16[2,512,128]{2,1,0:T(8,128)(2,1)} %pad_maximum_fusion), channel_id=1, source_target_pairs={{0,4},{4,8},{8,12},{1,5},{5,9},{9,13},{2,6},{6,10},{10,14},{3,7},{... | collective-permute-start | bytes 786440 | tf_op jit(solution)/shard_map/ppermute | solution.py:21
  12.4 50.0 %collective-permute-start.6 = (bf16[512,512]{1,0:T(8,128)(2,1)}, bf16[512,512]{1,0:T(8,128)(2,1)}, u32[]{:S(2)}, u32[]{:S(2)}) collective-permute-start(bf16[512,512]{1,0:T(8,128)(2,1)} %get-tuple-element.25), channel_id=1, source_target_pairs={{0,2},{1,3},{2,0},{3,1},{4,6},{5,7},{6,4},{7,5},{8,10},{9,11},{10,... | collective-permute-start | bytes 1572872 | tf_op jit(solution)/shard_map/ppermute | solution.py:25
  15.1 17.1 %collective-permute-start.20 = (bf16[512,256]{1,0:T(8,128)(2,1)}, bf16[512,256]{1,0:T(8,128)(2,1)}, u32[]{:S(2)}, u32[]{:S(2)}) collective-permute-start(bf16[512,256]{1,0:T(8,128)(2,1)} %get-tuple-element.27), channel_id=1, source_target_pairs={{0,3},{1,2},{2,1},{3,0},{4,7},{5,6},{6,5},{7,4},{8,11},{9,10},{10,... | collective-permute-start | bytes 786440 | tf_op jit(solution)/shard_map/ppermute | solution.py:25
  15.1 23.7 %collective-permute-start.17 = (bf16[512,256]{1,0:T(8,128)(2,1)S(1)}, bf16[512,256]{1,0:T(8,128)(2,1)}, u32[]{:S(2)}, u32[]{:S(2)}) collective-permute-start(bf16[512,256]{1,0:T(8,128)(2,1)S(1)} %get-tuple-element.28), channel_id=1, source_target_pairs={{0,2},{1,3},{2,0},{3,1},{4,6},{5,7},{6,4},{7,5},{8,10},{9,11},{10,... | collective-permute-start | bytes 786440 | tf_op jit(solution)/shard_map/ppermute | solution.py:25
  16.3 25.1 %copy-start = (bf16[512,128]{1,0:T(8,128)(2,1)S(1)}, bf16[512,128]{1,0:T(8,128)(2,1)}, u32[]{:S(2)}) copy-start(bf16[512,128]{1,0:T(8,128)(2,1)} %k0.3) | copy-start | bytes 393220
  16.3 25.1 %copy-start.1 = (bf16[512,128]{1,0:T(8,128)(2,1)S(1)}, bf16[512,128]{1,0:T(8,128)(2,1)}, u32[]{:S(2)}) copy-start(bf16[512,128]{1,0:T(8,128)(2,1)} %v0.3) | copy-start | bytes 393220
  20.2 44.7 %collective-permute-start.9 = (bf16[512,512]{1,0:T(8,128)(2,1)S(1)}, bf16[512,512]{1,0:T(8,128)(2,1)S(1)}, u32[]{:S(2)}, u32[]{:S(2)}) collective-permute-start(bf16[512,512]{1,0:T(8,128)(2,1)S(1)} %copy-done.6), channel_id=1, source_target_pairs={{0,3},{1,2},{2,1},{3,0},{4,7},{5,6},{6,5},{7,4},{8,11},{9,10},{10,... | collective-permute-start | bytes 1572872 | tf_op jit(solution)/shard_map/ppermute | solution.py:25
  32.2 12.8 %collective-permute-start.2 = (bf16[2,512,128]{2,1,0:T(8,128)(2,1)S(1)}, bf16[2,512,128]{2,1,0:T(8,128)(2,1)S(1)}, u32[]{:S(2)}, u32[]{:S(2)}) collective-permute-start(bf16[2,512,128]{2,1,0:T(8,128)(2,1)S(1)} %collective-permute-done.kv1), channel_id=1, source_target_pairs={{0,4},{4,8},{8,12},{1,5},{5,9},{9,13},{2,6},{6,10},{10,14},{3,7},{... | collective-permute-start | bytes 786440 | tf_op jit(solution)/shard_map/ppermute | solution.py:21
  38.8 13.7 %collective-permute-start.21 = (bf16[512,256]{1,0:T(8,128)(2,1)}, bf16[512,256]{1,0:T(8,128)(2,1)S(1)}, u32[]{:S(2)}, u32[]{:S(2)}) collective-permute-start(bf16[512,256]{1,0:T(8,128)(2,1)} %collective-permute-done.20), channel_id=1, source_target_pairs={{0,16},{16,0},{1,17},{17,1},{2,18},{18,2},{3,19},{19,3},{4,20},{20... | collective-permute-start | bytes 786440 | tf_op jit(solution)/shard_map/ppermute | solution.py:284
  44.9 52.2 %collective-permute-start.4 = (bf16[1024,512]{1,0:T(8,128)(2,1)S(1)}, bf16[1024,512]{1,0:T(8,128)(2,1)S(1)}, u32[]{:S(2)}, u32[]{:S(2)}) collective-permute-start(bf16[1024,512]{1,0:T(8,128)(2,1)S(1)} %constant_dynamic-slice_fusion.5), channel_id=1, source_target_pairs={{0,1},{1,0},{2,3},{3,2},{4,5},{5,4},{6,7},{7,6},{8,9},{9,8},{10,11... | collective-permute-start | bytes 3145736 | tf_op jit(solution)/shard_map/ppermute | solution.py:25
  45.0 61.5 %collective-permute-start.15 = (bf16[1024,256]{1,0:T(8,128)(2,1)S(1)}, bf16[1024,256]{1,0:T(8,128)(2,1)S(1)}, u32[]{:S(2)}, u32[]{:S(2)}) collective-permute-start(bf16[1024,256]{1,0:T(8,128)(2,1)S(1)} %constant_dynamic-slice_fusion.2), channel_id=1, source_target_pairs={{0,1},{1,0},{2,3},{3,2},{4,5},{5,4},{6,7},{7,6},{8,9},{9,8},{10,11... | collective-permute-start | bytes 1572872 | tf_op jit(solution)/shard_map/ppermute | solution.py:25
  52.5 8.6 %collective-permute-start.18 = (bf16[512,256]{1,0:T(8,128)(2,1)}, bf16[512,256]{1,0:T(8,128)(2,1)S(1)}, u32[]{:S(2)}, u32[]{:S(2)}) collective-permute-start(bf16[512,256]{1,0:T(8,128)(2,1)} %collective-permute-done.17), channel_id=1, source_target_pairs={{0,16},{16,0},{1,17},{17,1},{2,18},{18,2},{3,19},{19,3},{4,20},{20... | collective-permute-start | bytes 786440 | tf_op jit(solution)/shard_map/ppermute | solution.py:284
  61.1 11.1 %collective-permute-start.12 = (bf16[2,512,128]{2,1,0:T(8,128)(2,1)S(1)}, bf16[2,512,128]{2,1,0:T(8,128)(2,1)S(1)}, u32[]{:S(2)}, u32[]{:S(2)}) collective-permute-start(bf16[2,512,128]{2,1,0:T(8,128)(2,1)S(1)} %get-tuple-element.24), channel_id=1, source_target_pairs={{4,0},{8,4},{12,8},{5,1},{9,5},{13,9},{6,2},{10,6},{14,10},{7,3},{... | collective-permute-start | bytes 786440 | tf_op jit(solution)/shard_map/ppermute | solution.py:21
  62.4 15.4 %collective-permute-start.11 = (bf16[2,512,128]{2,1,0:T(8,128)(2,1)S(1)}, bf16[2,512,128]{2,1,0:T(8,128)(2,1)S(1)}, u32[]{:S(2)}, u32[]{:S(2)}) collective-permute-start(bf16[2,512,128]{2,1,0:T(8,128)(2,1)S(1)} %get-tuple-element.22), channel_id=1, source_target_pairs={{12,0},{13,1},{14,2},{15,3},{28,16},{29,17},{30,18},{31,19}} | collective-permute-start | bytes 786440 | tf_op jit(solution)/shard_map/ppermute | solution.py:21
  64.9 29.7 %collective-permute-start.5 = (bf16[512,512]{1,0:T(8,128)(2,1)S(1)}, bf16[512,512]{1,0:T(8,128)(2,1)S(1)}, u32[]{:S(2)}, u32[]{:S(2)}) collective-permute-start(bf16[512,512]{1,0:T(8,128)(2,1)S(1)} %get-tuple-element.20), channel_id=1, source_target_pairs={{0,2},{1,3},{2,0},{3,1},{4,6},{5,7},{6,4},{7,5},{8,10},{9,11},{10,... | collective-permute-start | bytes 1572872 | tf_op jit(solution)/shard_map/ppermute | solution.py:25
  72.3 9.5 %collective-permute-start.13 = (bf16[2,512,128]{2,1,0:T(8,128)(2,1)S(1)}, bf16[2,512,128]{2,1,0:T(8,128)(2,1)S(1)}, u32[]{:S(2)}, u32[]{:S(2)}) collective-permute-start(bf16[2,512,128]{2,1,0:T(8,128)(2,1)S(1)} %add_convert_fusion.2), channel_id=1, source_target_pairs={{4,0},{8,4},{12,8},{5,1},{9,5},{13,9},{6,2},{10,6},{14,10},{7,3},{... | collective-permute-start | bytes 786440 | tf_op jit(solution)/shard_map/ppermute | solution.py:21
  77.8 17.6 %collective-permute-start.3 = (bf16[512,512]{1,0:T(8,128)(2,1)S(1)}, bf16[512,512]{1,0:T(8,128)(2,1)S(1)}, u32[]{:S(2)}, u32[]{:S(2)}) collective-permute-start(bf16[512,512]{1,0:T(8,128)(2,1)S(1)} %get-tuple-element.20), channel_id=1, source_target_pairs={{0,1},{1,0},{2,3},{3,2},{4,5},{5,4},{6,7},{7,6},{8,9},{9,8},{10,11... | collective-permute-start | bytes 1572872 | tf_op jit(solution)/shard_map/ppermute | solution.py:25
  81.7 12.4 %collective-permute-start.7 = (bf16[512,512]{1,0:T(8,128)(2,1)}, bf16[512,512]{1,0:T(8,128)(2,1)S(1)}, u32[]{:S(2)}, u32[]{:S(2)}) collective-permute-start(bf16[512,512]{1,0:T(8,128)(2,1)} %collective-permute-done.6), channel_id=1, source_target_pairs={{0,16},{16,0},{1,17},{17,1},{2,18},{18,2},{3,19},{19,3},{4,20},{20... | collective-permute-start | bytes 1572872 | tf_op jit(solution)/shard_map/ppermute | solution.py:284
  94.2 11.3 %collective-permute-start.10 = (bf16[512,512]{1,0:T(8,128)(2,1)S(1)}, bf16[512,512]{1,0:T(8,128)(2,1)S(1)}, u32[]{:S(2)}, u32[]{:S(2)}) collective-permute-start(bf16[512,512]{1,0:T(8,128)(2,1)S(1)} %collective-permute-done.9), channel_id=1, source_target_pairs={{0,16},{16,0},{1,17},{17,1},{2,18},{18,2},{3,19},{19,3},{4,20},{20... | collective-permute-start | bytes 1572872 | tf_op jit(solution)/shard_map/ppermute | solution.py:284
  94.6 11.9 %collective-permute-start.14 = (bf16[512,256]{1,0:T(8,128)(2,1)S(1)}, bf16[512,256]{1,0:T(8,128)(2,1)S(1)}, u32[]{:S(2)}, u32[]{:S(2)}) collective-permute-start(bf16[512,256]{1,0:T(8,128)(2,1)S(1)} %pad_maximum_fusion.1), channel_id=1, source_target_pairs={{0,1},{1,0},{2,3},{3,2},{4,5},{5,4},{6,7},{7,6},{8,9},{9,8},{10,11... | collective-permute-start | bytes 786440 | tf_op jit(solution)/shard_map/ppermute | solution.py:25
  95.5 10.5 %collective-permute-start.16 = (bf16[512,256]{1,0:T(8,128)(2,1)S(1)}, bf16[512,256]{1,0:T(8,128)(2,1)S(1)}, u32[]{:S(2)}, u32[]{:S(2)}) collective-permute-start(bf16[512,256]{1,0:T(8,128)(2,1)S(1)} %pad_maximum_fusion.1), channel_id=1, source_target_pairs={{0,2},{1,3},{2,0},{3,1},{4,6},{5,7},{6,4},{7,5},{8,10},{9,11},{10,... | collective-permute-start | bytes 786440 | tf_op jit(solution)/shard_map/ppermute | solution.py:25
  97.1 9.9 %collective-permute-start.8 = (bf16[512,512]{1,0:T(8,128)(2,1)S(1)}, bf16[512,512]{1,0:T(8,128)(2,1)S(1)}, u32[]{:S(2)}, u32[]{:S(2)}) collective-permute-start(bf16[512,512]{1,0:T(8,128)(2,1)S(1)} %collective-permute-done.5), channel_id=1, source_target_pairs={{0,1},{1,0},{2,3},{3,2},{4,5},{5,4},{6,7},{7,6},{8,9},{9,8},{10,11... | collective-permute-start | bytes 1572872 | tf_op jit(solution)/shard_map/ppermute | solution.py:25
  106.0 1.8 %collective-permute-start.19 = (bf16[512,256]{1,0:T(8,128)(2,1)S(1)}, bf16[512,256]{1,0:T(8,128)(2,1)S(1)}, u32[]{:S(2)}, u32[]{:S(2)}) collective-permute-start(bf16[512,256]{1,0:T(8,128)(2,1)S(1)} %collective-permute-done.16), channel_id=1, source_target_pairs={{0,1},{1,0},{2,3},{3,2},{4,5},{5,4},{6,7},{7,6},{8,9},{9,8},{10,11... | collective-permute-start | bytes 786440 | tf_op jit(solution)/shard_map/ppermute | solution.py:25
  (6 other events, 63.9 us)

commit v2 on v1

v2 whole, which is shorter than its diff:
```python
import functools
import math

import jax
import jax.numpy as jnp
from jax import lax
from jax.experimental import pallas as pl
from jax.experimental.pallas import tpu as pltpu
from jax.sharding import PartitionSpec as P

HEAD_WIDTH = 128
BLOCK = 128
SCALE = HEAD_WIDTH ** (-0.5)
SCALE_LOG2 = SCALE * 1.4426950408889634
LOWEST = -1e30
NT = (((1,), (1,)), ((), ()))


def shifted(block, axis, distance):
    devices = range(lax.axis_size(axis))
    route = [(i - distance, i) for i in devices if i - distance in devices]
    return lax.ppermute(block, axis, route)


def swapped(block, axis, bits):
    return lax.ppermute(block, axis, [(i, i ^ bits) for i in range(lax.axis_size(axis))])


def key_range(distance, i, blocks, reach):
    if distance == 0:
        return 0, i + 1
    if distance == reach:
        return i, blocks
    return 0, blocks


def lane_range(distance, j, blocks, reach):
    if distance == 0:
        return j, blocks
    if distance == reach:
        return 0, j + 1
    return 0, blocks


def stack_heads(rows_ref, stack_ref, blocks, heads):
    for i in range(blocks):
        for h in range(heads):
            at = (i * heads + h) * BLOCK
            stack_ref[at : at + BLOCK, :] = rows_ref[
                i * BLOCK : (i + 1) * BLOCK, h * HEAD_WIDTH : (h + 1) * HEAD_WIDTH
            ]


def band_keep(offset, lanes):
    key_at = lax.broadcasted_iota(jnp.int32, (BLOCK, lanes), 0)
    query_at = lax.broadcasted_iota(jnp.int32, (BLOCK, lanes), 1) % BLOCK
    return key_at <= query_at if offset == 0 else key_at > query_at


def fold(tile, op):
    rows = tile.shape[0]
    total = tile[0:8]
    for at in range(8, rows, 8):
        total = op(total, tile[at : at + 8])
    return total


def keys_of(ref):
    return ref.at[:, 0:HEAD_WIDTH]


def values_of(ref):
    return ref.at[:, HEAD_WIDTH : 2 * HEAD_WIDTH]


def tiles_of(distances, i, blocks, reach):
    return [
        (c, d, j)
        for c, d in enumerate(distances)
        for j in range(*key_range(d, i, blocks, reach))
    ]


def score_pass(i, distances, blocks, reach, flag_ref, key_refs, value_refs, query_i, grad_i, s_ref, g_ref):
    rows = blocks * BLOCK
    top = None
    for c, d in enumerate(distances):
        low, high = key_range(d, i, blocks, reach)
        span = slice(low * BLOCK, high * BLOCK)
        at = slice(c * rows + low * BLOCK, c * rows + high * BLOCK)
        s_ref[at, :] = lax.dot_general(key_refs[c][span, :], query_i, NT, preferred_element_type=jnp.float32)
        g_ref[at, :] = lax.dot_general(value_refs[c][span, :], grad_i, NT, preferred_element_type=jnp.float32)
    for c, d, j in tiles_of(distances, i, blocks, reach):
        at = slice(c * rows + j * BLOCK, c * rows + (j + 1) * BLOCK)
        offset = d * blocks + i - j
        tile = s_ref[at, :]
        if offset < 2:
            tile = jnp.where(band_keep(offset, tile.shape[1]), tile, LOWEST)
            s_ref[at, :] = tile
        part = fold(tile, jnp.maximum)
        if offset > 0:
            part = jnp.where(flag_ref[i, d * blocks + j] != 0, part, LOWEST)
        top = part if top is None else jnp.maximum(top, part)
    return jnp.max(top, axis=0, keepdims=True)


def shift_of(flag_ref, i, d, j, blocks, base):
    if d * blocks + i - j == 0:
        return base
    return jnp.where(flag_ref[i, d * blocks + j] != 0, base, -LOWEST)


def weight_pass(i, distances, blocks, reach, flag_ref, s_ref, g_ref, base, keep):
    rows = blocks * BLOCK
    total = dot_total = None
    for c, d, j in tiles_of(distances, i, blocks, reach):
        at = slice(c * rows + j * BLOCK, c * rows + (j + 1) * BLOCK)
        weights = jnp.exp2(s_ref[at, :] * SCALE_LOG2 - shift_of(flag_ref, i, d, j, blocks, base))
        if keep:
            s_ref[at, :] = weights
        part = fold(weights, jnp.add)
        dot_part = fold(weights * g_ref[at, :], jnp.add)
        total = part if total is None else total + part
        dot_total = dot_part if dot_total is None else dot_total + dot_part
    return jnp.sum(total, axis=0, keepdims=True), jnp.sum(dot_total, axis=0, keepdims=True)


def key_value_sums(c, d, blocks, reach, lanes, p_ref, ds_ref, query_stack, grad_stack, out_ref):
    rows = blocks * BLOCK
    for j in range(blocks):
        low, high = lane_range(d, j, blocks, reach)
        at = slice(c * rows + j * BLOCK, c * rows + (j + 1) * BLOCK)
        span = slice(low * lanes, high * lanes)
        out = slice(j * BLOCK, (j + 1) * BLOCK)
        key_sum = jnp.dot(ds_ref[at, span], query_stack[span, :], preferred_element_type=jnp.float32)
        out_ref[out, 0:HEAD_WIDTH] = (key_sum * SCALE).astype(out_ref.dtype)
        value_sum = jnp.dot(p_ref[at, span], grad_stack[span, :], preferred_element_type=jnp.float32)
        out_ref[out, HEAD_WIDTH:] = value_sum.astype(out_ref.dtype)


def query_sum(i, distances, blocks, reach, lanes, key_turned, ds_ref):
    rows = blocks * BLOCK
    total = None
    for c, d in enumerate(distances):
        low, high = key_range(d, i, blocks, reach)
        at = slice(c * rows + low * BLOCK, c * rows + high * BLOCK)
        part = jnp.dot(
            key_turned[:, at], ds_ref[at, i * lanes : (i + 1) * lanes], preferred_element_type=jnp.float32
        )
        total = part if total is None else total + part
    return total


def near_stats_kernel(blocks, reach, heads, flag_ref, query_ref, grad_ref, k0, v0, kv1, m_ref, l_ref, r_ref, qs, gs, s_ref, g_ref):
    lanes = heads * BLOCK
    stack_heads(query_ref, qs, blocks, heads)
    stack_heads(grad_ref, gs, blocks, heads)
    for i in range(blocks):
        span = slice(i * lanes, (i + 1) * lanes)
        s_i, g_i = s_ref.at[i % 2], g_ref.at[i % 2]
        top = score_pass(
            i, (0, 1), blocks, reach, flag_ref, (k0, keys_of(kv1)), (v0, values_of(kv1)), qs[span, :], gs[span, :], s_i, g_i
        )
        total, dot_total = weight_pass(
            i, (0, 1), blocks, reach, flag_ref, s_i, g_i, top * SCALE_LOG2, False
        )
        m_ref[i : i + 1, :] = top
        l_ref[i : i + 1, :] = total
        r_ref[i : i + 1, :] = dot_total


def gradients(i, distances, blocks, reach, lanes, s_i, g_i, p_ref, ds_ref, inverse, delta):
    rows = blocks * BLOCK
    span = slice(i * lanes, (i + 1) * lanes)
    for c, d, j in tiles_of(distances, i, blocks, reach):
        at = slice(c * rows + j * BLOCK, c * rows + (j + 1) * BLOCK)
        probability = s_i[at, :] * inverse
        p_ref[at, span] = probability.astype(jnp.bfloat16)
        ds_ref[at, span] = (probability * (g_i[at, :] - delta)).astype(jnp.bfloat16)


def far_kernel(blocks, reach, heads, distances, middle, *refs):
    count = len(distances)
    flag_ref, query_ref, grad_ref, m_ref, l_ref, r_ref = refs[:6]
    kv_refs = refs[6 : 6 + count]
    stat_ref, part_ref = refs[6 + count : 8 + count]
    out_refs = refs[8 + count : 8 + count + len(middle)]
    qs, gs, kt, s_ref, g_ref, p_ref, ds_ref = refs[8 + count + len(middle) :]
    lanes = heads * BLOCK
    rows = blocks * BLOCK
    stack_heads(query_ref, qs, blocks, heads)
    stack_heads(grad_ref, gs, blocks, heads)
    keys = [keys_of(r) for r in kv_refs]
    values = [values_of(r) for r in kv_refs]
    for c in range(len(middle)):
        kt[:, c * rows : (c + 1) * rows] = keys[c][...].T
    for i in range(blocks):
        span = slice(i * lanes, (i + 1) * lanes)
        s_i, g_i = s_ref.at[i % 2], g_ref.at[i % 2]
        top = score_pass(
            i, distances, blocks, reach, flag_ref, keys, values, qs[span, :], gs[span, :], s_i, g_i
        )
        before = m_ref[i : i + 1, :]
        top = jnp.maximum(top, before)
        base = top * SCALE_LOG2
        total, dot_total = weight_pass(i, distances, blocks, reach, flag_ref, s_i, g_i, base, True)
        fade = jnp.exp2(before * SCALE_LOG2 - base)
        total = total + l_ref[i : i + 1, :] * fade
        dot_total = dot_total + r_ref[i : i + 1, :] * fade
        inverse = 1.0 / total
        delta = dot_total * inverse
        stat_ref[0, i : i + 1, :] = base
        stat_ref[1, i : i + 1, :] = inverse
        stat_ref[2, i : i + 1, :] = delta
        gradients(i, middle, blocks, reach, lanes, s_i, g_i, p_ref, ds_ref, inverse, delta)
    for c, d in enumerate(middle):
        key_value_sums(c, d, blocks, reach, lanes, p_ref, ds_ref, qs, gs, out_refs[c])
    for i in range(blocks):
        if middle:
            part_ref[i] = query_sum(i, middle, blocks, reach, lanes, kt, ds_ref)
        else:
            part_ref[i] = jnp.zeros_like(part_ref[i])


def gradient_kernel(blocks, reach, heads, distances, final, flag_ref, query_ref, grad_ref, stat_ref, part_ref, *refs):
    count = len(distances)
    keys, values = [], []
    for d in distances:
        if d == 0:
            keys.append(refs[0])
            values.append(refs[1])
            refs = refs[2:]
        else:
            keys.append(keys_of(refs[0]))
            values.append(values_of(refs[0]))
            refs = refs[1:]
    out_refs, query_out = refs[:count], refs[count]
    qs, gs, kt, s_ref, g_ref, p_ref, ds_ref = refs[count + 1 :]
    lanes = heads * BLOCK
    rows = blocks * BLOCK
    stack_heads(query_ref, qs, blocks, heads)
    stack_heads(grad_ref, gs, blocks, heads)
    for c in range(count):
        kt[:, c * rows : (c + 1) * rows] = keys[c][...].T
    for i in range(blocks):
        span = slice(i * lanes, (i + 1) * lanes)
        s_i, g_i = s_ref.at[i % 2], g_ref.at[i % 2]
        score_pass(i, distances, blocks, reach, flag_ref, keys, values, qs[span, :], gs[span, :], s_i, g_i)
        weight_pass(i, distances, blocks, reach, flag_ref, s_i, g_i, stat_ref[0, i : i + 1, :], True)
        gradients(
            i, distances, blocks, reach, lanes, s_i, g_i, p_ref, ds_ref,
            stat_ref[1, i : i + 1, :], stat_ref[2, i : i + 1, :],
        )
    for c, d in enumerate(distances):
        key_value_sums(c, d, blocks, reach, lanes, p_ref, ds_ref, qs, gs, out_refs[c])
    for i in range(blocks):
        total = part_ref[i] + query_sum(i, distances, blocks, reach, lanes, kt, ds_ref)
        if not final:
            query_out[i] = total
            continue
        total = total * SCALE
        for h in range(heads):
            query_out[i * BLOCK : (i + 1) * BLOCK, h * HEAD_WIDTH : (h + 1) * HEAD_WIDTH] = (
                total[:, h * BLOCK : (h + 1) * BLOCK].T.astype(query_out.dtype)
            )


def kernel_call(kernel, flags, arrays, outs, scratch, weight=0):
    size = sum(a.size * a.dtype.itemsize for a in arrays) + sum(a.size * a.dtype.itemsize for a in outs)
    held = sum(math.prod(s.shape) * jnp.dtype(s.dtype).itemsize for s in scratch)
    return pl.pallas_call(
        kernel,
        out_shape=outs,
        in_specs=[pl.BlockSpec(memory_space=pltpu.SMEM)] + [pl.BlockSpec(memory_space=pltpu.VMEM)] * len(arrays),
        out_specs=[pl.BlockSpec(memory_space=pltpu.VMEM)] * len(outs),
        scratch_shapes=scratch,
        compiler_params=pltpu.CompilerParams(vmem_limit_bytes=held + size + (8 << 20)),
        cost_estimate=pl.CostEstimate(flops=0, bytes_accessed=size * weight, transcendentals=0),
    )(flags, *arrays)


def attention_flags(doc_blocks, blocks, reach, place):
    query_ids = place * blocks + jnp.arange(blocks, dtype=jnp.int32)
    column = jnp.arange((reach + 1) * blocks, dtype=jnp.int32)
    key_ids = (place - column // blocks) * blocks + column % blocks
    behind = query_ids[:, None] - key_ids[None, :]
    listed = jnp.any(doc_blocks[:, :, None] == key_ids[None, None, :], axis=1)
    allowed = (key_ids[None, :] >= 0) & ((behind == 0) | (behind == 1) | ((behind >= 2) & listed))
    return allowed.astype(jnp.int32)


def pack_kernel(jobs, rows_ref, *refs):
    count = len(jobs)
    arrays, outs, sems = refs[: -count - 1], refs[-count - 1 : -1], refs[-1]
    copies = []
    for n, (members, size) in enumerate(jobs):
        start = pl.multiple_of(rows_ref[n], size)
        at = 0
        for member in members:
            array = arrays[member]
            width = array.shape[1]
            copies.append(
                pltpu.make_async_copy(
                    array.at[pl.ds(start, size), :], outs[n].at[:, at : at + width], sems.at[len(copies)]
                )
            )
            at += width
    for copy in copies:
        copy.start()
    for copy in copies:
        copy.wait()


def packed(jobs):
    arrays, plan = [], []
    for group, _, size in jobs:
        members = []
        for array in group:
            known = [n for n, a in enumerate(arrays) if a is array]
            if not known:
                arrays.append(array)
            members.append(known[0] if known else len(arrays) - 1)
        plan.append((tuple(members), size))
    starts = jnp.stack([jnp.asarray(start, jnp.int32) for _, start, _ in jobs])
    outs = [
        jax.ShapeDtypeStruct((size, sum(arrays[m].shape[1] for m in members)), arrays[0].dtype)
        for members, size in plan
    ]
    return pl.pallas_call(
        functools.partial(pack_kernel, plan),
        out_shape=outs,
        in_specs=[pl.BlockSpec(memory_space=pltpu.SMEM)] + [pl.BlockSpec(memory_space=pl.ANY)] * len(arrays),
        out_specs=[pl.BlockSpec(memory_space=pltpu.VMEM)] * len(outs),
        scratch_shapes=[pltpu.SemaphoreType.DMA((sum(len(members) for members, _ in plan),))],
        cost_estimate=pl.CostEstimate(
            flops=0, bytes_accessed=sum(2 * o.size * o.dtype.itemsize for o in outs), transcendentals=0
        ),
    )(starts, *arrays)


def first_product_kernel(tp_count, group_count, query_width, group_ref, *refs):
    acc_ref = refs[-1]
    product_kernel(tp_count, group_count, slice(0, query_width), group_ref, refs[:-1], None, acc_ref)


def last_product_kernel(tp_count, group_count, query_width, group_ref, acc_ref, *refs):
    product_kernel(tp_count, group_count, slice(query_width, None), group_ref, refs[:-1], acc_ref, refs[-1])


def product_kernel(tp_count, group_count, columns, group_ref, refs, acc_ref, out_ref):
    pieces, refs = refs[:tp_count], refs[tp_count:]
    whole, shares = refs[:2], refs[2:]
    share = whole[0].shape[0] // group_count
    group_place = group_ref[0]
    for step in range(group_count):
        source = lax.rem(group_place - step + group_count, group_count)
        span = pl.ds(pl.multiple_of(source * share, share), share)
        total = None if acc_ref is None else acc_ref[:, span]
        for bits in range(tp_count):
            if bits < 2:
                w = whole[bits][span, columns]
            else:
                w = shares[(bits - 2) * group_count + step][:, columns]
            part = lax.dot_general(pieces[bits][...], w, NT, preferred_element_type=jnp.float32)
            total = part if total is None else total + part
        out_ref[:, span] = total.astype(out_ref.dtype)


def body(query, key_head_rows, value_head_rows, output_gradient, doc_blocks, w_query, key_weight, value_weight):
    rows = query.shape[0]
    blocks = rows // BLOCK
    heads = query.shape[1] // key_head_rows.shape[1]
    lanes = heads * BLOCK
    reach = min(8, lax.axis_size("seq") - 1)
    place = lax.axis_index("seq")
    tp_count = lax.axis_size("tp")
    tp_place = lax.axis_index("tp")
    group_count = lax.axis_size("groups")
    group_place = lax.axis_index("groups")
    rows_out = w_query.shape[0] // tp_count
    share = rows_out // group_count
    bf16, f32 = jnp.bfloat16, jnp.float32

    weights = (w_query, key_weight, value_weight)
    own_kv = (key_head_rows, value_head_rows)

    def share_of(bits):
        return ((tp_place ^ bits) * rows_out + group_place * share, share)

    early = range(2, min(3, tp_count))
    late = range(3, tp_count)
    with jax.named_scope("pack_first"):
        key_value, *sent = packed([(own_kv, 0, rows)] + [(weights, *share_of(bits)) for bits in early])
    with jax.named_scope("kv_forward"):
        window = {1: shifted(key_value, "seq", 1)}
        if reach > 1:
            window[reach] = shifted(key_value, "seq", reach)
        for d in range(2, reach):
            window[d] = shifted(window[d - 1], "seq", 1)
        far = tuple(range(2, reach + 1))
    with jax.named_scope("pack_rest"):
        held, _ = lax.optimization_barrier((weights, key_value))
        pair_weights, own_weights, *more = packed(
            [(held, (tp_place ^ 1) * rows_out, rows_out), (held, tp_place * rows_out, rows_out)]
            + [(held, *share_of(bits)) for bits in late]
        )
    with jax.named_scope("weight_exchange"):
        whole = [own_weights, swapped(pair_weights, "tp", 1)]
        sent = [swapped(piece, "tp", bits) for bits, piece in zip([*early, *late], sent + more)]

    with jax.named_scope("flags"):
        flags = attention_flags(doc_blocks, blocks, reach, place)

    def scratch(count, gradient_count):
        stacks = [pltpu.VMEM((blocks * lanes, HEAD_WIDTH), bf16)] * 2
        tiles = [pltpu.VMEM((2, count * rows, lanes), f32)] * 2
        if not gradient_count:
            return stacks + tiles
        turned = [pltpu.VMEM((HEAD_WIDTH, gradient_count * rows), bf16)]
        return stacks + turned + tiles + [pltpu.VMEM((gradient_count * rows, blocks * lanes), bf16)] * 2

    near_in = [query, output_gradient, key_head_rows, value_head_rows, window[1]]
    stats = [jax.ShapeDtypeStruct((blocks, lanes), f32)] * 3
    near_in[0], pair_weights = lax.optimization_barrier((near_in[0], pair_weights))
    with jax.named_scope("near_stats"):
        top, total, dot_total = kernel_call(
            functools.partial(near_stats_kernel, blocks, reach, heads),
            flags, near_in, stats, scratch(2, 0),
        )
    grads = {}
    kv_shape = (rows, 2 * HEAD_WIDTH)
    part_shape = jax.ShapeDtypeStruct((blocks, HEAD_WIDTH, lanes), f32)
    if far:
        middle = far[:-1]
        with jax.named_scope("far_stats"):
            stat, part, *middle_grads = kernel_call(
                functools.partial(far_kernel, blocks, reach, heads, far, middle),
                flags,
                [query, output_gradient, top, total, dot_total] + [window[d] for d in far],
                [jax.ShapeDtypeStruct((3, blocks, lanes), f32), part_shape]
                + [jax.ShapeDtypeStruct(kv_shape, bf16)] * len(middle),
                scratch(len(far), max(len(middle), 1)),
            )
        grads = dict(zip(middle, middle_grads))
        with jax.named_scope("longest_gradients"):
            grads[reach], part = kernel_call(
                functools.partial(gradient_kernel, blocks, reach, heads, (reach,), False),
                flags,
                [query, output_gradient, stat, part, window[reach]],
                [jax.ShapeDtypeStruct(kv_shape, bf16), part_shape],
                scratch(1, 1),
            )
    else:
        stat = jnp.stack([top * SCALE_LOG2, 1.0 / total, dot_total / total])
        part = jnp.zeros(part_shape.shape, f32)
    def passed_on(piece, after):
        held, _ = lax.optimization_barrier((piece, after))
        moved = [piece]
        for step in range(1, group_count):
            route = [(i, (i + step) % group_count) for i in range(group_count)]
            moved.append(lax.ppermute(held, "groups", route))
        return moved

    with jax.named_scope("weight_exchange"):
        shares = passed_on(sent[0], stat) if sent else []

    with jax.named_scope("near_gradients"):
        own, grads[1], query_grad = kernel_call(
            functools.partial(gradient_kernel, blocks, reach, heads, (0, 1), True),
            flags,
            [query, output_gradient, stat, part, key_head_rows, value_head_rows, window[1]],
            [
                jax.ShapeDtypeStruct(kv_shape, f32),
                jax.ShapeDtypeStruct(kv_shape, f32),
                jax.ShapeDtypeStruct(query.shape, bf16),
            ],
            scratch(2, 2),
        )

    with jax.named_scope("weight_exchange"):
        for piece in sent[1:]:
            shares += passed_on(piece, query_grad)
    with jax.named_scope("kv_return"):
        if far:
            longest = shifted(grads[reach], "seq", -reach)
            passed = None
            for d in range(reach - 1, 0, -1):
                total = grads[d] if passed is None else (grads[d].astype(f32) + passed.astype(f32))
                total = total.astype(bf16)
                passed = shifted(total, "seq", -1)
        else:
            passed = shifted(grads[1].astype(bf16), "seq", -1)
        if far:
            longest, passed, *shares[1:2] = lax.optimization_barrier((longest, passed, *shares[1:2]))
            own = own + longest.astype(f32)
        key_value_grad = (own + passed.astype(f32)).astype(bf16)

    def gathered(block, before_last=None):
        pieces = {0: block, 1: swapped(block, "tp", 1)}
        for bits in range(2, tp_count, 2):
            pieces[bits] = swapped(block, "tp", bits)
            held = pieces[bits]
            if before_last is not None:
                held, _ = lax.optimization_barrier((held, before_last))
            pieces[bits + 1] = swapped(held, "tp", 1)
        return [pieces[bits] for bits in range(tp_count)]

    with jax.named_scope("query_grad_gather"):
        q_pieces = gathered(query_grad)
    group = jnp.full((1,), group_place, jnp.int32)
    out = jax.ShapeDtypeStruct((rows, rows_out), bf16)
    width = query.shape[1]
    with jax.named_scope("query_product"):
        (acc,) = kernel_call(
            functools.partial(first_product_kernel, tp_count, group_count, width),
            group, q_pieces + whole + shares, [jax.ShapeDtypeStruct((rows, rows_out), f32)], [], 1,
        )
    with jax.named_scope("kv_grad_gather"):
        kv_pieces = gathered(key_value_grad, acc)
    with jax.named_scope("kv_product"):
        (result,) = kernel_call(
            functools.partial(last_product_kernel, tp_count, group_count, width),
            group, [acc] + kv_pieces + whole + shares, [out], [], 1,
        )
    return result


def solution(mesh):
    in_specs = (
        P(("groups", "seq"), "tp"),
        P(("groups", "seq"), "tp"),
        P(("groups", "seq"), "tp"),
        P(("groups", "seq"), "tp"),
        P(("groups", "seq"), None),
        P(None, "tp"),
        P(None, "tp"),
        P(None, "tp"),
    )
    out_specs = P(("groups", "seq"), "tp")
    return jax.shard_map(body, mesh=mesh, in_specs=in_specs, out_specs=out_specs, check_vma=False)
```

time: 110 us -> 80.8 us (0.73)
  waiting for transfers between devices: 52.1 us -> 20.9 us
  Pallas kernels: 16 us -> 33.1 us
  matrix products: 7.65 us -> 0 us
  local copies, waits for them, and re-layouts: 8.52 us -> 0.92 us
    ppermute x12 -> x9, waiting for transfers between devices: 16.2 us -> 2.85 us  [swapped(): lax.ppermute(block, axis, [(i, i ^ bits) for i in range(lax.axis_size(axi...]
    ppermute x4 -> x2, waiting for transfers between devices: 21.6 us -> 9.25 us  [passed_on(): moved.append(lax.ppermute(held, 'groups', route))]
    pallas_call x3 -> x6, Pallas kernels: 16 us -> 25.4 us  [kernel_call(): pl.pallas_call(kernel, out_shape=outs, in_specs=[pl.BlockSpec(memory_spac...]
    pallas_call x0 -> x2, Pallas kernels: none -> 7.72 us  [packed(): pl.pallas_call(functools.partial(pack_kernel, plan), out_shape=outs, in_s...]
    dot_general x8 -> x0, matrix products: 7.65 us -> none  [body(): lax.dot_general(pieces[bits], weights[bits], NT, preferred_element_type=f32)]
    ppermute x6, waiting for transfers between devices: 14.2 us -> 8.84 us  [shifted(): return lax.ppermute(block, axis, route)]
    dynamic_slice x4 -> x0, local copies, waits for them, and re-layouts: 4.61 us -> none  [weight_pieces(): lax.dynamic_slice_in_dim(w, peer * rows_out + group_place * share, share,...]
    dynamic_update_slice x8 -> x0, local copies, waits for them, and re-layouts: 3.2 us -> none  [the longest x4 3.07 us: gathered_rows(): lax.dynamic_update_slice_in_dim(whole, piece, group_place * share, axis=0)]
  transfers between devices with their start and end apart: 22 -> 17, of which waited for: 9 -> 6; matrix products, arithmetic and copies ran while one was open for 13% -> 1% of each run, Pallas kernels for 15% -> 34%
where the time goes in v2:
time: 80.8 us; the launch traced here: 79.8 us
  Pallas kernels  33.1 us (41%)
  starting transfers between devices  23 us (28%)
  waiting for transfers between devices  20.9 us (26%)
  other arithmetic  1.6 us (2%)
  local copies, waits for them, and re-layouts  0.92 us (1%)
    pallas_call x6, Pallas kernels, kernel_call(): pl.pallas_call(kernel, out_shape=outs, in_specs=[pl.BlockSpec(memory_spac...  25.4 us
    ppermute x6, starting transfers between devices, shifted(): return lax.ppermute(block, axis, route)  14.5 us
    ppermute x2, waiting for transfers between devices, passed_on(): moved.append(lax.ppermute(held, 'groups', route))  9.25 us
    ppermute x6, waiting for transfers between devices, shifted(): return lax.ppermute(block, axis, route)  8.84 us
    pallas_call x2, Pallas kernels, packed(): pl.pallas_call(functools.partial(pack_kernel, plan), out_shape=outs, in_s...  7.72 us
    ppermute x9, starting transfers between devices, swapped(): lax.ppermute(block, axis, [(i, i ^ bits) for i in range(lax.axis_size(axi...  5.62 us
    ppermute x2, starting transfers between devices, passed_on(): moved.append(lax.ppermute(held, 'groups', route))  2.94 us
    ppermute x9, waiting for transfers between devices, swapped(): lax.ppermute(block, axis, [(i, i ^ bits) for i in range(lax.axis_size(axi...  2.85 us
  transfers between devices with their start and end apart: 17, of which 6 were waited for; matrix products, arithmetic and copies ran while one was open for 1% of the time, Pallas kernels for 34%

profile of v2, /device:TPU:0, one launch (start us, length us, event | category | flops | bytes accessed | tf_op | source)
XLA Modules:
  0.0 79.8 jit_solution(11737307992521656263)
XLA Ops:
  0.7 2.9 %pack_first.1 = (bf16[512,256]{1,0:T(8,128)(2,1)}, bf16[512,768]{1,0:T(8,128)(2,1)}) custom-call(s32[2]{0:T(128)} %pad_add_fusion.1.rows_ref, bf16[512,128]{1,0:T(8,128)(2,1)} %refs_0_.4, bf16[512,128]{1,0:T(8,128)(2,1)} %refs_1_.6, bf16[4096,512]{1,0:T(8,128)(2,1)} %refs_0_.3, bf16[4096,128]{1,0:T(8,128)(2,1)} %refs_1_.4, bf16[4096,128]{1,0:T(8,128)(2,1)} %refs_2_.3), custom_call_target="tpu_custom_call" | custom-call | bytes 2097152 | tf_op jit(solution)/shard_map/pack_first/pallas_call | solution.py:329
  3.6 5.6 %collective-permute-start = (bf16[512,256]{1,0:T(8,128)(2,1)}, bf16[512,256]{1,0:T(8,128)(2,1)}, u32[]{:S(2)}, u32[]{:S(2)}) collective-permute-start(bf16[512,256]{1,0:T(8,128)(2,1)} %get-tuple-element.31), channel_id=1, source_target_pairs={{0,4},{4,8},{8,12},{1,5},{5,9},{9,13},{2,6},{6,10},{10,14},{3,7},{... | collective-permute-start | bytes 786440 | tf_op jit(solution)/shard_map/kv_forward/ppermute | solution.py:22
  9.2 3.3 %collective-permute-start.2 = (bf16[512,256]{1,0:T(8,128)(2,1)}, bf16[512,256]{1,0:T(8,128)(2,1)}, u32[]{:S(2)}, u32[]{:S(2)}) collective-permute-start(bf16[512,256]{1,0:T(8,128)(2,1)} %get-tuple-element.31), channel_id=1, source_target_pairs={{0,12},{1,13},{2,14},{3,15},{16,28},{17,29},{18,30},{19,31}} | collective-permute-start | bytes 786440 | tf_op jit(solution)/shard_map/kv_forward/ppermute | solution.py:22
  12.5 1.5 %collective-permute-start.7 = (bf16[512,768]{1,0:T(8,128)(2,1)}, bf16[512,768]{1,0:T(8,128)(2,1)S(1)}, u32[]{:S(2)}, u32[]{:S(2)}) collective-permute-start(bf16[512,768]{1,0:T(8,128)(2,1)} %get-tuple-element.45), channel_id=1, source_target_pairs={{0,2},{1,3},{2,0},{3,1},{4,6},{5,7},{6,4},{7,5},{8,10},{9,11},{10,... | collective-permute-start | bytes 2359304 | tf_op jit(solution)/shard_map/weight_exchange/ppermute | solution.py:26
  14.6 4.8 %pack_rest.1 = (bf16[1024,768]{1,0:T(8,128)(2,1)}, bf16[1024,768]{1,0:T(8,128)(2,1)}, bf16[512,768]{1,0:T(8,128)(2,1)}) custom-call(s32[3]{0:T(128)} %pad_add_fusion.rows_ref, bf16[4096,512]{1,0:T(8,128)(2,1)} %refs_0_.3, bf16[4096,128]{1,0:T(8,128)(2,1)} %refs_1_.4, bf16[4096,128]{1,0:T(8,128)(2,1)} %refs_2_.3), custom_call_target="tpu_custom_call" | custom-call | bytes 7864320 | tf_op jit(solution)/shard_map/pack_rest/pallas_call | solution.py:329
  20.3 1.3 %collective-permute-start.1 = (bf16[512,256]{1,0:T(8,128)(2,1)}, bf16[512,256]{1,0:T(8,128)(2,1)S(1)}, u32[]{:S(2)}, u32[]{:S(2)}) collective-permute-start(bf16[512,256]{1,0:T(8,128)(2,1)} %collective-permute-done.kv1.refs_2_), channel_id=1, source_target_pairs={{0,4},{4,8},{8,12},{1,5},{5,9},{9,13},{2,6},{6,10},{10,14},{3,7},{... | collective-permute-start | bytes 786440 | tf_op jit(solution)/shard_map/kv_forward/ppermute | solution.py:22
  22.6 3.9 %near_stats.1 = (f32[4,512]{1,0:T(4,128)S(1)}, f32[4,512]{1,0:T(4,128)S(1)}, f32[4,512]{1,0:T(4,128)S(1)}) custom-call(s32[4,16]{1,0:T(4,128)S(1)} %fusion.4.flag_ref.refs_0_, bf16[512,512]{1,0:T(8,128)(2,1)S(1)} %copy-done, bf16[512,512]{1,0:T(8,128)(2,1)S(1)} %copy-done.1, bf16[512,128]{1,0:T(8,128)(2,1)S(1)} %copy-done.3, bf16[512,128]{1,0:T(8,128)(2,1)S(1)} %copy-done.4, ...), custom_call_target="tpu_custom_call" | custom-call | tf_op jit(solution)/shard_map/near_stats/pallas_call | solution.py:271
  26.6 1.3 %collective-permute-done.1.refs_6_ = bf16[512,256]{1,0:T(8,128)(2,1)S(1)} collective-permute-done((bf16[512,256]{1,0:T(8,128)(2,1)}, bf16[512,256]{1,0:T(8,128)(2,1)S(1)}, u32[]{:S(2)}, u32[]{:S(2)}) %collective-permute-start.1) | collective-permute-done | bytes 262176 | tf_op jit(solution)/shard_map/kv_forward/ppermute | solution.py:22
  27.9 6.1 %far_stats.1 = (f32[3,4,512]{2,1,0:T(4,128)S(1)}, f32[4,128,512]{2,1,0:T(8,128)S(1)}, bf16[512,256]{1,0:T(8,128)(2,1)S(1)}) custom-call(s32[4,16]{1,0:T(4,128)S(1)} %fusion.4.flag_ref.refs_0_, bf16[512,512]{1,0:T(8,128)(2,1)S(1)} %copy-done, bf16[512,512]{1,0:T(8,128)(2,1)S(1)} %copy-done.1, f32[4,512]{1,0:T(4,128)S(1)} %get-tuple-element.37.refs_3_, ...), custom_call_target="tpu_custom_call" | custom-call | tf_op jit(solution)/shard_map/far_stats/pallas_call | solution.py:271
  34.0 1.4 %collective-permute-start.9 = (bf16[512,256]{1,0:T(8,128)(2,1)S(1)}, bf16[512,256]{1,0:T(8,128)(2,1)S(1)}, u32[]{:S(2)}, u32[]{:S(2)}) collective-permute-start(bf16[512,256]{1,0:T(8,128)(2,1)S(1)} %get-tuple-element.48), channel_id=1, source_target_pairs={{4,0},{8,4},{12,8},{5,1},{9,5},{13,9},{6,2},{10,6},{14,10},{7,3},{... | collective-permute-start | bytes 786440 | tf_op jit(solution)/shard_map/kv_return/ppermute | solution.py:22
  35.4 1.6 %collective-permute-start.11 = (bf16[512,768]{1,0:T(8,128)(2,1)S(1)}, bf16[512,768]{1,0:T(8,128)(2,1)S(1)}, u32[]{:S(2)}, u32[]{:S(2)}) collective-permute-start(bf16[512,768]{1,0:T(8,128)(2,1)S(1)} %collective-permute-done.7.refs_6_), channel_id=1, source_target_pairs={{0,16},{16,0},{1,17},{17,1},{2,18},{18,2},{3,19},{19,3},{4,20},{20... | collective-permute-start | bytes 2359304 | tf_op jit(solution)/shard_map/weight_exchange/ppermute | solution.py:461
  37.0 2.9 %longest_gradients.1 = (bf16[512,256]{1,0:T(8,128)(2,1)S(1)}, f32[4,128,512]{2,1,0:T(8,128)S(1)}) custom-call(s32[4,16]{1,0:T(4,128)S(1)} %fusion.4.flag_ref.refs_0_, bf16[512,512]{1,0:T(8,128)(2,1)S(1)} %copy-done, bf16[512,512]{1,0:T(8,128)(2,1)S(1)} %copy-done.1, f32[3,4,512]{2,1,0:T(4,128)S(1)} %get-tuple-element.40.stat_ref, ...), custom_call_target="tpu_custom_call" | custom-call | tf_op jit(solution)/shard_map/longest_gradients/pallas_call | solution.py:271
  39.9 1.5 %collective-permute-start.8 = (bf16[512,256]{1,0:T(8,128)(2,1)S(1)}, bf16[512,256]{1,0:T(8,128)(2,1)S(1)}, u32[]{:S(2)}, u32[]{:S(2)}) collective-permute-start(bf16[512,256]{1,0:T(8,128)(2,1)S(1)} %get-tuple-element.46), channel_id=1, source_target_pairs={{12,0},{13,1},{14,2},{15,3},{28,16},{29,17},{30,18},{31,19}} | collective-permute-start | bytes 786440 | tf_op jit(solution)/shard_map/kv_return/ppermute | solution.py:22
  41.4 5.6 %near_gradients.1 = (f32[512,256]{1,0:T(8,128)S(1)}, f32[512,256]{1,0:T(8,128)S(1)}, bf16[512,512]{1,0:T(8,128)(2,1)S(1)}) custom-call(s32[4,16]{1,0:T(4,128)S(1)} %fusion.4.flag_ref.refs_0_, bf16[512,512]{1,0:T(8,128)(2,1)S(1)} %copy-done, bf16[512,512]{1,0:T(8,128)(2,1)S(1)} %copy-done.1, f32[3,4,512]{2,1,0:T(4,128)S(1)} %get-tuple-element.40.stat_ref, ...), custom_call_target="tpu_custom_call" | custom-call | tf_op jit(solution)/shard_map/near_gradients/pallas_call | solution.py:271
  47.0 1.6 %collective-permute-start.4 = (bf16[512,512]{1,0:T(8,128)(2,1)S(1)}, bf16[512,512]{1,0:T(8,128)(2,1)S(1)}, u32[]{:S(2)}, u32[]{:S(2)}) collective-permute-start(bf16[512,512]{1,0:T(8,128)(2,1)S(1)} %get-tuple-element.43.refs_0_), channel_id=1, source_target_pairs={{0,2},{1,3},{2,0},{3,1},{4,6},{5,7},{6,4},{7,5},{8,10},{9,11},{10,... | collective-permute-start | bytes 1572872 | tf_op jit(solution)/shard_map/query_grad_gather/ppermute | solution.py:26
  50.0 1.7 %collective-permute-done.8 = bf16[512,256]{1,0:T(8,128)(2,1)S(1)} collective-permute-done((bf16[512,256]{1,0:T(8,128)(2,1)S(1)}, bf16[512,256]{1,0:T(8,128)(2,1)S(1)}, u32[]{:S(2)}, u32[]{:S(2)}) %collective-permute-start.8) | collective-permute-done | bytes 262176 | tf_op jit(solution)/shard_map/kv_return/ppermute | solution.py:22
  51.7 1.4 %collective-permute-start.13 = (bf16[512,768]{1,0:T(8,128)(2,1)}, bf16[512,768]{1,0:T(8,128)(2,1)S(1)}, u32[]{:S(2)}, u32[]{:S(2)}) collective-permute-start(bf16[512,768]{1,0:T(8,128)(2,1)} %collective-permute-done.12.refs_8_), channel_id=1, source_target_pairs={{0,16},{16,0},{1,17},{17,1},{2,18},{18,2},{3,19},{19,3},{4,20},{20... | collective-permute-start | bytes 2359304 | tf_op jit(solution)/shard_map/weight_exchange/ppermute | solution.py:461
  53.0 5.8 %collective-permute-done.10 = bf16[512,256]{1,0:T(8,128)(2,1)S(1)} collective-permute-done((bf16[512,256]{1,0:T(8,128)(2,1)S(1)}, bf16[512,256]{1,0:T(8,128)(2,1)S(1)}, u32[]{:S(2)}, u32[]{:S(2)}) %collective-permute-start.10) | collective-permute-done | bytes 262176 | tf_op jit(solution)/shard_map/kv_return/ppermute | solution.py:22
  58.8 1.3 %collective-permute-done.4.refs_2_ = bf16[512,512]{1,0:T(8,128)(2,1)S(1)} collective-permute-done((bf16[512,512]{1,0:T(8,128)(2,1)S(1)}, bf16[512,512]{1,0:T(8,128)(2,1)S(1)}, u32[]{:S(2)}, u32[]{:S(2)}) %collective-permute-start.4) | collective-permute-done | bytes 524320 | tf_op jit(solution)/shard_map/query_grad_gather/ppermute | solution.py:26
  60.2 1.6 %collective-permute-start.15 = (bf16[512,256]{1,0:T(8,128)(2,1)S(1)}, bf16[512,256]{1,0:T(8,128)(2,1)S(1)}, u32[]{:S(2)}, u32[]{:S(2)}) collective-permute-start(bf16[512,256]{1,0:T(8,128)(2,1)S(1)} %add_convert_fusion.refs_0_), channel_id=1, source_target_pairs={{0,2},{1,3},{2,0},{3,1},{4,6},{5,7},{6,4},{7,5},{8,10},{9,11},{10,... | collective-permute-start | bytes 786440 | tf_op jit(solution)/shard_map/kv_grad_gather/ppermute | solution.py:26
  62.0 9.2 %collective-permute-done.13.refs_9_ = bf16[512,768]{1,0:T(8,128)(2,1)S(1)} collective-permute-done((bf16[512,768]{1,0:T(8,128)(2,1)}, bf16[512,768]{1,0:T(8,128)(2,1)S(1)}, u32[]{:S(2)}, u32[]{:S(2)}) %collective-permute-start.13) | collective-permute-done | bytes 786464 | tf_op jit(solution)/shard_map/weight_exchange/ppermute | solution.py:461
  71.3 3.5 %query_product.1.acc_ref = f32[512,1024]{1,0:T(8,128)S(1)} custom-call(s32[1]{0:T(128)} %bitcast.group_ref, bf16[512,512]{1,0:T(8,128)(2,1)S(1)} %get-tuple-element.43.refs_0_, bf16[512,512]{1,0:T(8,128)(2,1)S(1)} %collective-permute-done.3.refs_1_, bf16[512,512]{1,0:T(8,128)(2,1)S(1)} %collective-permute-done.4.refs_2_, ...), custom_call_target="tpu_custom_call" | custom-call | bytes 10485760 | tf_op jit(solution)/shard_map/query_product/pallas_call | solution.py:271
  74.9 1.5 %collective-permute-done.16.refs_3_ = bf16[512,256]{1,0:T(8,128)(2,1)S(1)} collective-permute-done((bf16[512,256]{1,0:T(8,128)(2,1)S(1)}, bf16[512,256]{1,0:T(8,128)(2,1)S(1)}, u32[]{:S(2)}, u32[]{:S(2)}) %collective-permute-start.16) | collective-permute-done | bytes 262176 | tf_op jit(solution)/shard_map/kv_grad_gather/ppermute | solution.py:26
  76.4 3.4 %kv_product.1 = bf16[512,1024]{1,0:T(8,128)(2,1)} custom-call(s32[1]{0:T(128)} %bitcast.group_ref, f32[512,1024]{1,0:T(8,128)S(1)} %query_product.1.acc_ref, bf16[512,256]{1,0:T(8,128)(2,1)S(1)} %add_convert_fusion.refs_0_, bf16[512,256]{1,0:T(8,128)(2,1)S(1)} %collective-permute-done.14.refs_1_, bf16[512,256]{1,0:T(8,128)(2,1)S(1)} %collective-permute-done.15.refs_2_, ...), custom_call_target="tpu_custom_call" | custom-call | bytes 10485760 | tf_op jit(solution)/shard_map/kv_product/pallas_call | solution.py:271
  (41 shorter events, 4.9 us)
Async XLA Ops:
  3.6 16.7 %collective-permute-start = (bf16[512,256]{1,0:T(8,128)(2,1)}, bf16[512,256]{1,0:T(8,128)(2,1)}, u32[]{:S(2)}, u32[]{:S(2)}) collective-permute-start(bf16[512,256]{1,0:T(8,128)(2,1)} %get-tuple-element.31), channel_id=1, source_target_pairs={{0,4},{4,8},{8,12},{1,5},{5,9},{9,13},{2,6},{6,10},{10,14},{3,7},{... | collective-permute-start | bytes 786440 | tf_op jit(solution)/shard_map/kv_forward/ppermute | solution.py:22
  9.2 17.3 %collective-permute-start.2 = (bf16[512,256]{1,0:T(8,128)(2,1)}, bf16[512,256]{1,0:T(8,128)(2,1)}, u32[]{:S(2)}, u32[]{:S(2)}) collective-permute-start(bf16[512,256]{1,0:T(8,128)(2,1)} %get-tuple-element.31), channel_id=1, source_target_pairs={{0,12},{1,13},{2,14},{3,15},{16,28},{17,29},{18,30},{19,31}} | collective-permute-start | bytes 786440 | tf_op jit(solution)/shard_map/kv_forward/ppermute | solution.py:22
  12.5 22.9 %collective-permute-start.7 = (bf16[512,768]{1,0:T(8,128)(2,1)}, bf16[512,768]{1,0:T(8,128)(2,1)S(1)}, u32[]{:S(2)}, u32[]{:S(2)}) collective-permute-start(bf16[512,768]{1,0:T(8,128)(2,1)} %get-tuple-element.45), channel_id=1, source_target_pairs={{0,2},{1,3},{2,0},{3,1},{4,6},{5,7},{6,4},{7,5},{8,10},{9,11},{10,... | collective-permute-start | bytes 2359304 | tf_op jit(solution)/shard_map/weight_exchange/ppermute | solution.py:26
  14.6 5.6 %copy-start.6 = (s32[4,8]{1,0:T(4,128)S(1)}, s32[4,8]{1,0:T(4,128)}, u32[]{:S(2)}) copy-start(s32[4,8]{1,0:T(4,128)} %param.12) | copy-start | bytes 388
  14.6 7.1 %copy-start = (bf16[512,512]{1,0:T(8,128)(2,1)S(1)}, bf16[512,512]{1,0:T(8,128)(2,1)}, u32[]{:S(2)}) copy-start(bf16[512,512]{1,0:T(8,128)(2,1)} %query_ref.4) | copy-start | bytes 1572868
  14.6 7.1 %copy-start.1 = (bf16[512,512]{1,0:T(8,128)(2,1)S(1)}, bf16[512,512]{1,0:T(8,128)(2,1)}, u32[]{:S(2)}) copy-start(bf16[512,512]{1,0:T(8,128)(2,1)} %grad_ref.5) | copy-start | bytes 1572868
  14.6 7.1 %copy-start.3 = (bf16[512,128]{1,0:T(8,128)(2,1)S(1)}, bf16[512,128]{1,0:T(8,128)(2,1)}, u32[]{:S(2)}) copy-start(bf16[512,128]{1,0:T(8,128)(2,1)} %refs_0_.4) | copy-start | bytes 393220
  19.5 29.2 %collective-permute-start.12 = (bf16[512,768]{1,0:T(8,128)(2,1)}, bf16[512,768]{1,0:T(8,128)(2,1)}, u32[]{:S(2)}, u32[]{:S(2)}) collective-permute-start(bf16[512,768]{1,0:T(8,128)(2,1)} %get-tuple-element.51), channel_id=1, source_target_pairs={{0,3},{1,2},{2,1},{3,0},{4,7},{5,6},{6,5},{7,4},{8,11},{9,10},{10,... | collective-permute-start | bytes 2359304 | tf_op jit(solution)/shard_map/weight_exchange/ppermute | solution.py:26
  19.5 51.7 %collective-permute-start.6 = (bf16[1024,768]{1,0:T(8,128)(2,1)}, bf16[1024,768]{1,0:T(8,128)(2,1)S(1)}, u32[]{:S(2)}, u32[]{:S(2)}) collective-permute-start(bf16[1024,768]{1,0:T(8,128)(2,1)} %get-tuple-element.35), channel_id=1, source_target_pairs={{0,1},{1,0},{2,3},{3,2},{4,5},{5,4},{6,7},{7,6},{8,9},{9,8},{10,11... | collective-permute-start | bytes 4718600 | tf_op jit(solution)/shard_map/weight_exchange/ppermute | solution.py:26
  20.3 7.6 %collective-permute-start.1 = (bf16[512,256]{1,0:T(8,128)(2,1)}, bf16[512,256]{1,0:T(8,128)(2,1)S(1)}, u32[]{:S(2)}, u32[]{:S(2)}) collective-permute-start(bf16[512,256]{1,0:T(8,128)(2,1)} %collective-permute-done.kv1.refs_2_), channel_id=1, source_target_pairs={{0,4},{4,8},{8,12},{1,5},{5,9},{9,13},{2,6},{6,10},{10,14},{3,7},{... | collective-permute-start | bytes 786440 | tf_op jit(solution)/shard_map/kv_forward/ppermute | solution.py:22
  21.7 0.9 %copy-start.4 = (bf16[512,128]{1,0:T(8,128)(2,1)S(1)}, bf16[512,128]{1,0:T(8,128)(2,1)}, u32[]{:S(2)}) copy-start(bf16[512,128]{1,0:T(8,128)(2,1)} %refs_1_.6) | copy-start | bytes 393220
  34.0 7.4 %copy-start.5 = (bf16[512,128]{1,0:T(8,128)(2,1)S(1)}, bf16[512,128]{1,0:T(8,128)(2,1)}, u32[]{:S(2)}) copy-start(bf16[512,128]{1,0:T(8,128)(2,1)} %refs_1_.6) | copy-start | bytes 393220
  34.0 13.0 %collective-permute-start.9 = (bf16[512,256]{1,0:T(8,128)(2,1)S(1)}, bf16[512,256]{1,0:T(8,128)(2,1)S(1)}, u32[]{:S(2)}, u32[]{:S(2)}) collective-permute-start(bf16[512,256]{1,0:T(8,128)(2,1)S(1)} %get-tuple-element.48), channel_id=1, source_target_pairs={{4,0},{8,4},{12,8},{5,1},{9,5},{13,9},{6,2},{10,6},{14,10},{7,3},{... | collective-permute-start | bytes 786440 | tf_op jit(solution)/shard_map/kv_return/ppermute | solution.py:22
  35.4 24.7 %collective-permute-start.11 = (bf16[512,768]{1,0:T(8,128)(2,1)S(1)}, bf16[512,768]{1,0:T(8,128)(2,1)S(1)}, u32[]{:S(2)}, u32[]{:S(2)}) collective-permute-start(bf16[512,768]{1,0:T(8,128)(2,1)S(1)} %collective-permute-done.7.refs_6_), channel_id=1, source_target_pairs={{0,16},{16,0},{1,17},{17,1},{2,18},{18,2},{3,19},{19,3},{4,20},{20... | collective-permute-start | bytes 2359304 | tf_op jit(solution)/shard_map/weight_exchange/ppermute | solution.py:461
  39.9 11.8 %collective-permute-start.8 = (bf16[512,256]{1,0:T(8,128)(2,1)S(1)}, bf16[512,256]{1,0:T(8,128)(2,1)S(1)}, u32[]{:S(2)}, u32[]{:S(2)}) collective-permute-start(bf16[512,256]{1,0:T(8,128)(2,1)S(1)} %get-tuple-element.46), channel_id=1, source_target_pairs={{12,0},{13,1},{14,2},{15,3},{28,16},{29,17},{30,18},{31,19}} | collective-permute-start | bytes 786440 | tf_op jit(solution)/shard_map/kv_return/ppermute | solution.py:22
  47.0 24.3 %copy-start.2 = (bf16[1024,768]{1,0:T(8,128)(2,1)S(1)}, bf16[1024,768]{1,0:T(8,128)(2,1)}, u32[]{:S(2)}) copy-start(bf16[1024,768]{1,0:T(8,128)(2,1)} %get-tuple-element.44.refs_4_) | copy-start | bytes 4718596
  47.0 13.1 %collective-permute-start.4 = (bf16[512,512]{1,0:T(8,128)(2,1)S(1)}, bf16[512,512]{1,0:T(8,128)(2,1)S(1)}, u32[]{:S(2)}, u32[]{:S(2)}) collective-permute-start(bf16[512,512]{1,0:T(8,128)(2,1)S(1)} %get-tuple-element.43.refs_0_), channel_id=1, source_target_pairs={{0,2},{1,3},{2,0},{3,1},{4,6},{5,7},{6,4},{7,5},{8,10},{9,11},{10,... | collective-permute-start | bytes 1572872 | tf_op jit(solution)/shard_map/query_grad_gather/ppermute | solution.py:26
  48.7 10.1 %collective-permute-start.10 = (bf16[512,256]{1,0:T(8,128)(2,1)S(1)}, bf16[512,256]{1,0:T(8,128)(2,1)S(1)}, u32[]{:S(2)}, u32[]{:S(2)}) collective-permute-start(bf16[512,256]{1,0:T(8,128)(2,1)S(1)} %add_convert_fusion.1), channel_id=1, source_target_pairs={{4,0},{8,4},{12,8},{5,1},{9,5},{13,9},{6,2},{10,6},{14,10},{7,3},{... | collective-permute-start | bytes 786440 | tf_op jit(solution)/shard_map/kv_return/ppermute | solution.py:22
  51.7 19.6 %collective-permute-start.13 = (bf16[512,768]{1,0:T(8,128)(2,1)}, bf16[512,768]{1,0:T(8,128)(2,1)S(1)}, u32[]{:S(2)}, u32[]{:S(2)}) collective-permute-start(bf16[512,768]{1,0:T(8,128)(2,1)} %collective-permute-done.12.refs_8_), channel_id=1, source_target_pairs={{0,16},{16,0},{1,17},{17,1},{2,18},{18,2},{3,19},{19,3},{4,20},{20... | collective-permute-start | bytes 2359304 | tf_op jit(solution)/shard_map/weight_exchange/ppermute | solution.py:461
  58.8 3.0 %collective-permute-start.3 = (bf16[512,512]{1,0:T(8,128)(2,1)S(1)}, bf16[512,512]{1,0:T(8,128)(2,1)S(1)}, u32[]{:S(2)}, u32[]{:S(2)}) collective-permute-start(bf16[512,512]{1,0:T(8,128)(2,1)S(1)} %get-tuple-element.43.refs_0_), channel_id=1, source_target_pairs={{0,1},{1,0},{2,3},{3,2},{4,5},{5,4},{6,7},{7,6},{8,9},{9,8},{10,11... | collective-permute-start | bytes 1572872 | tf_op jit(solution)/shard_map/query_grad_gather/ppermute | solution.py:26
  60.1 1.9 %collective-permute-start.5 = (bf16[512,512]{1,0:T(8,128)(2,1)S(1)}, bf16[512,512]{1,0:T(8,128)(2,1)S(1)}, u32[]{:S(2)}, u32[]{:S(2)}) collective-permute-start(bf16[512,512]{1,0:T(8,128)(2,1)S(1)} %collective-permute-done.4.refs_2_), channel_id=1, source_target_pairs={{0,1},{1,0},{2,3},{3,2},{4,5},{5,4},{6,7},{7,6},{8,9},{9,8},{10,11... | collective-permute-start | bytes 1572872 | tf_op jit(solution)/shard_map/query_grad_gather/ppermute | solution.py:26
  60.2 14.6 %collective-permute-start.15 = (bf16[512,256]{1,0:T(8,128)(2,1)S(1)}, bf16[512,256]{1,0:T(8,128)(2,1)S(1)}, u32[]{:S(2)}, u32[]{:S(2)}) collective-permute-start(bf16[512,256]{1,0:T(8,128)(2,1)S(1)} %add_convert_fusion.refs_0_), channel_id=1, source_target_pairs={{0,2},{1,3},{2,0},{3,1},{4,6},{5,7},{6,4},{7,5},{8,10},{9,11},{10,... | collective-permute-start | bytes 786440 | tf_op jit(solution)/shard_map/kv_grad_gather/ppermute | solution.py:26
  61.8 13.1 %collective-permute-start.14 = (bf16[512,256]{1,0:T(8,128)(2,1)S(1)}, bf16[512,256]{1,0:T(8,128)(2,1)S(1)}, u32[]{:S(2)}, u32[]{:S(2)}) collective-permute-start(bf16[512,256]{1,0:T(8,128)(2,1)S(1)} %add_convert_fusion.refs_0_), channel_id=1, source_target_pairs={{0,1},{1,0},{2,3},{3,2},{4,5},{5,4},{6,7},{7,6},{8,9},{9,8},{10,11... | collective-permute-start | bytes 786440 | tf_op jit(solution)/shard_map/kv_grad_gather/ppermute | solution.py:26
  74.8 1.6 %collective-permute-start.16 = (bf16[512,256]{1,0:T(8,128)(2,1)S(1)}, bf16[512,256]{1,0:T(8,128)(2,1)S(1)}, u32[]{:S(2)}, u32[]{:S(2)}) collective-permute-start(bf16[512,256]{1,0:T(8,128)(2,1)S(1)} %collective-permute-done.15.refs_2_), channel_id=1, source_target_pairs={{0,1},{1,0},{2,3},{3,2},{4,5},{5,4},{6,7},{7,6},{8,9},{9,8},{10,11... | collective-permute-start | bytes 786440 | tf_op jit(solution)/shard_map/kv_grad_gather/ppermute | solution.py:26

commit v3 on v2

--- a/solution.py
+++ b/solution.py
@@ -265,13 +265,15 @@
             )
 
 
-def kernel_call(kernel, flags, arrays, outs, scratch, weight=0):
-    size = sum(a.size * a.dtype.itemsize for a in arrays) + sum(a.size * a.dtype.itemsize for a in outs)
-    held = sum(math.prod(s.shape) * jnp.dtype(s.dtype).itemsize for s in scratch)
+def kernel_call(kernel, flags, arrays, outs, scratch, weight=0, in_place=()):
+    size = sum(a.size * a.dtype.itemsize for n, a in enumerate(arrays) if n not in in_place)
+    size += sum(a.size * a.dtype.itemsize for a in outs)
+    held = sum(math.prod(s.shape) * jnp.dtype(s.dtype).itemsize for s in scratch if hasattr(s, "dtype") and len(s.shape) > 1)
     return pl.pallas_call(
         kernel,
         out_shape=outs,
-        in_specs=[pl.BlockSpec(memory_space=pltpu.SMEM)] + [pl.BlockSpec(memory_space=pltpu.VMEM)] * len(arrays),
+        in_specs=[pl.BlockSpec(memory_space=pltpu.SMEM)]
+        + [pl.BlockSpec(memory_space=pl.ANY if n in in_place else pltpu.VMEM) for n in range(len(arrays))],
         out_specs=[pl.BlockSpec(memory_space=pltpu.VMEM)] * len(outs),
         scratch_shapes=scratch,
         compiler_params=pltpu.CompilerParams(vmem_limit_bytes=held + size + (8 << 20)),
@@ -338,32 +340,43 @@
     )(starts, *arrays)
 
 
-def first_product_kernel(tp_count, group_count, query_width, group_ref, *refs):
-    acc_ref = refs[-1]
-    product_kernel(tp_count, group_count, slice(0, query_width), group_ref, refs[:-1], None, acc_ref)
-
-
-def last_product_kernel(tp_count, group_count, query_width, group_ref, acc_ref, *refs):
-    product_kernel(tp_count, group_count, slice(query_width, None), group_ref, refs[:-1], acc_ref, refs[-1])
-
-
-def product_kernel(tp_count, group_count, columns, group_ref, refs, acc_ref, out_ref):
-    pieces, refs = refs[:tp_count], refs[tp_count:]
-    whole, shares = refs[:2], refs[2:]
-    share = whole[0].shape[0] // group_count
-    group_place = group_ref[0]
-    for step in range(group_count):
-        source = lax.rem(group_place - step + group_count, group_count)
-        span = pl.ds(pl.multiple_of(source * share, share), share)
-        total = None if acc_ref is None else acc_ref[:, span]
-        for bits in range(tp_count):
-            if bits < 2:
-                w = whole[bits][span, columns]
+def product_kernel(tp_count, group_count, query_width, place_ref, *refs):
+    q_pieces, kv_pieces, refs = refs[:tp_count], refs[tp_count : 2 * tp_count], refs[2 * tp_count :]
+    out_ref, left, right, acc, sems = refs[-5:]
+    whole, shares = refs[:2], refs[2:-5]
+    rows_out = right.shape[1]
+    share = rows_out // group_count
+    copies = []
+    for bits in range(tp_count):
+        moves = [
+            (q_pieces[bits], left.at[bits, :, 0:query_width]),
+            (kv_pieces[bits], left.at[bits, :, query_width:]),
+        ]
+        if bits < 2:
+            moves.append((whole[bits], right.at[bits]))
+        else:
+            for step in range(group_count):
+                source = lax.rem(place_ref[0] - step + group_count, group_count)
+                span = pl.ds(pl.multiple_of(source * share, share), share)
+                moves.append((shares[(bits - 2) * group_count + step], right.at[bits, span, :]))
+        copies.append(
+            [pltpu.make_async_copy(a, b, sems.at[bits * (2 + group_count) + n]) for n, (a, b) in enumerate(moves)]
+        )
+    for group in copies:
+        for copy in group:
+            copy.start()
+    for bits in range(tp_count):
+        for copy in copies[bits]:
+            copy.wait()
+        for at in range(0, rows_out, rows_out // 4):
+            span = slice(at, at + rows_out // 4)
+            total = lax.dot_general(left[bits], right[bits, span, :], NT, preferred_element_type=jnp.float32)
+            if bits:
+                total = total + acc[:, span]
+            if bits < tp_count - 1:
+                acc[:, span] = total
             else:
-                w = shares[(bits - 2) * group_count + step][:, columns]
-            part = lax.dot_general(pieces[bits][...], w, NT, preferred_element_type=jnp.float32)
-            total = part if total is None else total + part
-        out_ref[:, span] = total.astype(out_ref.dtype)
+                out_ref[:, span] = total.astype(out_ref.dtype)
 
 
 def body(query, key_head_rows, value_head_rows, output_gradient, doc_blocks, w_query, key_weight, value_weight):
@@ -496,31 +509,36 @@
         key_value_grad = (own + passed.astype(f32)).astype(bf16)
 
     def gathered(block, before_last=None):
-        pieces = {0: block, 1: swapped(block, "tp", 1)}
+        pieces = [block, swapped(block, "tp", 1)]
         for bits in range(2, tp_count, 2):
-            pieces[bits] = swapped(block, "tp", bits)
-            held = pieces[bits]
+            pieces.append(swapped(block, "tp", bits))
+            held = pieces[-1]
             if before_last is not None:
                 held, _ = lax.optimization_barrier((held, before_last))
-            pieces[bits + 1] = swapped(held, "tp", 1)
-        return [pieces[bits] for bits in range(tp_count)]
+            pieces.append(swapped(held, "tp", 1))
+        return pieces
 
     with jax.named_scope("query_grad_gather"):
         q_pieces = gathered(query_grad)
-    group = jnp.full((1,), group_place, jnp.int32)
-    out = jax.ShapeDtypeStruct((rows, rows_out), bf16)
+    with jax.named_scope("kv_grad_gather"):
+        kv_pieces = gathered(key_value_grad, shares[-1])
     width = query.shape[1]
-    with jax.named_scope("query_product"):
-        (acc,) = kernel_call(
-            functools.partial(first_product_kernel, tp_count, group_count, width),
-            group, q_pieces + whole + shares, [jax.ShapeDtypeStruct((rows, rows_out), f32)], [], 1,
-        )
-    with jax.named_scope("kv_grad_gather"):
-        kv_pieces = gathered(key_value_grad, acc)
-    with jax.named_scope("kv_product"):
+    total_width = width + 2 * HEAD_WIDTH
+    arrays = q_pieces + kv_pieces + whole + shares
+    with jax.named_scope("product"):
         (result,) = kernel_call(
-            functools.partial(last_product_kernel, tp_count, group_count, width),
-            group, [acc] + kv_pieces + whole + shares, [out], [], 1,
+            functools.partial(product_kernel, tp_count, group_count, width),
+            jnp.full((1,), group_place, jnp.int32),
+            arrays,
+            [jax.ShapeDtypeStruct((rows, rows_out), bf16)],
+            [
+                pltpu.VMEM((tp_count, rows, total_width), bf16),
+                pltpu.VMEM((tp_count, rows_out, total_width), bf16),
+                pltpu.VMEM((rows, rows_out), f32),
+                pltpu.SemaphoreType.DMA((tp_count * (2 + group_count),)),
+            ],
+            1,
+            range(len(arrays)),
         )
     return result
 

time: 80.8 us -> 79.3 us (0.981)
  Pallas kernels: 33.1 us -> 29.9 us
  starting transfers between devices: 23 us -> 24.7 us
  waiting for transfers between devices: 20.9 us -> 22.4 us
  local copies, waits for them, and re-layouts: 0.92 us -> 0.03 us
    ppermute x6, waiting for transfers between devices: 8.84 us -> 14 us  [shifted(): return lax.ppermute(block, axis, route)]
    pallas_call x6 -> x5, Pallas kernels: 25.4 us -> 22.2 us  [kernel_call(): pl.pallas_call(kernel, out_shape=outs, in_specs=[pl.BlockSpec(memory_spac...]
    ppermute x2, waiting for transfers between devices: 9.25 us -> 6.86 us  [passed_on(): moved.append(lax.ppermute(held, 'groups', route))]
    ppermute x6, starting transfers between devices: 14.5 us -> 16.6 us  [shifted(): return lax.ppermute(block, axis, route)]
    ppermute x9, waiting for transfers between devices: 2.85 us -> 1.53 us  [swapped(): lax.ppermute(block, axis, [(i, i ^ bits) for i in range(lax.axis_size(axi...]
    unnamed x14 -> x12, local copies, waits for them, and re-layouts: 0.92 us -> 0.03 us
    ppermute x2, starting transfers between devices: 2.94 us -> 2.08 us  [passed_on(): moved.append(lax.ppermute(held, 'groups', route))]
  transfers between devices with their start and end apart: 17 -> 17, of which waited for: 6 -> 8; matrix products, arithmetic and copies ran while one was open for 1% -> 1% of each run, Pallas kernels for 34% -> 27%
where the time goes in v3:
time: 79.3 us; the launch traced here: 79 us
  Pallas kernels  29.9 us (38%)
  starting transfers between devices  24.7 us (31%)
  waiting for transfers between devices  22.4 us (28%)
  other arithmetic  1.59 us (2%)
    pallas_call x5, Pallas kernels, kernel_call(): pl.pallas_call(kernel, out_shape=outs, in_specs=[pl.BlockSpec(memory_spac...  22.2 us
    ppermute x6, starting transfers between devices, shifted(): return lax.ppermute(block, axis, route)  16.6 us
    ppermute x6, waiting for transfers between devices, shifted(): return lax.ppermute(block, axis, route)  14 us
    pallas_call x2, Pallas kernels, packed(): pl.pallas_call(functools.partial(pack_kernel, plan), out_shape=outs, in_s...  7.68 us
    ppermute x2, waiting for transfers between devices, passed_on(): moved.append(lax.ppermute(held, 'groups', route))  6.86 us
    ppermute x9, starting transfers between devices, swapped(): lax.ppermute(block, axis, [(i, i ^ bits) for i in range(lax.axis_size(axi...  6 us
    ppermute x2, starting transfers between devices, passed_on(): moved.append(lax.ppermute(held, 'groups', route))  2.08 us
  transfers between devices with their start and end apart: 17, of which 8 were waited for; matrix products, arithmetic and copies ran while one was open for 1% of the time, Pallas kernels for 27%

profile of v3, /device:TPU:0, one launch (start us, length us, event | category | flops | bytes accessed | tf_op | source)
XLA Modules:
  0.0 79.0 jit_solution(10813422884252549111)
XLA Ops:
  0.6 2.9 %pack_first.1 = (bf16[512,256]{1,0:T(8,128)(2,1)}, bf16[512,768]{1,0:T(8,128)(2,1)}) custom-call(s32[2]{0:T(128)} %pad_add_fusion.1.rows_ref, bf16[512,128]{1,0:T(8,128)(2,1)} %refs_0_.4, bf16[512,128]{1,0:T(8,128)(2,1)} %refs_1_.6, bf16[4096,512]{1,0:T(8,128)(2,1)} %refs_0_.3, bf16[4096,128]{1,0:T(8,128)(2,1)} %refs_1_.4, bf16[4096,128]{1,0:T(8,128)(2,1)} %refs_2_.3), custom_call_target="tpu_custom_call" | custom-call | bytes 2097152 | tf_op jit(solution)/shard_map/pack_first/pallas_call | solution.py:331
  3.5 7.0 %collective-permute-start.2 = (bf16[512,256]{1,0:T(8,128)(2,1)}, bf16[512,256]{1,0:T(8,128)(2,1)S(1)}, u32[]{:S(2)}, u32[]{:S(2)}) collective-permute-start(bf16[512,256]{1,0:T(8,128)(2,1)} %get-tuple-element.31), channel_id=1, source_target_pairs={{0,12},{1,13},{2,14},{3,15},{16,28},{17,29},{18,30},{19,31}} | collective-permute-start | bytes 786440 | tf_op jit(solution)/shard_map/kv_forward/ppermute | solution.py:22
  10.5 1.3 %collective-permute-start = (bf16[512,256]{1,0:T(8,128)(2,1)}, bf16[512,256]{1,0:T(8,128)(2,1)S(1)}, u32[]{:S(2)}, u32[]{:S(2)}) collective-permute-start(bf16[512,256]{1,0:T(8,128)(2,1)} %get-tuple-element.31), channel_id=1, source_target_pairs={{0,4},{4,8},{8,12},{1,5},{5,9},{9,13},{2,6},{6,10},{10,14},{3,7},{... | collective-permute-start | bytes 786440 | tf_op jit(solution)/shard_map/kv_forward/ppermute | solution.py:22
  11.8 1.6 %collective-permute-start.9 = (bf16[512,768]{1,0:T(8,128)(2,1)}, bf16[512,768]{1,0:T(8,128)(2,1)}, u32[]{:S(2)}, u32[]{:S(2)}) collective-permute-start(bf16[512,768]{1,0:T(8,128)(2,1)} %get-tuple-element.48), channel_id=1, source_target_pairs={{0,2},{1,3},{2,0},{3,1},{4,6},{5,7},{6,4},{7,5},{8,10},{9,11},{10,... | collective-permute-start | bytes 2359304 | tf_op jit(solution)/shard_map/weight_exchange/ppermute | solution.py:26
  13.3 0.7 pad_add_fusion.rows_ref
  14.0 4.8 %pack_rest.1 = (bf16[1024,768]{1,0:T(8,128)(2,1)}, bf16[1024,768]{1,0:T(8,128)(2,1)}, bf16[512,768]{1,0:T(8,128)(2,1)}) custom-call(s32[3]{0:T(128)} %pad_add_fusion.rows_ref, bf16[4096,512]{1,0:T(8,128)(2,1)} %refs_0_.3, bf16[4096,128]{1,0:T(8,128)(2,1)} %refs_1_.4, bf16[4096,128]{1,0:T(8,128)(2,1)} %refs_2_.3), custom_call_target="tpu_custom_call" | custom-call | bytes 7864320 | tf_op jit(solution)/shard_map/pack_rest/pallas_call | solution.py:331
  19.6 2.4 %collective-permute-done.kv1.refs_2_ = bf16[512,256]{1,0:T(8,128)(2,1)S(1)} collective-permute-done((bf16[512,256]{1,0:T(8,128)(2,1)}, bf16[512,256]{1,0:T(8,128)(2,1)S(1)}, u32[]{:S(2)}, u32[]{:S(2)}) %collective-permute-start) | collective-permute-done | bytes 262176 | tf_op jit(solution)/shard_map/kv_forward/ppermute | solution.py:22
  22.0 4.3 %collective-permute-start.1 = (bf16[512,256]{1,0:T(8,128)(2,1)S(1)}, bf16[512,256]{1,0:T(8,128)(2,1)S(1)}, u32[]{:S(2)}, u32[]{:S(2)}) collective-permute-start(bf16[512,256]{1,0:T(8,128)(2,1)S(1)} %collective-permute-done.kv1.refs_2_), channel_id=1, source_target_pairs={{0,4},{4,8},{8,12},{1,5},{5,9},{9,13},{2,6},{6,10},{10,14},{3,7},{... | collective-permute-start | bytes 786440 | tf_op jit(solution)/shard_map/kv_forward/ppermute | solution.py:22
  26.4 3.5 %near_stats.1 = (f32[4,512]{1,0:T(4,128)S(1)}, f32[4,512]{1,0:T(4,128)S(1)}, f32[4,512]{1,0:T(4,128)S(1)}) custom-call(s32[4,16]{1,0:T(4,128)S(1)} %fusion.4.flag_ref.refs_0_, bf16[512,512]{1,0:T(8,128)(2,1)S(1)} %copy-done, bf16[512,512]{1,0:T(8,128)(2,1)S(1)} %copy-done.1, bf16[512,128]{1,0:T(8,128)(2,1)S(1)} %copy-done.3, bf16[512,128]{1,0:T(8,128)(2,1)S(1)} %copy-done.4, ...), custom_call_target="tpu_custom_call" | custom-call | tf_op jit(solution)/shard_map/near_stats/pallas_call | solution.py:272
  29.9 1.1 %collective-permute-done.1.refs_6_ = bf16[512,256]{1,0:T(8,128)(2,1)S(1)} collective-permute-done((bf16[512,256]{1,0:T(8,128)(2,1)S(1)}, bf16[512,256]{1,0:T(8,128)(2,1)S(1)}, u32[]{:S(2)}, u32[]{:S(2)}) %collective-permute-start.1) | collective-permute-done | bytes 262176 | tf_op jit(solution)/shard_map/kv_forward/ppermute | solution.py:22
  31.1 5.7 %far_stats.1 = (f32[3,4,512]{2,1,0:T(4,128)S(1)}, f32[4,128,512]{2,1,0:T(8,128)S(1)}, bf16[512,256]{1,0:T(8,128)(2,1)S(1)}) custom-call(s32[4,16]{1,0:T(4,128)S(1)} %fusion.4.flag_ref.refs_0_, bf16[512,512]{1,0:T(8,128)(2,1)S(1)} %copy-done, bf16[512,512]{1,0:T(8,128)(2,1)S(1)} %copy-done.1, f32[4,512]{1,0:T(4,128)S(1)} %get-tuple-element.37.refs_3_, ...), custom_call_target="tpu_custom_call" | custom-call | tf_op jit(solution)/shard_map/far_stats/pallas_call | solution.py:272
  36.8 1.6 %collective-permute-start.10 = (bf16[512,768]{1,0:T(8,128)(2,1)}, bf16[512,768]{1,0:T(8,128)(2,1)S(1)}, u32[]{:S(2)}, u32[]{:S(2)}) collective-permute-start(bf16[512,768]{1,0:T(8,128)(2,1)} %collective-permute-done.9.refs_10_), channel_id=1, source_target_pairs={{0,16},{16,0},{1,17},{17,1},{2,18},{18,2},{3,19},{19,3},{4,20},{20... | collective-permute-start | bytes 2359304 | tf_op jit(solution)/shard_map/weight_exchange/ppermute | solution.py:474
  38.4 1.3 %collective-permute-start.7 = (bf16[512,256]{1,0:T(8,128)(2,1)S(1)}, bf16[512,256]{1,0:T(8,128)(2,1)S(1)}, u32[]{:S(2)}, u32[]{:S(2)}) collective-permute-start(bf16[512,256]{1,0:T(8,128)(2,1)S(1)} %get-tuple-element.47), channel_id=1, source_target_pairs={{4,0},{8,4},{12,8},{5,1},{9,5},{13,9},{6,2},{10,6},{14,10},{7,3},{... | collective-permute-start | bytes 786440 | tf_op jit(solution)/shard_map/kv_return/ppermute | solution.py:22
  39.7 2.5 %longest_gradients.1 = (bf16[512,256]{1,0:T(8,128)(2,1)S(1)}, f32[4,128,512]{2,1,0:T(8,128)S(1)}) custom-call(s32[4,16]{1,0:T(4,128)S(1)} %fusion.4.flag_ref.refs_0_, bf16[512,512]{1,0:T(8,128)(2,1)S(1)} %copy-done, bf16[512,512]{1,0:T(8,128)(2,1)S(1)} %copy-done.1, f32[3,4,512]{2,1,0:T(4,128)S(1)} %get-tuple-element.40.stat_ref, ...), custom_call_target="tpu_custom_call" | custom-call | tf_op jit(solution)/shard_map/longest_gradients/pallas_call | solution.py:272
  42.1 1.5 %collective-permute-start.6 = (bf16[512,256]{1,0:T(8,128)(2,1)S(1)}, bf16[512,256]{1,0:T(8,128)(2,1)S(1)}, u32[]{:S(2)}, u32[]{:S(2)}) collective-permute-start(bf16[512,256]{1,0:T(8,128)(2,1)S(1)} %get-tuple-element.45), channel_id=1, source_target_pairs={{12,0},{13,1},{14,2},{15,3},{28,16},{29,17},{30,18},{31,19}} | collective-permute-start | bytes 786440 | tf_op jit(solution)/shard_map/kv_return/ppermute | solution.py:22
  43.6 5.2 %near_gradients.1 = (f32[512,256]{1,0:T(8,128)S(1)}, f32[512,256]{1,0:T(8,128)S(1)}, bf16[512,512]{1,0:T(8,128)(2,1)S(1)}) custom-call(s32[4,16]{1,0:T(4,128)S(1)} %fusion.4.flag_ref.refs_0_, bf16[512,512]{1,0:T(8,128)(2,1)S(1)} %copy-done, bf16[512,512]{1,0:T(8,128)(2,1)S(1)} %copy-done.1, f32[3,4,512]{2,1,0:T(4,128)S(1)} %get-tuple-element.40.stat_ref, ...), custom_call_target="tpu_custom_call" | custom-call | tf_op jit(solution)/shard_map/near_gradients/pallas_call | solution.py:272
  48.9 1.6 %collective-permute-start.4 = (bf16[512,512]{1,0:T(8,128)(2,1)S(1)}, bf16[512,512]{1,0:T(8,128)(2,1)S(1)}, u32[]{:S(2)}, u32[]{:S(2)}) collective-permute-start(bf16[512,512]{1,0:T(8,128)(2,1)S(1)} %get-tuple-element.43.refs_0_), channel_id=1, source_target_pairs={{0,2},{1,3},{2,0},{3,1},{4,6},{5,7},{6,4},{7,5},{8,10},{9,11},{10,... | collective-permute-start | bytes 1572872 | tf_op jit(solution)/shard_map/query_grad_gather/ppermute | solution.py:26
  51.0 3.4 %collective-permute-done.6 = bf16[512,256]{1,0:T(8,128)(2,1)S(1)} collective-permute-done((bf16[512,256]{1,0:T(8,128)(2,1)S(1)}, bf16[512,256]{1,0:T(8,128)(2,1)S(1)}, u32[]{:S(2)}, u32[]{:S(2)}) %collective-permute-start.6) | collective-permute-done | bytes 262176 | tf_op jit(solution)/shard_map/kv_return/ppermute | solution.py:22
  54.4 1.3 %collective-permute-start.8 = (bf16[512,256]{1,0:T(8,128)(2,1)S(1)}, bf16[512,256]{1,0:T(8,128)(2,1)S(1)}, u32[]{:S(2)}, u32[]{:S(2)}) collective-permute-start(bf16[512,256]{1,0:T(8,128)(2,1)S(1)} %add_convert_fusion.1), channel_id=1, source_target_pairs={{4,0},{8,4},{12,8},{5,1},{9,5},{13,9},{6,2},{10,6},{14,10},{7,3},{... | collective-permute-start | bytes 786440 | tf_op jit(solution)/shard_map/kv_return/ppermute | solution.py:22
  55.6 7.2 %collective-permute-done.8 = bf16[512,256]{1,0:T(8,128)(2,1)S(1)} collective-permute-done((bf16[512,256]{1,0:T(8,128)(2,1)S(1)}, bf16[512,256]{1,0:T(8,128)(2,1)S(1)}, u32[]{:S(2)}, u32[]{:S(2)}) %collective-permute-start.8) | collective-permute-done | bytes 262176 | tf_op jit(solution)/shard_map/kv_return/ppermute | solution.py:22
  62.9 1.6 %collective-permute-start.12 = (bf16[512,256]{1,0:T(8,128)(2,1)S(1)}, bf16[512,256]{1,0:T(8,128)(2,1)S(1)}, u32[]{:S(2)}, u32[]{:S(2)}) collective-permute-start(bf16[512,256]{1,0:T(8,128)(2,1)S(1)} %add_convert_fusion.refs_4_), channel_id=1, source_target_pairs={{0,2},{1,3},{2,0},{3,1},{4,6},{5,7},{6,4},{7,5},{8,10},{9,11},{10,... | collective-permute-start | bytes 786440 | tf_op jit(solution)/shard_map/kv_grad_gather/ppermute | solution.py:26
  64.7 6.9 %collective-permute-done.14.refs_13_ = bf16[512,768]{1,0:T(8,128)(2,1)S(1)} collective-permute-done((bf16[512,768]{1,0:T(8,128)(2,1)}, bf16[512,768]{1,0:T(8,128)(2,1)S(1)}, u32[]{:S(2)}, u32[]{:S(2)}) %collective-permute-start.14) | collective-permute-done | bytes 786464 | tf_op jit(solution)/shard_map/weight_exchange/ppermute | solution.py:474
  72.1 1.0 %collective-permute-done.11.refs_5_ = bf16[512,256]{1,0:T(8,128)(2,1)S(1)} collective-permute-done((bf16[512,256]{1,0:T(8,128)(2,1)S(1)}, bf16[512,256]{1,0:T(8,128)(2,1)S(1)}, u32[]{:S(2)}, u32[]{:S(2)}) %collective-permute-start.11) | collective-permute-done | bytes 262176 | tf_op jit(solution)/shard_map/kv_grad_gather/ppermute | solution.py:26
  73.5 5.4 %product.1 = bf16[512,1024]{1,0:T(8,128)(2,1)} custom-call(s32[1]{0:T(128)} %bitcast.place_ref, bf16[512,512]{1,0:T(8,128)(2,1)S(1)} %get-tuple-element.43.refs_0_, bf16[512,512]{1,0:T(8,128)(2,1)S(1)} %collective-permute-done.3.refs_1_, bf16[512,512]{1,0:T(8,128)(2,1)S(1)} %collective-permute-done.4.refs_2_, ...), custom_call_target="tpu_custom_call" | custom-call | bytes 1048576 | tf_op jit(solution)/shard_map/product/pallas_call | solution.py:272
  (38 shorter events, 3.3 us)
Async XLA Ops:
  3.5 26.4 %collective-permute-start.2 = (bf16[512,256]{1,0:T(8,128)(2,1)}, bf16[512,256]{1,0:T(8,128)(2,1)S(1)}, u32[]{:S(2)}, u32[]{:S(2)}) collective-permute-start(bf16[512,256]{1,0:T(8,128)(2,1)} %get-tuple-element.31), channel_id=1, source_target_pairs={{0,12},{1,13},{2,14},{3,15},{16,28},{17,29},{18,30},{19,31}} | collective-permute-start | bytes 786440 | tf_op jit(solution)/shard_map/kv_forward/ppermute | solution.py:22
  10.5 11.5 %collective-permute-start = (bf16[512,256]{1,0:T(8,128)(2,1)}, bf16[512,256]{1,0:T(8,128)(2,1)S(1)}, u32[]{:S(2)}, u32[]{:S(2)}) collective-permute-start(bf16[512,256]{1,0:T(8,128)(2,1)} %get-tuple-element.31), channel_id=1, source_target_pairs={{0,4},{4,8},{8,12},{1,5},{5,9},{9,13},{2,6},{6,10},{10,14},{3,7},{... | collective-permute-start | bytes 786440 | tf_op jit(solution)/shard_map/kv_forward/ppermute | solution.py:22
  11.8 25.0 %collective-permute-start.9 = (bf16[512,768]{1,0:T(8,128)(2,1)}, bf16[512,768]{1,0:T(8,128)(2,1)}, u32[]{:S(2)}, u32[]{:S(2)}) collective-permute-start(bf16[512,768]{1,0:T(8,128)(2,1)} %get-tuple-element.48), channel_id=1, source_target_pairs={{0,2},{1,3},{2,0},{3,1},{4,6},{5,7},{6,4},{7,5},{8,10},{9,11},{10,... | collective-permute-start | bytes 2359304 | tf_op jit(solution)/shard_map/weight_exchange/ppermute | solution.py:26
  14.0 5.5 %copy-start.5 = (s32[4,8]{1,0:T(4,128)S(1)}, s32[4,8]{1,0:T(4,128)}, u32[]{:S(2)}) copy-start(s32[4,8]{1,0:T(4,128)} %param.12) | copy-start | bytes 388
  14.0 12.4 %copy-start = (bf16[512,512]{1,0:T(8,128)(2,1)S(1)}, bf16[512,512]{1,0:T(8,128)(2,1)}, u32[]{:S(2)}) copy-start(bf16[512,512]{1,0:T(8,128)(2,1)} %query_ref.4) | copy-start | bytes 1572868
  14.0 12.4 %copy-start.1 = (bf16[512,512]{1,0:T(8,128)(2,1)S(1)}, bf16[512,512]{1,0:T(8,128)(2,1)}, u32[]{:S(2)}) copy-start(bf16[512,512]{1,0:T(8,128)(2,1)} %grad_ref.5) | copy-start | bytes 1572868
  14.0 12.4 %copy-start.3 = (bf16[512,128]{1,0:T(8,128)(2,1)S(1)}, bf16[512,128]{1,0:T(8,128)(2,1)}, u32[]{:S(2)}) copy-start(bf16[512,128]{1,0:T(8,128)(2,1)} %refs_0_.4) | copy-start | bytes 393220
  14.0 12.4 %copy-start.4 = (bf16[512,128]{1,0:T(8,128)(2,1)S(1)}, bf16[512,128]{1,0:T(8,128)(2,1)}, u32[]{:S(2)}) copy-start(bf16[512,128]{1,0:T(8,128)(2,1)} %refs_1_.6) | copy-start | bytes 393220
  18.8 30.0 %collective-permute-start.13 = (bf16[512,768]{1,0:T(8,128)(2,1)}, bf16[512,768]{1,0:T(8,128)(2,1)}, u32[]{:S(2)}, u32[]{:S(2)}) collective-permute-start(bf16[512,768]{1,0:T(8,128)(2,1)} %get-tuple-element.52), channel_id=1, source_target_pairs={{0,3},{1,2},{2,1},{3,0},{4,7},{5,6},{6,5},{7,4},{8,11},{9,10},{10,... | collective-permute-start | bytes 2359304 | tf_op jit(solution)/shard_map/weight_exchange/ppermute | solution.py:26
  18.9 53.2 %collective-permute-start.16 = (bf16[1024,768]{1,0:T(8,128)(2,1)}, bf16[1024,768]{1,0:T(8,128)(2,1)S(1)}, u32[]{:S(2)}, u32[]{:S(2)}) collective-permute-start(bf16[1024,768]{1,0:T(8,128)(2,1)} %get-tuple-element.35), channel_id=1, source_target_pairs={{0,1},{1,0},{2,3},{3,2},{4,5},{5,4},{6,7},{7,6},{8,9},{9,8},{10,11... | collective-permute-start | bytes 4718600 | tf_op jit(solution)/shard_map/weight_exchange/ppermute | solution.py:26
  22.0 9.1 %collective-permute-start.1 = (bf16[512,256]{1,0:T(8,128)(2,1)S(1)}, bf16[512,256]{1,0:T(8,128)(2,1)S(1)}, u32[]{:S(2)}, u32[]{:S(2)}) collective-permute-start(bf16[512,256]{1,0:T(8,128)(2,1)S(1)} %collective-permute-done.kv1.refs_2_), channel_id=1, source_target_pairs={{0,4},{4,8},{8,12},{1,5},{5,9},{9,13},{2,6},{6,10},{10,14},{3,7},{... | collective-permute-start | bytes 786440 | tf_op jit(solution)/shard_map/kv_forward/ppermute | solution.py:22
  36.8 26.0 %collective-permute-start.10 = (bf16[512,768]{1,0:T(8,128)(2,1)}, bf16[512,768]{1,0:T(8,128)(2,1)S(1)}, u32[]{:S(2)}, u32[]{:S(2)}) collective-permute-start(bf16[512,768]{1,0:T(8,128)(2,1)} %collective-permute-done.9.refs_10_), channel_id=1, source_target_pairs={{0,16},{16,0},{1,17},{17,1},{2,18},{18,2},{3,19},{19,3},{4,20},{20... | collective-permute-start | bytes 2359304 | tf_op jit(solution)/shard_map/weight_exchange/ppermute | solution.py:474
  38.4 12.1 %collective-permute-start.7 = (bf16[512,256]{1,0:T(8,128)(2,1)S(1)}, bf16[512,256]{1,0:T(8,128)(2,1)S(1)}, u32[]{:S(2)}, u32[]{:S(2)}) collective-permute-start(bf16[512,256]{1,0:T(8,128)(2,1)S(1)} %get-tuple-element.47), channel_id=1, source_target_pairs={{4,0},{8,4},{12,8},{5,1},{9,5},{13,9},{6,2},{10,6},{14,10},{7,3},{... | collective-permute-start | bytes 786440 | tf_op jit(solution)/shard_map/kv_return/ppermute | solution.py:22
  42.1 12.2 %collective-permute-start.6 = (bf16[512,256]{1,0:T(8,128)(2,1)S(1)}, bf16[512,256]{1,0:T(8,128)(2,1)S(1)}, u32[]{:S(2)}, u32[]{:S(2)}) collective-permute-start(bf16[512,256]{1,0:T(8,128)(2,1)S(1)} %get-tuple-element.45), channel_id=1, source_target_pairs={{12,0},{13,1},{14,2},{15,3},{28,16},{29,17},{30,18},{31,19}} | collective-permute-start | bytes 786440 | tf_op jit(solution)/shard_map/kv_return/ppermute | solution.py:22
  48.8 24.6 %copy-start.2 = (bf16[1024,768]{1,0:T(8,128)(2,1)S(1)}, bf16[1024,768]{1,0:T(8,128)(2,1)}, u32[]{:S(2)}) copy-start(bf16[1024,768]{1,0:T(8,128)(2,1)} %get-tuple-element.55.refs_8_) | copy-start | bytes 4718596
  48.9 15.6 %collective-permute-start.4 = (bf16[512,512]{1,0:T(8,128)(2,1)S(1)}, bf16[512,512]{1,0:T(8,128)(2,1)S(1)}, u32[]{:S(2)}, u32[]{:S(2)}) collective-permute-start(bf16[512,512]{1,0:T(8,128)(2,1)S(1)} %get-tuple-element.43.refs_0_), channel_id=1, source_target_pairs={{0,2},{1,3},{2,0},{3,1},{4,6},{5,7},{6,4},{7,5},{8,10},{9,11},{10,... | collective-permute-start | bytes 1572872 | tf_op jit(solution)/shard_map/query_grad_gather/ppermute | solution.py:26
  50.4 21.1 %collective-permute-start.14 = (bf16[512,768]{1,0:T(8,128)(2,1)}, bf16[512,768]{1,0:T(8,128)(2,1)S(1)}, u32[]{:S(2)}, u32[]{:S(2)}) collective-permute-start(bf16[512,768]{1,0:T(8,128)(2,1)} %collective-permute-done.13.refs_12_), channel_id=1, source_target_pairs={{0,16},{16,0},{1,17},{17,1},{2,18},{18,2},{3,19},{19,3},{4,20},{20... | collective-permute-start | bytes 2359304 | tf_op jit(solution)/shard_map/weight_exchange/ppermute | solution.py:474
  54.4 8.4 %collective-permute-start.8 = (bf16[512,256]{1,0:T(8,128)(2,1)S(1)}, bf16[512,256]{1,0:T(8,128)(2,1)S(1)}, u32[]{:S(2)}, u32[]{:S(2)}) collective-permute-start(bf16[512,256]{1,0:T(8,128)(2,1)S(1)} %add_convert_fusion.1), channel_id=1, source_target_pairs={{4,0},{8,4},{12,8},{5,1},{9,5},{13,9},{6,2},{10,6},{14,10},{7,3},{... | collective-permute-start | bytes 786440 | tf_op jit(solution)/shard_map/kv_return/ppermute | solution.py:22
  62.8 9.3 %collective-permute-start.3 = (bf16[512,512]{1,0:T(8,128)(2,1)S(1)}, bf16[512,512]{1,0:T(8,128)(2,1)S(1)}, u32[]{:S(2)}, u32[]{:S(2)}) collective-permute-start(bf16[512,512]{1,0:T(8,128)(2,1)S(1)} %get-tuple-element.43.refs_0_), channel_id=1, source_target_pairs={{0,1},{1,0},{2,3},{3,2},{4,5},{5,4},{6,7},{7,6},{8,9},{9,8},{10,11... | collective-permute-start | bytes 1572872 | tf_op jit(solution)/shard_map/query_grad_gather/ppermute | solution.py:26
  62.9 8.8 %collective-permute-start.12 = (bf16[512,256]{1,0:T(8,128)(2,1)S(1)}, bf16[512,256]{1,0:T(8,128)(2,1)S(1)}, u32[]{:S(2)}, u32[]{:S(2)}) collective-permute-start(bf16[512,256]{1,0:T(8,128)(2,1)S(1)} %add_convert_fusion.refs_4_), channel_id=1, source_target_pairs={{0,2},{1,3},{2,0},{3,1},{4,6},{5,7},{6,4},{7,5},{8,10},{9,11},{10,... | collective-permute-start | bytes 786440 | tf_op jit(solution)/shard_map/kv_grad_gather/ppermute | solution.py:26
  64.5 7.6 %collective-permute-start.5 = (bf16[512,512]{1,0:T(8,128)(2,1)S(1)}, bf16[512,512]{1,0:T(8,128)(2,1)S(1)}, u32[]{:S(2)}, u32[]{:S(2)}) collective-permute-start(bf16[512,512]{1,0:T(8,128)(2,1)S(1)} %collective-permute-done.4.refs_2_), channel_id=1, source_target_pairs={{0,1},{1,0},{2,3},{3,2},{4,5},{5,4},{6,7},{7,6},{8,9},{9,8},{10,11... | collective-permute-start | bytes 1572872 | tf_op jit(solution)/shard_map/query_grad_gather/ppermute | solution.py:26
  71.5 1.5 %collective-permute-start.11 = (bf16[512,256]{1,0:T(8,128)(2,1)S(1)}, bf16[512,256]{1,0:T(8,128)(2,1)S(1)}, u32[]{:S(2)}, u32[]{:S(2)}) collective-permute-start(bf16[512,256]{1,0:T(8,128)(2,1)S(1)} %add_convert_fusion.refs_4_), channel_id=1, source_target_pairs={{0,1},{1,0},{2,3},{3,2},{4,5},{5,4},{6,7},{7,6},{8,9},{9,8},{10,11... | collective-permute-start | bytes 786440 | tf_op jit(solution)/shard_map/kv_grad_gather/ppermute | solution.py:26
  71.7 1.8 %collective-permute-start.15 = (bf16[512,256]{1,0:T(8,128)(2,1)S(1)}, bf16[512,256]{1,0:T(8,128)(2,1)S(1)}, u32[]{:S(2)}, u32[]{:S(2)}) collective-permute-start(bf16[512,256]{1,0:T(8,128)(2,1)S(1)} %collective-permute-done.12.refs_6_), channel_id=1, source_target_pairs={{0,1},{1,0},{2,3},{3,2},{4,5},{5,4},{6,7},{7,6},{8,9},{9,8},{10,11... | collective-permute-start | bytes 786440 | tf_op jit(solution)/shard_map/kv_grad_gather/ppermute | solution.py:26

commit v4 on v3

--- a/solution.py
+++ b/solution.py
@@ -127,11 +127,12 @@
 
 def key_value_sums(c, d, blocks, reach, lanes, p_ref, ds_ref, query_stack, grad_stack, out_ref):
     rows = blocks * BLOCK
-    for j in range(blocks):
-        low, high = lane_range(d, j, blocks, reach)
-        at = slice(c * rows + j * BLOCK, c * rows + (j + 1) * BLOCK)
+    ranges = [lane_range(d, j, blocks, reach) for j in range(blocks)]
+    whole = all(r == (0, blocks) for r in ranges)
+    for j, (low, high) in enumerate(ranges[:1] if whole else ranges):
+        out = slice(j * BLOCK, rows if whole else (j + 1) * BLOCK)
+        at = slice(c * rows + out.start, c * rows + out.stop)
         span = slice(low * lanes, high * lanes)
-        out = slice(j * BLOCK, (j + 1) * BLOCK)
         key_sum = jnp.dot(ds_ref[at, span], query_stack[span, :], preferred_element_type=jnp.float32)
         out_ref[out, 0:HEAD_WIDTH] = (key_sum * SCALE).astype(out_ref.dtype)
         value_sum = jnp.dot(p_ref[at, span], grad_stack[span, :], preferred_element_type=jnp.float32)
@@ -340,40 +341,43 @@
     )(starts, *arrays)
 
 
-def product_kernel(tp_count, group_count, query_width, place_ref, *refs):
-    q_pieces, kv_pieces, refs = refs[:tp_count], refs[tp_count : 2 * tp_count], refs[2 * tp_count :]
+def product_kernel(peers, group_count, query_width, last, place_ref, *refs):
+    before, refs = (refs[0], refs[1:]) if last else (None, refs)
     out_ref, left, right, acc, sems = refs[-5:]
-    whole, shares = refs[:2], refs[2:-5]
     rows_out = right.shape[1]
-    share = rows_out // group_count
     copies = []
-    for bits in range(tp_count):
-        moves = [
-            (q_pieces[bits], left.at[bits, :, 0:query_width]),
-            (kv_pieces[bits], left.at[bits, :, query_width:]),
-        ]
-        if bits < 2:
-            moves.append((whole[bits], right.at[bits]))
-        else:
-            for step in range(group_count):
-                source = lax.rem(place_ref[0] - step + group_count, group_count)
-                span = pl.ds(pl.multiple_of(source * share, share), share)
-                moves.append((shares[(bits - 2) * group_count + step], right.at[bits, span, :]))
-        copies.append(
-            [pltpu.make_async_copy(a, b, sems.at[bits * (2 + group_count) + n]) for n, (a, b) in enumerate(moves)]
-        )
+    at = 0
+    for n, (parts, low, high) in enumerate(peers):
+        moves = []
+        for piece, first in parts:
+            width = refs[piece].shape[1]
+            moves.append((refs[piece], left.at[n, :, first : first + width]))
+        columns = slice(parts[0][1], parts[-1][1] + refs[parts[-1][0]].shape[1])
+        weights = refs[low:high]
+        share = rows_out // len(weights)
+        for step, array in enumerate(weights):
+            source = lax.rem(place_ref[0] - step + group_count, group_count) if len(weights) > 1 else 0
+            span = pl.ds(pl.multiple_of(source * share, share), share)
+            moves.append((array.at[:, columns], right.at[n, span, columns]))
+        copies.append([pltpu.make_async_copy(a, b, sems.at[at + m]) for m, (a, b) in enumerate(moves)])
+        at += len(moves)
+    if last:
+        copies[0].append(pltpu.make_async_copy(before, acc, sems.at[at]))
     for group in copies:
         for copy in group:
             copy.start()
-    for bits in range(tp_count):
-        for copy in copies[bits]:
+    for n, (parts, _, _) in enumerate(peers):
+        for copy in copies[n]:
             copy.wait()
+        columns = slice(parts[0][1], parts[-1][1] + refs[parts[-1][0]].shape[1])
         for at in range(0, rows_out, rows_out // 4):
             span = slice(at, at + rows_out // 4)
-            total = lax.dot_general(left[bits], right[bits, span, :], NT, preferred_element_type=jnp.float32)
-            if bits:
+            total = lax.dot_general(
+                left[n, :, columns], right[n, span, columns], NT, preferred_element_type=jnp.float32
+            )
+            if n or last:
                 total = total + acc[:, span]
-            if bits < tp_count - 1:
+            if n < len(peers) - 1:
                 acc[:, span] = total
             else:
                 out_ref[:, span] = total.astype(out_ref.dtype)
@@ -520,27 +524,49 @@
 
     with jax.named_scope("query_grad_gather"):
         q_pieces = gathered(query_grad)
-    with jax.named_scope("kv_grad_gather"):
-        kv_pieces = gathered(key_value_grad, shares[-1])
     width = query.shape[1]
     total_width = width + 2 * HEAD_WIDTH
-    arrays = q_pieces + kv_pieces + whole + shares
-    with jax.named_scope("product"):
-        (result,) = kernel_call(
-            functools.partial(product_kernel, tp_count, group_count, width),
-            jnp.full((1,), group_place, jnp.int32),
-            arrays,
-            [jax.ShapeDtypeStruct((rows, rows_out), bf16)],
-            [
-                pltpu.VMEM((tp_count, rows, total_width), bf16),
-                pltpu.VMEM((tp_count, rows_out, total_width), bf16),
-                pltpu.VMEM((rows, rows_out), f32),
-                pltpu.SemaphoreType.DMA((tp_count * (2 + group_count),)),
-            ],
-            1,
-            range(len(arrays)),
-        )
-    return result
+    place_ids = jnp.full((1,), group_place, jnp.int32)
+
+    def product(scope, before, entries, out_type):
+        arrays = [] if before is None else [before]
+        peers = []
+        for parts, weights in entries:
+            placed = []
+            for piece, first in parts:
+                placed.append((len(arrays) - (before is not None), first))
+                arrays.append(piece)
+            low = len(arrays) - (before is not None)
+            arrays += weights
+            peers.append((tuple(placed), low, low + len(weights)))
+        count = sum(len(parts) + len(weights) for parts, weights in entries) + 1
+        with jax.named_scope(scope):
+            (result,) = kernel_call(
+                functools.partial(product_kernel, peers, group_count, width, before is not None),
+                place_ids,
+                arrays,
+                [jax.ShapeDtypeStruct((rows, rows_out), out_type)],
+                [
+                    pltpu.VMEM((len(entries), rows, total_width), bf16),
+                    pltpu.VMEM((len(entries), rows_out, total_width), bf16),
+                    pltpu.VMEM((rows, rows_out), f32),
+                    pltpu.SemaphoreType.DMA((count,)),
+                ],
+                0,
+                range(len(arrays)),
+            )
+        return result
+
+    sets = [[whole[0]], [whole[1]]]
+    sets += [shares[at : at + group_count] for at in range(0, len(shares), group_count)]
+    acc = product(
+        "query_product", None, [([(q_pieces[bits], 0)], sets[bits]) for bits in range(tp_count - 1)], f32
+    )
+    with jax.named_scope("kv_grad_gather"):
+        kv_pieces = gathered(key_value_grad, [acc] + shares[-1:])
+    entries = [([(kv_pieces[bits], width)], sets[bits]) for bits in range(tp_count - 1)]
+    entries.append(([(q_pieces[-1], 0), (kv_pieces[-1], width)], sets[-1]))
+    return product("last_product", acc, entries, bf16)
 
 
 def solution(mesh):

time: 79.3 us -> 76.4 us (0.963)
  waiting for transfers between devices: 22.4 us -> 18.1 us
  Pallas kernels: 29.9 us -> 32.2 us
  starting transfers between devices: 24.7 us -> 22.8 us
  local copies, waits for them, and re-layouts: 0.03 us -> 0.92 us
    ppermute x9, waiting for transfers between devices: 1.53 us -> 9.02 us  [swapped(): lax.ppermute(block, axis, [(i, i ^ bits) for i in range(lax.axis_size(axi...]
    ppermute x2, waiting for transfers between devices: 6.86 us -> 0.01 us  [passed_on(): moved.append(lax.ppermute(held, 'groups', route))]
    ppermute x6, waiting for transfers between devices: 14 us -> 9.12 us  [shifted(): return lax.ppermute(block, axis, route)]
    pallas_call x5 -> x6, Pallas kernels: 22.2 us -> 24.5 us  [kernel_call(): pl.pallas_call(kernel, out_shape=outs, in_specs=[pl.BlockSpec(memory_spac...]
    ppermute x6, starting transfers between devices: 16.6 us -> 14.5 us  [shifted(): return lax.ppermute(block, axis, route)]
    unnamed x12 -> x14, local copies, waits for them, and re-layouts: 0.03 us -> 0.92 us
  transfers between devices with their start and end apart: 17 -> 17, of which waited for: 8 -> 5; matrix products, arithmetic and copies ran while one was open for 1% -> 1% of each run, Pallas kernels for 27% -> 34%
where the time goes in v4:
time: 76.4 us; the launch traced here: 76 us
  Pallas kernels  32.2 us (42%)
  starting transfers between devices  22.8 us (30%)
  waiting for transfers between devices  18.1 us (24%)
  other arithmetic  1.58 us (2%)
  local copies, waits for them, and re-layouts  0.92 us (1%)
    pallas_call x6, Pallas kernels, kernel_call(): pl.pallas_call(kernel, out_shape=outs, in_specs=[pl.BlockSpec(memory_spac...  24.5 us
    ppermute x6, starting transfers between devices, shifted(): return lax.ppermute(block, axis, route)  14.5 us
    ppermute x6, waiting for transfers between devices, shifted(): return lax.ppermute(block, axis, route)  9.12 us
    ppermute x9, waiting for transfers between devices, swapped(): lax.ppermute(block, axis, [(i, i ^ bits) for i in range(lax.axis_size(axi...  9.02 us
    pallas_call x2, Pallas kernels, packed(): pl.pallas_call(functools.partial(pack_kernel, plan), out_shape=outs, in_s...  7.72 us
    ppermute x9, starting transfers between devices, swapped(): lax.ppermute(block, axis, [(i, i ^ bits) for i in range(lax.axis_size(axi...  5.86 us
    ppermute x2, starting transfers between devices, passed_on(): moved.append(lax.ppermute(held, 'groups', route))  2.46 us
  transfers between devices with their start and end apart: 17, of which 5 were waited for; matrix products, arithmetic and copies ran while one was open for 1% of the time, Pallas kernels for 34%

profile of v4, /device:TPU:0, one launch (start us, length us, event | category | flops | bytes accessed | tf_op | source)
XLA Modules:
  0.0 76.0 jit_solution(6230295865257707541)
XLA Ops:
  0.7 2.9 %pack_first.1 = (bf16[512,256]{1,0:T(8,128)(2,1)}, bf16[512,768]{1,0:T(8,128)(2,1)}) custom-call(s32[2]{0:T(128)} %pad_add_fusion.1.rows_ref, bf16[512,128]{1,0:T(8,128)(2,1)} %refs_0_.4, bf16[512,128]{1,0:T(8,128)(2,1)} %refs_1_.6, bf16[4096,512]{1,0:T(8,128)(2,1)} %refs_0_.3, bf16[4096,128]{1,0:T(8,128)(2,1)} %refs_1_.4, bf16[4096,128]{1,0:T(8,128)(2,1)} %refs_2_.3), custom_call_target="tpu_custom_call" | custom-call | bytes 2097152 | tf_op jit(solution)/shard_map/pack_first/pallas_call | solution.py:332
  3.6 5.6 %collective-permute-start = (bf16[512,256]{1,0:T(8,128)(2,1)}, bf16[512,256]{1,0:T(8,128)(2,1)}, u32[]{:S(2)}, u32[]{:S(2)}) collective-permute-start(bf16[512,256]{1,0:T(8,128)(2,1)} %get-tuple-element.31), channel_id=1, source_target_pairs={{0,4},{4,8},{8,12},{1,5},{5,9},{9,13},{2,6},{6,10},{10,14},{3,7},{... | collective-permute-start | bytes 786440 | tf_op jit(solution)/shard_map/kv_forward/ppermute | solution.py:22
  9.2 3.3 %collective-permute-start.2 = (bf16[512,256]{1,0:T(8,128)(2,1)}, bf16[512,256]{1,0:T(8,128)(2,1)}, u32[]{:S(2)}, u32[]{:S(2)}) collective-permute-start(bf16[512,256]{1,0:T(8,128)(2,1)} %get-tuple-element.31), channel_id=1, source_target_pairs={{0,12},{1,13},{2,14},{3,15},{16,28},{17,29},{18,30},{19,31}} | collective-permute-start | bytes 786440 | tf_op jit(solution)/shard_map/kv_forward/ppermute | solution.py:22
  12.5 1.5 %collective-permute-start.6 = (bf16[512,768]{1,0:T(8,128)(2,1)}, bf16[512,768]{1,0:T(8,128)(2,1)S(1)}, u32[]{:S(2)}, u32[]{:S(2)}) collective-permute-start(bf16[512,768]{1,0:T(8,128)(2,1)} %get-tuple-element.45), channel_id=1, source_target_pairs={{0,2},{1,3},{2,0},{3,1},{4,6},{5,7},{6,4},{7,5},{8,10},{9,11},{10,... | collective-permute-start | bytes 2359304 | tf_op jit(solution)/shard_map/weight_exchange/ppermute | solution.py:26
  14.6 4.8 %pack_rest.1 = (bf16[1024,768]{1,0:T(8,128)(2,1)}, bf16[1024,768]{1,0:T(8,128)(2,1)}, bf16[512,768]{1,0:T(8,128)(2,1)}) custom-call(s32[3]{0:T(128)} %pad_add_fusion.rows_ref, bf16[4096,512]{1,0:T(8,128)(2,1)} %refs_0_.3, bf16[4096,128]{1,0:T(8,128)(2,1)} %refs_1_.4, bf16[4096,128]{1,0:T(8,128)(2,1)} %refs_2_.3), custom_call_target="tpu_custom_call" | custom-call | bytes 7864320 | tf_op jit(solution)/shard_map/pack_rest/pallas_call | solution.py:332
  20.3 1.3 %collective-permute-start.1 = (bf16[512,256]{1,0:T(8,128)(2,1)}, bf16[512,256]{1,0:T(8,128)(2,1)S(1)}, u32[]{:S(2)}, u32[]{:S(2)}) collective-permute-start(bf16[512,256]{1,0:T(8,128)(2,1)} %collective-permute-done.kv1.refs_2_), channel_id=1, source_target_pairs={{0,4},{4,8},{8,12},{1,5},{5,9},{9,13},{2,6},{6,10},{10,14},{3,7},{... | collective-permute-start | bytes 786440 | tf_op jit(solution)/shard_map/kv_forward/ppermute | solution.py:22
  21.7 0.9 %copy-done.4 = bf16[512,128]{1,0:T(8,128)(2,1)S(1)} copy-done((bf16[512,128]{1,0:T(8,128)(2,1)S(1)}, bf16[512,128]{1,0:T(8,128)(2,1)}, u32[]{:S(2)}) %copy-start.4) | copy-done | bytes 131096
  22.6 3.9 %near_stats.1 = (f32[4,512]{1,0:T(4,128)S(1)}, f32[4,512]{1,0:T(4,128)S(1)}, f32[4,512]{1,0:T(4,128)S(1)}) custom-call(s32[4,16]{1,0:T(4,128)S(1)} %fusion.4.flag_ref.refs_0_, bf16[512,512]{1,0:T(8,128)(2,1)S(1)} %copy-done, bf16[512,512]{1,0:T(8,128)(2,1)S(1)} %copy-done.1, bf16[512,128]{1,0:T(8,128)(2,1)S(1)} %copy-done.3, bf16[512,128]{1,0:T(8,128)(2,1)S(1)} %copy-done.4, ...), custom_call_target="tpu_custom_call" | custom-call | tf_op jit(solution)/shard_map/near_stats/pallas_call | solution.py:273
  26.6 1.4 %collective-permute-done.1.refs_6_ = bf16[512,256]{1,0:T(8,128)(2,1)S(1)} collective-permute-done((bf16[512,256]{1,0:T(8,128)(2,1)}, bf16[512,256]{1,0:T(8,128)(2,1)S(1)}, u32[]{:S(2)}, u32[]{:S(2)}) %collective-permute-start.1) | collective-permute-done | bytes 262176 | tf_op jit(solution)/shard_map/kv_forward/ppermute | solution.py:22
  28.0 5.9 %far_stats.1 = (f32[3,4,512]{2,1,0:T(4,128)S(1)}, f32[4,128,512]{2,1,0:T(8,128)S(1)}, bf16[512,256]{1,0:T(8,128)(2,1)S(1)}) custom-call(s32[4,16]{1,0:T(4,128)S(1)} %fusion.4.flag_ref.refs_0_, bf16[512,512]{1,0:T(8,128)(2,1)S(1)} %copy-done, bf16[512,512]{1,0:T(8,128)(2,1)S(1)} %copy-done.1, f32[4,512]{1,0:T(4,128)S(1)} %get-tuple-element.37.refs_3_, ...), custom_call_target="tpu_custom_call" | custom-call | tf_op jit(solution)/shard_map/far_stats/pallas_call | solution.py:273
  34.0 1.6 %collective-permute-start.10 = (bf16[512,768]{1,0:T(8,128)(2,1)S(1)}, bf16[512,768]{1,0:T(8,128)(2,1)S(1)}, u32[]{:S(2)}, u32[]{:S(2)}) collective-permute-start(bf16[512,768]{1,0:T(8,128)(2,1)S(1)} %collective-permute-done.6.refs_5_.refs_6_), channel_id=1, source_target_pairs={{0,16},{16,0},{1,17},{17,1},{2,18},{18,2},{3,19},{19,3},{4,20},{20... | collective-permute-start | bytes 2359304 | tf_op jit(solution)/shard_map/weight_exchange/ppermute | solution.py:478
  35.5 1.3 %collective-permute-start.8 = (bf16[512,256]{1,0:T(8,128)(2,1)S(1)}, bf16[512,256]{1,0:T(8,128)(2,1)S(1)}, u32[]{:S(2)}, u32[]{:S(2)}) collective-permute-start(bf16[512,256]{1,0:T(8,128)(2,1)S(1)} %get-tuple-element.48), channel_id=1, source_target_pairs={{4,0},{8,4},{12,8},{5,1},{9,5},{13,9},{6,2},{10,6},{14,10},{7,3},{... | collective-permute-start | bytes 786440 | tf_op jit(solution)/shard_map/kv_return/ppermute | solution.py:22
  36.8 2.9 %longest_gradients.1 = (bf16[512,256]{1,0:T(8,128)(2,1)S(1)}, f32[4,128,512]{2,1,0:T(8,128)S(1)}) custom-call(s32[4,16]{1,0:T(4,128)S(1)} %fusion.4.flag_ref.refs_0_, bf16[512,512]{1,0:T(8,128)(2,1)S(1)} %copy-done, bf16[512,512]{1,0:T(8,128)(2,1)S(1)} %copy-done.1, f32[3,4,512]{2,1,0:T(4,128)S(1)} %get-tuple-element.40.stat_ref, ...), custom_call_target="tpu_custom_call" | custom-call | tf_op jit(solution)/shard_map/longest_gradients/pallas_call | solution.py:273
  39.7 1.5 %collective-permute-start.7 = (bf16[512,256]{1,0:T(8,128)(2,1)S(1)}, bf16[512,256]{1,0:T(8,128)(2,1)S(1)}, u32[]{:S(2)}, u32[]{:S(2)}) collective-permute-start(bf16[512,256]{1,0:T(8,128)(2,1)S(1)} %get-tuple-element.46), channel_id=1, source_target_pairs={{12,0},{13,1},{14,2},{15,3},{28,16},{29,17},{30,18},{31,19}} | collective-permute-start | bytes 786440 | tf_op jit(solution)/shard_map/kv_return/ppermute | solution.py:22
  41.2 5.6 %near_gradients.1 = (f32[512,256]{1,0:T(8,128)S(1)}, f32[512,256]{1,0:T(8,128)S(1)}, bf16[512,512]{1,0:T(8,128)(2,1)S(1)}) custom-call(s32[4,16]{1,0:T(4,128)S(1)} %fusion.4.flag_ref.refs_0_, bf16[512,512]{1,0:T(8,128)(2,1)S(1)} %copy-done, bf16[512,512]{1,0:T(8,128)(2,1)S(1)} %copy-done.1, f32[3,4,512]{2,1,0:T(4,128)S(1)} %get-tuple-element.40.stat_ref, ...), custom_call_target="tpu_custom_call" | custom-call | tf_op jit(solution)/shard_map/near_gradients/pallas_call | solution.py:273
  46.9 1.4 %collective-permute-start.9 = (bf16[512,256]{1,0:T(8,128)(2,1)S(1)}, bf16[512,256]{1,0:T(8,128)(2,1)S(1)}, u32[]{:S(2)}, u32[]{:S(2)}) collective-permute-start(bf16[512,256]{1,0:T(8,128)(2,1)S(1)} %add_convert_fusion.1), channel_id=1, source_target_pairs={{4,0},{8,4},{12,8},{5,1},{9,5},{13,9},{6,2},{10,6},{14,10},{7,3},{... | collective-permute-start | bytes 786440 | tf_op jit(solution)/shard_map/kv_return/ppermute | solution.py:22
  49.2 3.6 %collective-permute-done.7 = bf16[512,256]{1,0:T(8,128)(2,1)S(1)} collective-permute-done((bf16[512,256]{1,0:T(8,128)(2,1)S(1)}, bf16[512,256]{1,0:T(8,128)(2,1)S(1)}, u32[]{:S(2)}, u32[]{:S(2)}) %collective-permute-start.7) | collective-permute-done | bytes 262176 | tf_op jit(solution)/shard_map/kv_return/ppermute | solution.py:22
  52.9 1.5 %collective-permute-start.5 = (bf16[512,512]{1,0:T(8,128)(2,1)S(1)}, bf16[512,512]{1,0:T(8,128)(2,1)S(1)}, u32[]{:S(2)}, u32[]{:S(2)}) collective-permute-start(bf16[512,512]{1,0:T(8,128)(2,1)S(1)} %get-tuple-element.43.refs_0_), channel_id=1, source_target_pairs={{0,2},{1,3},{2,0},{3,1},{4,6},{5,7},{6,4},{7,5},{8,10},{9,11},{10,... | collective-permute-start | bytes 1572872 | tf_op jit(solution)/shard_map/query_grad_gather/ppermute | solution.py:26
  54.4 4.1 %collective-permute-done.9 = bf16[512,256]{1,0:T(8,128)(2,1)S(1)} collective-permute-done((bf16[512,256]{1,0:T(8,128)(2,1)S(1)}, bf16[512,256]{1,0:T(8,128)(2,1)S(1)}, u32[]{:S(2)}, u32[]{:S(2)}) %collective-permute-start.9) | collective-permute-done | bytes 262176 | tf_op jit(solution)/shard_map/kv_return/ppermute | solution.py:22
  58.5 1.6 %collective-permute-start.12 = (bf16[512,256]{1,0:T(8,128)(2,1)S(1)}, bf16[512,256]{1,0:T(8,128)(2,1)S(1)}, u32[]{:S(2)}, u32[]{:S(2)}) collective-permute-start(bf16[512,256]{1,0:T(8,128)(2,1)S(1)} %add_convert_fusion.refs_1_), channel_id=1, source_target_pairs={{0,2},{1,3},{2,0},{3,1},{4,6},{5,7},{6,4},{7,5},{8,10},{9,11},{10,... | collective-permute-start | bytes 786440 | tf_op jit(solution)/shard_map/kv_grad_gather/ppermute | solution.py:26
  60.1 7.5 %collective-permute-done.5.refs_4_ = bf16[512,512]{1,0:T(8,128)(2,1)S(1)} collective-permute-done((bf16[512,512]{1,0:T(8,128)(2,1)S(1)}, bf16[512,512]{1,0:T(8,128)(2,1)S(1)}, u32[]{:S(2)}, u32[]{:S(2)}) %collective-permute-start.5) | collective-permute-done | bytes 524320 | tf_op jit(solution)/shard_map/query_grad_gather/ppermute | solution.py:26
  68.1 2.4 %query_product.1.refs_0_ = f32[512,1024]{1,0:T(8,128)S(1)} custom-call(s32[1]{0:T(128)} %bitcast.place_ref, bf16[512,512]{1,0:T(8,128)(2,1)S(1)} %get-tuple-element.43.refs_0_, bf16[1024,768]{1,0:T(8,128)(2,1)S(1)} %copy-done.2, bf16[512,512]{1,0:T(8,128)(2,1)S(1)} %collective-permute-done.3.refs_2_, ...), custom_call_target="tpu_custom_call" | custom-call | tf_op jit(solution)/shard_map/query_product/pallas_call | solution.py:273
  70.6 1.5 %collective-permute-done.16.refs_9_ = bf16[512,256]{1,0:T(8,128)(2,1)S(1)} collective-permute-done((bf16[512,256]{1,0:T(8,128)(2,1)S(1)}, bf16[512,256]{1,0:T(8,128)(2,1)S(1)}, u32[]{:S(2)}, u32[]{:S(2)}) %collective-permute-start.16) | collective-permute-done | bytes 262176 | tf_op jit(solution)/shard_map/kv_grad_gather/ppermute | solution.py:26
  72.1 3.7 %last_product.1 = bf16[512,1024]{1,0:T(8,128)(2,1)} custom-call(s32[1]{0:T(128)} %bitcast.place_ref, f32[512,1024]{1,0:T(8,128)S(1)} %query_product.1.refs_0_, bf16[512,256]{1,0:T(8,128)(2,1)S(1)} %add_convert_fusion.refs_1_, bf16[1024,768]{1,0:T(8,128)(2,1)S(1)} %copy-done.2, bf16[512,256]{1,0:T(8,128)(2,1)S(1)} %collective-permute-done.11.refs_3_, ...), custom_call_target="tpu_custom_call" | custom-call | tf_op jit(solution)/shard_map/last_product/pallas_call | solution.py:273
  (41 shorter events, 3.8 us)
Async XLA Ops:
  3.6 16.7 %collective-permute-start = (bf16[512,256]{1,0:T(8,128)(2,1)}, bf16[512,256]{1,0:T(8,128)(2,1)}, u32[]{:S(2)}, u32[]{:S(2)}) collective-permute-start(bf16[512,256]{1,0:T(8,128)(2,1)} %get-tuple-element.31), channel_id=1, source_target_pairs={{0,4},{4,8},{8,12},{1,5},{5,9},{9,13},{2,6},{6,10},{10,14},{3,7},{... | collective-permute-start | bytes 786440 | tf_op jit(solution)/shard_map/kv_forward/ppermute | solution.py:22
  9.2 17.4 %collective-permute-start.2 = (bf16[512,256]{1,0:T(8,128)(2,1)}, bf16[512,256]{1,0:T(8,128)(2,1)}, u32[]{:S(2)}, u32[]{:S(2)}) collective-permute-start(bf16[512,256]{1,0:T(8,128)(2,1)} %get-tuple-element.31), channel_id=1, source_target_pairs={{0,12},{1,13},{2,14},{3,15},{16,28},{17,29},{18,30},{19,31}} | collective-permute-start | bytes 786440 | tf_op jit(solution)/shard_map/kv_forward/ppermute | solution.py:22
  12.5 21.4 %collective-permute-start.6 = (bf16[512,768]{1,0:T(8,128)(2,1)}, bf16[512,768]{1,0:T(8,128)(2,1)S(1)}, u32[]{:S(2)}, u32[]{:S(2)}) collective-permute-start(bf16[512,768]{1,0:T(8,128)(2,1)} %get-tuple-element.45), channel_id=1, source_target_pairs={{0,2},{1,3},{2,0},{3,1},{4,6},{5,7},{6,4},{7,5},{8,10},{9,11},{10,... | collective-permute-start | bytes 2359304 | tf_op jit(solution)/shard_map/weight_exchange/ppermute | solution.py:26
  14.6 5.6 %copy-start.6 = (s32[4,8]{1,0:T(4,128)S(1)}, s32[4,8]{1,0:T(4,128)}, u32[]{:S(2)}) copy-start(s32[4,8]{1,0:T(4,128)} %param.12) | copy-start | bytes 388
  14.6 7.1 %copy-start = (bf16[512,512]{1,0:T(8,128)(2,1)S(1)}, bf16[512,512]{1,0:T(8,128)(2,1)}, u32[]{:S(2)}) copy-start(bf16[512,512]{1,0:T(8,128)(2,1)} %query_ref.4) | copy-start | bytes 1572868
  14.6 7.1 %copy-start.1 = (bf16[512,512]{1,0:T(8,128)(2,1)S(1)}, bf16[512,512]{1,0:T(8,128)(2,1)}, u32[]{:S(2)}) copy-start(bf16[512,512]{1,0:T(8,128)(2,1)} %grad_ref.5) | copy-start | bytes 1572868
  14.6 7.1 %copy-start.3 = (bf16[512,128]{1,0:T(8,128)(2,1)S(1)}, bf16[512,128]{1,0:T(8,128)(2,1)}, u32[]{:S(2)}) copy-start(bf16[512,128]{1,0:T(8,128)(2,1)} %refs_0_.4) | copy-start | bytes 393220
  19.5 48.7 %collective-permute-start.4 = (bf16[1024,768]{1,0:T(8,128)(2,1)}, bf16[1024,768]{1,0:T(8,128)(2,1)S(1)}, u32[]{:S(2)}, u32[]{:S(2)}) collective-permute-start(bf16[1024,768]{1,0:T(8,128)(2,1)} %get-tuple-element.35), channel_id=1, source_target_pairs={{0,1},{1,0},{2,3},{3,2},{4,5},{5,4},{6,7},{7,6},{8,9},{9,8},{10,11... | collective-permute-start | bytes 4718600 | tf_op jit(solution)/shard_map/weight_exchange/ppermute | solution.py:26
  19.5 28.8 %collective-permute-start.14 = (bf16[512,768]{1,0:T(8,128)(2,1)}, bf16[512,768]{1,0:T(8,128)(2,1)}, u32[]{:S(2)}, u32[]{:S(2)}) collective-permute-start(bf16[512,768]{1,0:T(8,128)(2,1)} %get-tuple-element.54), channel_id=1, source_target_pairs={{0,3},{1,2},{2,1},{3,0},{4,7},{5,6},{6,5},{7,4},{8,11},{9,10},{10,... | collective-permute-start | bytes 2359304 | tf_op jit(solution)/shard_map/weight_exchange/ppermute | solution.py:26
  20.3 7.7 %collective-permute-start.1 = (bf16[512,256]{1,0:T(8,128)(2,1)}, bf16[512,256]{1,0:T(8,128)(2,1)S(1)}, u32[]{:S(2)}, u32[]{:S(2)}) collective-permute-start(bf16[512,256]{1,0:T(8,128)(2,1)} %collective-permute-done.kv1.refs_2_), channel_id=1, source_target_pairs={{0,4},{4,8},{8,12},{1,5},{5,9},{9,13},{2,6},{6,10},{10,14},{3,7},{... | collective-permute-start | bytes 786440 | tf_op jit(solution)/shard_map/kv_forward/ppermute | solution.py:22
  21.7 0.9 %copy-start.4 = (bf16[512,128]{1,0:T(8,128)(2,1)S(1)}, bf16[512,128]{1,0:T(8,128)(2,1)}, u32[]{:S(2)}) copy-start(bf16[512,128]{1,0:T(8,128)(2,1)} %refs_1_.6) | copy-start | bytes 393220
  33.9 7.3 %copy-start.5 = (bf16[512,128]{1,0:T(8,128)(2,1)S(1)}, bf16[512,128]{1,0:T(8,128)(2,1)}, u32[]{:S(2)}) copy-start(bf16[512,128]{1,0:T(8,128)(2,1)} %refs_1_.6) | copy-start | bytes 393220
  34.0 24.5 %collective-permute-start.10 = (bf16[512,768]{1,0:T(8,128)(2,1)S(1)}, bf16[512,768]{1,0:T(8,128)(2,1)S(1)}, u32[]{:S(2)}, u32[]{:S(2)}) collective-permute-start(bf16[512,768]{1,0:T(8,128)(2,1)S(1)} %collective-permute-done.6.refs_5_.refs_6_), channel_id=1, source_target_pairs={{0,16},{16,0},{1,17},{17,1},{2,18},{18,2},{3,19},{19,3},{4,20},{20... | collective-permute-start | bytes 2359304 | tf_op jit(solution)/shard_map/weight_exchange/ppermute | solution.py:478
  35.5 11.3 %collective-permute-start.8 = (bf16[512,256]{1,0:T(8,128)(2,1)S(1)}, bf16[512,256]{1,0:T(8,128)(2,1)S(1)}, u32[]{:S(2)}, u32[]{:S(2)}) collective-permute-start(bf16[512,256]{1,0:T(8,128)(2,1)S(1)} %get-tuple-element.48), channel_id=1, source_target_pairs={{4,0},{8,4},{12,8},{5,1},{9,5},{13,9},{6,2},{10,6},{14,10},{7,3},{... | collective-permute-start | bytes 786440 | tf_op jit(solution)/shard_map/kv_return/ppermute | solution.py:22
  39.7 13.2 %collective-permute-start.7 = (bf16[512,256]{1,0:T(8,128)(2,1)S(1)}, bf16[512,256]{1,0:T(8,128)(2,1)S(1)}, u32[]{:S(2)}, u32[]{:S(2)}) collective-permute-start(bf16[512,256]{1,0:T(8,128)(2,1)S(1)} %get-tuple-element.46), channel_id=1, source_target_pairs={{12,0},{13,1},{14,2},{15,3},{28,16},{29,17},{30,18},{31,19}} | collective-permute-start | bytes 786440 | tf_op jit(solution)/shard_map/kv_return/ppermute | solution.py:22
  46.8 21.3 %copy-start.2 = (bf16[1024,768]{1,0:T(8,128)(2,1)S(1)}, bf16[1024,768]{1,0:T(8,128)(2,1)}, u32[]{:S(2)}) copy-start(bf16[1024,768]{1,0:T(8,128)(2,1)} %get-tuple-element.44.refs_1_.refs_2_) | copy-start | bytes 4718596
  46.9 11.5 %collective-permute-start.9 = (bf16[512,256]{1,0:T(8,128)(2,1)S(1)}, bf16[512,256]{1,0:T(8,128)(2,1)S(1)}, u32[]{:S(2)}, u32[]{:S(2)}) collective-permute-start(bf16[512,256]{1,0:T(8,128)(2,1)S(1)} %add_convert_fusion.1), channel_id=1, source_target_pairs={{4,0},{8,4},{12,8},{5,1},{9,5},{13,9},{6,2},{10,6},{14,10},{7,3},{... | collective-permute-start | bytes 786440 | tf_op jit(solution)/shard_map/kv_return/ppermute | solution.py:22
  48.4 22.1 %collective-permute-start.15 = (bf16[512,768]{1,0:T(8,128)(2,1)}, bf16[512,768]{1,0:T(8,128)(2,1)S(1)}, u32[]{:S(2)}, u32[]{:S(2)}) collective-permute-start(bf16[512,768]{1,0:T(8,128)(2,1)} %collective-permute-done.14.refs_10_), channel_id=1, source_target_pairs={{0,16},{16,0},{1,17},{17,1},{2,18},{18,2},{3,19},{19,3},{4,20},{20... | collective-permute-start | bytes 2359304 | tf_op jit(solution)/shard_map/weight_exchange/ppermute | solution.py:478
  52.9 14.7 %collective-permute-start.5 = (bf16[512,512]{1,0:T(8,128)(2,1)S(1)}, bf16[512,512]{1,0:T(8,128)(2,1)S(1)}, u32[]{:S(2)}, u32[]{:S(2)}) collective-permute-start(bf16[512,512]{1,0:T(8,128)(2,1)S(1)} %get-tuple-element.43.refs_0_), channel_id=1, source_target_pairs={{0,2},{1,3},{2,0},{3,1},{4,6},{5,7},{6,4},{7,5},{8,10},{9,11},{10,... | collective-permute-start | bytes 1572872 | tf_op jit(solution)/shard_map/query_grad_gather/ppermute | solution.py:26
  58.4 9.2 %collective-permute-start.3 = (bf16[512,512]{1,0:T(8,128)(2,1)S(1)}, bf16[512,512]{1,0:T(8,128)(2,1)S(1)}, u32[]{:S(2)}, u32[]{:S(2)}) collective-permute-start(bf16[512,512]{1,0:T(8,128)(2,1)S(1)} %get-tuple-element.43.refs_0_), channel_id=1, source_target_pairs={{0,1},{1,0},{2,3},{3,2},{4,5},{5,4},{6,7},{7,6},{8,9},{9,8},{10,11... | collective-permute-start | bytes 1572872 | tf_op jit(solution)/shard_map/query_grad_gather/ppermute | solution.py:26
  58.5 12.0 %collective-permute-start.12 = (bf16[512,256]{1,0:T(8,128)(2,1)S(1)}, bf16[512,256]{1,0:T(8,128)(2,1)S(1)}, u32[]{:S(2)}, u32[]{:S(2)}) collective-permute-start(bf16[512,256]{1,0:T(8,128)(2,1)S(1)} %add_convert_fusion.refs_1_), channel_id=1, source_target_pairs={{0,2},{1,3},{2,0},{3,1},{4,6},{5,7},{6,4},{7,5},{8,10},{9,11},{10,... | collective-permute-start | bytes 786440 | tf_op jit(solution)/shard_map/kv_grad_gather/ppermute | solution.py:26
  67.6 3.0 %collective-permute-start.13 = (bf16[512,512]{1,0:T(8,128)(2,1)S(1)}, bf16[512,512]{1,0:T(8,128)(2,1)S(1)}, u32[]{:S(2)}, u32[]{:S(2)}) collective-permute-start(bf16[512,512]{1,0:T(8,128)(2,1)S(1)} %collective-permute-done.5.refs_4_), channel_id=1, source_target_pairs={{0,1},{1,0},{2,3},{3,2},{4,5},{5,4},{6,7},{7,6},{8,9},{9,8},{10,11... | collective-permute-start | bytes 1572872 | tf_op jit(solution)/shard_map/query_grad_gather/ppermute | solution.py:26
  67.6 3.0 %collective-permute-start.11 = (bf16[512,256]{1,0:T(8,128)(2,1)S(1)}, bf16[512,256]{1,0:T(8,128)(2,1)S(1)}, u32[]{:S(2)}, u32[]{:S(2)}) collective-permute-start(bf16[512,256]{1,0:T(8,128)(2,1)S(1)} %add_convert_fusion.refs_1_), channel_id=1, source_target_pairs={{0,1},{1,0},{2,3},{3,2},{4,5},{5,4},{6,7},{7,6},{8,9},{9,8},{10,11... | collective-permute-start | bytes 786440 | tf_op jit(solution)/shard_map/kv_grad_gather/ppermute | solution.py:26
  70.5 1.6 %collective-permute-start.16 = (bf16[512,256]{1,0:T(8,128)(2,1)S(1)}, bf16[512,256]{1,0:T(8,128)(2,1)S(1)}, u32[]{:S(2)}, u32[]{:S(2)}) collective-permute-start(bf16[512,256]{1,0:T(8,128)(2,1)S(1)} %collective-permute-done.12.refs_5_), channel_id=1, source_target_pairs={{0,1},{1,0},{2,3},{3,2},{4,5},{5,4},{6,7},{7,6},{8,9},{9,8},{10,11... | collective-permute-start | bytes 786440 | tf_op jit(solution)/shard_map/kv_grad_gather/ppermute | solution.py:26

commit v5 on v4

--- a/solution.py
+++ b/solution.py
@@ -182,15 +182,13 @@
 
 def far_kernel(blocks, reach, heads, distances, middle, *refs):
     count = len(distances)
-    flag_ref, query_ref, grad_ref, m_ref, l_ref, r_ref = refs[:6]
+    flag_ref, qs, gs, m_ref, l_ref, r_ref = refs[:6]
     kv_refs = refs[6 : 6 + count]
     stat_ref, part_ref = refs[6 + count : 8 + count]
     out_refs = refs[8 + count : 8 + count + len(middle)]
-    qs, gs, kt, s_ref, g_ref, p_ref, ds_ref = refs[8 + count + len(middle) :]
+    kt, s_ref, g_ref, p_ref, ds_ref = refs[8 + count + len(middle) :]
     lanes = heads * BLOCK
     rows = blocks * BLOCK
-    stack_heads(query_ref, qs, blocks, heads)
-    stack_heads(grad_ref, gs, blocks, heads)
     keys = [keys_of(r) for r in kv_refs]
     values = [values_of(r) for r in kv_refs]
     for c in range(len(middle)):
@@ -223,7 +221,7 @@
             part_ref[i] = jnp.zeros_like(part_ref[i])
 
 
-def gradient_kernel(blocks, reach, heads, distances, final, flag_ref, query_ref, grad_ref, stat_ref, part_ref, *refs):
+def gradient_kernel(blocks, reach, heads, distances, final, flag_ref, qs, gs, stat_ref, part_ref, *refs):
     count = len(distances)
     keys, values = [], []
     for d in distances:
@@ -236,11 +234,9 @@
             values.append(values_of(refs[0]))
             refs = refs[1:]
     out_refs, query_out = refs[:count], refs[count]
-    qs, gs, kt, s_ref, g_ref, p_ref, ds_ref = refs[count + 1 :]
+    kt, s_ref, g_ref, p_ref, ds_ref = refs[count + 1 :]
     lanes = heads * BLOCK
     rows = blocks * BLOCK
-    stack_heads(query_ref, qs, blocks, heads)
-    stack_heads(grad_ref, gs, blocks, heads)
     for c in range(count):
         kt[:, c * rows : (c + 1) * rows] = keys[c][...].T
     for i in range(blocks):
@@ -343,7 +339,7 @@
 
 def product_kernel(peers, group_count, query_width, last, place_ref, *refs):
     before, refs = (refs[0], refs[1:]) if last else (None, refs)
-    out_ref, left, right, acc, sems = refs[-5:]
+    out_ref, left, right, acc, base, sems = refs[-6:]
     rows_out = right.shape[1]
     copies = []
     at = 0
@@ -362,7 +358,7 @@
         copies.append([pltpu.make_async_copy(a, b, sems.at[at + m]) for m, (a, b) in enumerate(moves)])
         at += len(moves)
     if last:
-        copies[0].append(pltpu.make_async_copy(before, acc, sems.at[at]))
+        copies[-1].append(pltpu.make_async_copy(before, base, sems.at[at]))
     for group in copies:
         for copy in group:
             copy.start()
@@ -375,8 +371,10 @@
             total = lax.dot_general(
                 left[n, :, columns], right[n, span, columns], NT, preferred_element_type=jnp.float32
             )
-            if n or last:
+            if n:
                 total = total + acc[:, span]
+            if last and n == len(peers) - 1:
+                total = total + base[:, span].astype(jnp.float32)
             if n < len(peers) - 1:
                 acc[:, span] = total
             else:
@@ -429,18 +427,18 @@
         flags = attention_flags(doc_blocks, blocks, reach, place)
 
     def scratch(count, gradient_count):
-        stacks = [pltpu.VMEM((blocks * lanes, HEAD_WIDTH), bf16)] * 2
         tiles = [pltpu.VMEM((2, count * rows, lanes), f32)] * 2
         if not gradient_count:
-            return stacks + tiles
+            return tiles
         turned = [pltpu.VMEM((HEAD_WIDTH, gradient_count * rows), bf16)]
-        return stacks + turned + tiles + [pltpu.VMEM((gradient_count * rows, blocks * lanes), bf16)] * 2
+        return turned + tiles + [pltpu.VMEM((gradient_count * rows, blocks * lanes), bf16)] * 2
 
     near_in = [query, output_gradient, key_head_rows, value_head_rows, window[1]]
     stats = [jax.ShapeDtypeStruct((blocks, lanes), f32)] * 3
+    stats += [jax.ShapeDtypeStruct((blocks * lanes, HEAD_WIDTH), bf16)] * 2
     near_in[0], pair_weights = lax.optimization_barrier((near_in[0], pair_weights))
     with jax.named_scope("near_stats"):
-        top, total, dot_total = kernel_call(
+        top, total, dot_total, query_stack, grad_stack = kernel_call(
             functools.partial(near_stats_kernel, blocks, reach, heads),
             flags, near_in, stats, scratch(2, 0),
         )
@@ -453,7 +451,7 @@
             stat, part, *middle_grads = kernel_call(
                 functools.partial(far_kernel, blocks, reach, heads, far, middle),
                 flags,
-                [query, output_gradient, top, total, dot_total] + [window[d] for d in far],
+                [query_stack, grad_stack, top, total, dot_total] + [window[d] for d in far],
                 [jax.ShapeDtypeStruct((3, blocks, lanes), f32), part_shape]
                 + [jax.ShapeDtypeStruct(kv_shape, bf16)] * len(middle),
                 scratch(len(far), max(len(middle), 1)),
@@ -463,7 +461,7 @@
             grads[reach], part = kernel_call(
                 functools.partial(gradient_kernel, blocks, reach, heads, (reach,), False),
                 flags,
-                [query, output_gradient, stat, part, window[reach]],
+                [query_stack, grad_stack, stat, part, window[reach]],
                 [jax.ShapeDtypeStruct(kv_shape, bf16), part_shape],
                 scratch(1, 1),
             )
@@ -485,7 +483,7 @@
         own, grads[1], query_grad = kernel_call(
             functools.partial(gradient_kernel, blocks, reach, heads, (0, 1), True),
             flags,
-            [query, output_gradient, stat, part, key_head_rows, value_head_rows, window[1]],
+            [query_stack, grad_stack, stat, part, key_head_rows, value_head_rows, window[1]],
             [
                 jax.ShapeDtypeStruct(kv_shape, f32),
                 jax.ShapeDtypeStruct(kv_shape, f32),
@@ -550,9 +548,10 @@
                     pltpu.VMEM((len(entries), rows, total_width), bf16),
                     pltpu.VMEM((len(entries), rows_out, total_width), bf16),
                     pltpu.VMEM((rows, rows_out), f32),
+                    pltpu.VMEM((rows, rows_out), f32 if before is None else before.dtype),
                     pltpu.SemaphoreType.DMA((count,)),
                 ],
-                0,
+                1,
                 range(len(arrays)),
             )
         return result

time: 76.4 us -> 74.4 us (0.974)
  Pallas kernels: 32.2 us -> 30.5 us
  starting transfers between devices: 22.8 us -> 21.6 us
  local copies, waits for them, and re-layouts: 0.92 us -> 2.1 us
    ppermute x9, waiting for transfers between devices: 9.02 us -> 7.17 us  [swapped(): lax.ppermute(block, axis, [(i, i ^ bits) for i in range(lax.axis_size(axi...]
    pallas_call x6, Pallas kernels: 24.5 us -> 22.8 us  [kernel_call(): pl.pallas_call(kernel, out_shape=outs, in_specs=[pl.BlockSpec(memory_spac...]
    unnamed x14 -> x12, local copies, waits for them, and re-layouts: 0.92 us -> 2.1 us
    ppermute x6, starting transfers between devices: 14.5 us -> 13.6 us  [shifted(): return lax.ppermute(block, axis, route)]
    ppermute x6, waiting for transfers between devices: 9.12 us -> 9.93 us  [shifted(): return lax.ppermute(block, axis, route)]
  transfers between devices with their start and end apart: 17 -> 17, of which waited for: 5 -> 7; matrix products, arithmetic and copies ran while one was open for 1% -> 1% of each run, Pallas kernels for 34% -> 32%
where the time goes in v5:
time: 74.4 us; the launch traced here: 74 us
  Pallas kernels  30.5 us (41%)
  starting transfers between devices  21.6 us (29%)
  waiting for transfers between devices  17.9 us (24%)
  local copies, waits for them, and re-layouts  2.1 us (3%)
  other arithmetic  1.57 us (2%)
    pallas_call x6, Pallas kernels, kernel_call(): pl.pallas_call(kernel, out_shape=outs, in_specs=[pl.BlockSpec(memory_spac...  22.8 us
    ppermute x6, starting transfers between devices, shifted(): return lax.ppermute(block, axis, route)  13.6 us
    ppermute x6, waiting for transfers between devices, shifted(): return lax.ppermute(block, axis, route)  9.93 us
    pallas_call x2, Pallas kernels, packed(): pl.pallas_call(functools.partial(pack_kernel, plan), out_shape=outs, in_s...  7.72 us
    ppermute x9, waiting for transfers between devices, swapped(): lax.ppermute(block, axis, [(i, i ^ bits) for i in range(lax.axis_size(axi...  7.17 us
    ppermute x9, starting transfers between devices, swapped(): lax.ppermute(block, axis, [(i, i ^ bits) for i in range(lax.axis_size(axi...  5.84 us
    ppermute x2, starting transfers between devices, passed_on(): moved.append(lax.ppermute(held, 'groups', route))  2.17 us
    unnamed x12, local copies, waits for them, and re-layouts  2.1 us
  transfers between devices with their start and end apart: 17, of which 7 were waited for; matrix products, arithmetic and copies ran while one was open for 1% of the time, Pallas kernels for 32%

profile of v5, /device:TPU:0, one launch (start us, length us, event | category | flops | bytes accessed | tf_op | source)
XLA Modules:
  0.0 74.0 jit_solution(4285746337552612327)
XLA Ops:
  0.6 2.9 %pack_first.1 = (bf16[512,256]{1,0:T(8,128)(2,1)}, bf16[512,768]{1,0:T(8,128)(2,1)}) custom-call(s32[2]{0:T(128)} %pad_add_fusion.1.rows_ref, bf16[512,128]{1,0:T(8,128)(2,1)} %refs_0_.4, bf16[512,128]{1,0:T(8,128)(2,1)} %refs_1_.4, bf16[4096,512]{1,0:T(8,128)(2,1)} %refs_0_.3, bf16[4096,128]{1,0:T(8,128)(2,1)} %refs_1_.3, bf16[4096,128]{1,0:T(8,128)(2,1)} %refs_2_.2), custom_call_target="tpu_custom_call" | custom-call | bytes 2097152 | tf_op jit(solution)/shard_map/pack_first/pallas_call | solution.py:328
  3.5 4.9 %collective-permute-start = (bf16[512,256]{1,0:T(8,128)(2,1)}, bf16[512,256]{1,0:T(8,128)(2,1)S(1)}, u32[]{:S(2)}, u32[]{:S(2)}) collective-permute-start(bf16[512,256]{1,0:T(8,128)(2,1)} %get-tuple-element.33), channel_id=1, source_target_pairs={{0,4},{4,8},{8,12},{1,5},{5,9},{9,13},{2,6},{6,10},{10,14},{3,7},{... | collective-permute-start | bytes 786440 | tf_op jit(solution)/shard_map/kv_forward/ppermute | solution.py:22
  8.5 3.3 %collective-permute-start.2 = (bf16[512,256]{1,0:T(8,128)(2,1)}, bf16[512,256]{1,0:T(8,128)(2,1)S(1)}, u32[]{:S(2)}, u32[]{:S(2)}) collective-permute-start(bf16[512,256]{1,0:T(8,128)(2,1)} %get-tuple-element.33), channel_id=1, source_target_pairs={{0,12},{1,13},{2,14},{3,15},{16,28},{17,29},{18,30},{19,31}} | collective-permute-start | bytes 786440 | tf_op jit(solution)/shard_map/kv_forward/ppermute | solution.py:22
  11.8 1.6 %collective-permute-start.6 = (bf16[512,768]{1,0:T(8,128)(2,1)}, bf16[512,768]{1,0:T(8,128)(2,1)S(1)}, u32[]{:S(2)}, u32[]{:S(2)}) collective-permute-start(bf16[512,768]{1,0:T(8,128)(2,1)} %get-tuple-element.49), channel_id=1, source_target_pairs={{0,2},{1,3},{2,0},{3,1},{4,6},{5,7},{6,4},{7,5},{8,10},{9,11},{10,... | collective-permute-start | bytes 2359304 | tf_op jit(solution)/shard_map/weight_exchange/ppermute | solution.py:26
  14.0 4.8 %pack_rest.1 = (bf16[1024,768]{1,0:T(8,128)(2,1)}, bf16[1024,768]{1,0:T(8,128)(2,1)}, bf16[512,768]{1,0:T(8,128)(2,1)}) custom-call(s32[3]{0:T(128)} %pad_add_fusion.rows_ref, bf16[4096,512]{1,0:T(8,128)(2,1)} %refs_0_.3, bf16[4096,128]{1,0:T(8,128)(2,1)} %refs_1_.3, bf16[4096,128]{1,0:T(8,128)(2,1)} %refs_2_.2), custom_call_target="tpu_custom_call" | custom-call | bytes 7864320 | tf_op jit(solution)/shard_map/pack_rest/pallas_call | solution.py:328
  19.7 1.3 %collective-permute-start.1 = (bf16[512,256]{1,0:T(8,128)(2,1)S(1)}, bf16[512,256]{1,0:T(8,128)(2,1)S(1)}, u32[]{:S(2)}, u32[]{:S(2)}) collective-permute-start(bf16[512,256]{1,0:T(8,128)(2,1)S(1)} %collective-permute-done.kv1.refs_2_), channel_id=1, source_target_pairs={{0,4},{4,8},{8,12},{1,5},{5,9},{9,13},{2,6},{6,10},{10,14},{3,7},{... | collective-permute-start | bytes 786440 | tf_op jit(solution)/shard_map/kv_forward/ppermute | solution.py:22
  22.1 1.0 %copy-done.4 = bf16[512,512]{1,0:T(8,128)(2,1)S(1)} copy-done((bf16[512,512]{1,0:T(8,128)(2,1)S(1)}, bf16[512,512]{1,0:T(8,128)(2,1)}, u32[]{:S(2)}) %copy-start.4) | copy-done | bytes 524312
  23.2 3.6 %near_stats.1 = (f32[4,512]{1,0:T(4,128)S(1)}, f32[4,512]{1,0:T(4,128)S(1)}, f32[4,512]{1,0:T(4,128)S(1)}, bf16[2048,128]{1,0:T(8,128)(2,1)S(1)}, bf16[2048,128]{1,0:T(8,128)(2,1)S(1)}) custom-call(s32[4,16]{1,0:T(4,128)S(1)} %fusion.4.flag_ref.refs_0_, bf16[512,512]{1,0:T(8,128)(2,1)S(1)} %copy-done.3, bf16[512,512]{1,0:T(8,128)(2,1)S(1)} %copy-done.4, ...), custom_call_target="tpu_custom_call" | custom-call | tf_op jit(solution)/shard_map/near_stats/pallas_call | solution.py:269
  27.0 5.5 %far_stats.1 = (f32[3,4,512]{2,1,0:T(4,128)S(1)}, f32[4,128,512]{2,1,0:T(8,128)S(1)}, bf16[512,256]{1,0:T(8,128)(2,1)S(1)}) custom-call(s32[4,16]{1,0:T(4,128)S(1)} %fusion.4.flag_ref.refs_0_, bf16[2048,128]{1,0:T(8,128)(2,1)S(1)} %get-tuple-element.39.refs_1_.qs, bf16[2048,128]{1,0:T(8,128)(2,1)S(1)} %get-tuple-element.40.refs_2_.gs, ...), custom_call_target="tpu_custom_call" | custom-call | tf_op jit(solution)/shard_map/far_stats/pallas_call | solution.py:269
  32.5 1.6 %collective-permute-start.10 = (bf16[512,768]{1,0:T(8,128)(2,1)S(1)}, bf16[512,768]{1,0:T(8,128)(2,1)S(1)}, u32[]{:S(2)}, u32[]{:S(2)}) collective-permute-start(bf16[512,768]{1,0:T(8,128)(2,1)S(1)} %collective-permute-done.6.refs_5_.refs_6_), channel_id=1, source_target_pairs={{0,16},{16,0},{1,17},{17,1},{2,18},{18,2},{3,19},{19,3},{4,20},{20... | collective-permute-start | bytes 2359304 | tf_op jit(solution)/shard_map/weight_exchange/ppermute | solution.py:476
  34.1 1.3 %collective-permute-start.8 = (bf16[512,256]{1,0:T(8,128)(2,1)S(1)}, bf16[512,256]{1,0:T(8,128)(2,1)S(1)}, u32[]{:S(2)}, u32[]{:S(2)}) collective-permute-start(bf16[512,256]{1,0:T(8,128)(2,1)S(1)} %get-tuple-element.52), channel_id=1, source_target_pairs={{4,0},{8,4},{12,8},{5,1},{9,5},{13,9},{6,2},{10,6},{14,10},{7,3},{... | collective-permute-start | bytes 786440 | tf_op jit(solution)/shard_map/kv_return/ppermute | solution.py:22
  35.4 2.5 %longest_gradients.1 = (bf16[512,256]{1,0:T(8,128)(2,1)S(1)}, f32[4,128,512]{2,1,0:T(8,128)S(1)}) custom-call(s32[4,16]{1,0:T(4,128)S(1)} %fusion.4.flag_ref.refs_0_, bf16[2048,128]{1,0:T(8,128)(2,1)S(1)} %get-tuple-element.39.refs_1_.qs, bf16[2048,128]{1,0:T(8,128)(2,1)S(1)} %get-tuple-element.40.refs_2_.gs, f32[3,4,512]{2,1,0:T(4,128)S(1)} %get-tuple-element.44.stat_ref, ...), custom_call_target="tpu_custom_call" | custom-call | tf_op jit(solution)/shard_map/longest_gradients/pallas_call | solution.py:269
  37.9 1.5 %collective-permute-start.7 = (bf16[512,256]{1,0:T(8,128)(2,1)S(1)}, bf16[512,256]{1,0:T(8,128)(2,1)S(1)}, u32[]{:S(2)}, u32[]{:S(2)}) collective-permute-start(bf16[512,256]{1,0:T(8,128)(2,1)S(1)} %get-tuple-element.50), channel_id=1, source_target_pairs={{12,0},{13,1},{14,2},{15,3},{28,16},{29,17},{30,18},{31,19}} | collective-permute-start | bytes 786440 | tf_op jit(solution)/shard_map/kv_return/ppermute | solution.py:22
  39.4 5.3 %near_gradients.1 = (f32[512,256]{1,0:T(8,128)S(1)}, f32[512,256]{1,0:T(8,128)S(1)}, bf16[512,512]{1,0:T(8,128)(2,1)S(1)}) custom-call(s32[4,16]{1,0:T(4,128)S(1)} %fusion.4.flag_ref.refs_0_, bf16[2048,128]{1,0:T(8,128)(2,1)S(1)} %get-tuple-element.39.refs_1_.qs, bf16[2048,128]{1,0:T(8,128)(2,1)S(1)} %get-tuple-element.40.refs_2_.gs, ...), custom_call_target="tpu_custom_call" | custom-call | tf_op jit(solution)/shard_map/near_gradients/pallas_call | solution.py:269
  44.7 2.3 %collective-permute-done.8 = bf16[512,256]{1,0:T(8,128)(2,1)S(1)} collective-permute-done((bf16[512,256]{1,0:T(8,128)(2,1)S(1)}, bf16[512,256]{1,0:T(8,128)(2,1)S(1)}, u32[]{:S(2)}, u32[]{:S(2)}) %collective-permute-start.8) | collective-permute-done | bytes 262176 | tf_op jit(solution)/shard_map/kv_return/ppermute | solution.py:22
  47.0 1.3 %collective-permute-start.9 = (bf16[512,256]{1,0:T(8,128)(2,1)S(1)}, bf16[512,256]{1,0:T(8,128)(2,1)S(1)}, u32[]{:S(2)}, u32[]{:S(2)}) collective-permute-start(bf16[512,256]{1,0:T(8,128)(2,1)S(1)} %add_convert_fusion.1), channel_id=1, source_target_pairs={{4,0},{8,4},{12,8},{5,1},{9,5},{13,9},{6,2},{10,6},{14,10},{7,3},{... | collective-permute-start | bytes 786440 | tf_op jit(solution)/shard_map/kv_return/ppermute | solution.py:22
  48.9 3.6 %collective-permute-done.7 = bf16[512,256]{1,0:T(8,128)(2,1)S(1)} collective-permute-done((bf16[512,256]{1,0:T(8,128)(2,1)S(1)}, bf16[512,256]{1,0:T(8,128)(2,1)S(1)}, u32[]{:S(2)}, u32[]{:S(2)}) %collective-permute-start.7) | collective-permute-done | bytes 262176 | tf_op jit(solution)/shard_map/kv_return/ppermute | solution.py:22
  52.4 1.5 %collective-permute-start.5 = (bf16[512,512]{1,0:T(8,128)(2,1)S(1)}, bf16[512,512]{1,0:T(8,128)(2,1)S(1)}, u32[]{:S(2)}, u32[]{:S(2)}) collective-permute-start(bf16[512,512]{1,0:T(8,128)(2,1)S(1)} %get-tuple-element.47.refs_0_), channel_id=1, source_target_pairs={{0,2},{1,3},{2,0},{3,1},{4,6},{5,7},{6,4},{7,5},{8,10},{9,11},{10,... | collective-permute-start | bytes 1572872 | tf_op jit(solution)/shard_map/query_grad_gather/ppermute | solution.py:26
  53.9 3.8 %collective-permute-done.9 = bf16[512,256]{1,0:T(8,128)(2,1)S(1)} collective-permute-done((bf16[512,256]{1,0:T(8,128)(2,1)S(1)}, bf16[512,256]{1,0:T(8,128)(2,1)S(1)}, u32[]{:S(2)}, u32[]{:S(2)}) %collective-permute-start.9) | collective-permute-done | bytes 262176 | tf_op jit(solution)/shard_map/kv_return/ppermute | solution.py:22
  57.9 1.6 %collective-permute-start.12 = (bf16[512,256]{1,0:T(8,128)(2,1)S(1)}, bf16[512,256]{1,0:T(8,128)(2,1)S(1)}, u32[]{:S(2)}, u32[]{:S(2)}) collective-permute-start(bf16[512,256]{1,0:T(8,128)(2,1)S(1)} %add_convert_fusion.refs_1_), channel_id=1, source_target_pairs={{0,2},{1,3},{2,0},{3,1},{4,6},{5,7},{6,4},{7,5},{8,10},{9,11},{10,... | collective-permute-start | bytes 786440 | tf_op jit(solution)/shard_map/kv_grad_gather/ppermute | solution.py:26
  59.4 5.6 %collective-permute-done.5.refs_4_ = bf16[512,512]{1,0:T(8,128)(2,1)S(1)} collective-permute-done((bf16[512,512]{1,0:T(8,128)(2,1)S(1)}, bf16[512,512]{1,0:T(8,128)(2,1)S(1)}, u32[]{:S(2)}, u32[]{:S(2)}) %collective-permute-start.5) | collective-permute-done | bytes 524320 | tf_op jit(solution)/shard_map/query_grad_gather/ppermute | solution.py:26
  65.6 2.4 %query_product.1.refs_0_ = f32[512,1024]{1,0:T(8,128)S(1)} custom-call(s32[1]{0:T(128)} %bitcast.place_ref, bf16[512,512]{1,0:T(8,128)(2,1)S(1)} %get-tuple-element.47.refs_0_, bf16[1024,768]{1,0:T(8,128)(2,1)S(1)} %copy-done, bf16[512,512]{1,0:T(8,128)(2,1)S(1)} %collective-permute-done.3.refs_2_, ...), custom_call_target="tpu_custom_call" | custom-call | bytes 2097152 | tf_op jit(solution)/shard_map/query_product/pallas_call | solution.py:269
  68.8 1.5 %collective-permute-done.16.refs_9_ = bf16[512,256]{1,0:T(8,128)(2,1)S(1)} collective-permute-done((bf16[512,256]{1,0:T(8,128)(2,1)S(1)}, bf16[512,256]{1,0:T(8,128)(2,1)S(1)}, u32[]{:S(2)}, u32[]{:S(2)}) %collective-permute-start.16) | collective-permute-done | bytes 262176 | tf_op jit(solution)/shard_map/kv_grad_gather/ppermute | solution.py:26
  70.3 3.6 %last_product.1 = bf16[512,1024]{1,0:T(8,128)(2,1)} custom-call(s32[1]{0:T(128)} %bitcast.place_ref, f32[512,1024]{1,0:T(8,128)S(1)} %query_product.1.refs_0_, bf16[512,256]{1,0:T(8,128)(2,1)S(1)} %add_convert_fusion.refs_1_, bf16[1024,768]{1,0:T(8,128)(2,1)S(1)} %copy-done, bf16[512,256]{1,0:T(8,128)(2,1)S(1)} %collective-permute-done.11.refs_3_, ...), custom_call_target="tpu_custom_call" | custom-call | bytes 1048576 | tf_op jit(solution)/shard_map/last_product/pallas_call | solution.py:269
  (39 shorter events, 5.5 us)
Async XLA Ops:
  3.5 16.2 %collective-permute-start = (bf16[512,256]{1,0:T(8,128)(2,1)}, bf16[512,256]{1,0:T(8,128)(2,1)S(1)}, u32[]{:S(2)}, u32[]{:S(2)}) collective-permute-start(bf16[512,256]{1,0:T(8,128)(2,1)} %get-tuple-element.33), channel_id=1, source_target_pairs={{0,4},{4,8},{8,12},{1,5},{5,9},{9,13},{2,6},{6,10},{10,14},{3,7},{... | collective-permute-start | bytes 786440 | tf_op jit(solution)/shard_map/kv_forward/ppermute | solution.py:22
  8.5 18.3 %collective-permute-start.2 = (bf16[512,256]{1,0:T(8,128)(2,1)}, bf16[512,256]{1,0:T(8,128)(2,1)S(1)}, u32[]{:S(2)}, u32[]{:S(2)}) collective-permute-start(bf16[512,256]{1,0:T(8,128)(2,1)} %get-tuple-element.33), channel_id=1, source_target_pairs={{0,12},{1,13},{2,14},{3,15},{16,28},{17,29},{18,30},{19,31}} | collective-permute-start | bytes 786440 | tf_op jit(solution)/shard_map/kv_forward/ppermute | solution.py:22
  11.8 20.7 %collective-permute-start.6 = (bf16[512,768]{1,0:T(8,128)(2,1)}, bf16[512,768]{1,0:T(8,128)(2,1)S(1)}, u32[]{:S(2)}, u32[]{:S(2)}) collective-permute-start(bf16[512,768]{1,0:T(8,128)(2,1)} %get-tuple-element.49), channel_id=1, source_target_pairs={{0,2},{1,3},{2,0},{3,1},{4,6},{5,7},{6,4},{7,5},{8,10},{9,11},{10,... | collective-permute-start | bytes 2359304 | tf_op jit(solution)/shard_map/weight_exchange/ppermute | solution.py:26
  14.0 5.6 %copy-start.5 = (s32[4,8]{1,0:T(4,128)S(1)}, s32[4,8]{1,0:T(4,128)}, u32[]{:S(2)}) copy-start(s32[4,8]{1,0:T(4,128)} %param.12) | copy-start | bytes 388
  14.0 7.1 %copy-start.1 = (bf16[512,128]{1,0:T(8,128)(2,1)S(1)}, bf16[512,128]{1,0:T(8,128)(2,1)}, u32[]{:S(2)}) copy-start(bf16[512,128]{1,0:T(8,128)(2,1)} %refs_0_.4) | copy-start | bytes 393220
  14.0 7.1 %copy-start.2 = (bf16[512,128]{1,0:T(8,128)(2,1)S(1)}, bf16[512,128]{1,0:T(8,128)(2,1)}, u32[]{:S(2)}) copy-start(bf16[512,128]{1,0:T(8,128)(2,1)} %refs_1_.4) | copy-start | bytes 393220
  18.8 46.8 %collective-permute-start.4 = (bf16[1024,768]{1,0:T(8,128)(2,1)}, bf16[1024,768]{1,0:T(8,128)(2,1)S(1)}, u32[]{:S(2)}, u32[]{:S(2)}) collective-permute-start(bf16[1024,768]{1,0:T(8,128)(2,1)} %get-tuple-element.37), channel_id=1, source_target_pairs={{0,1},{1,0},{2,3},{3,2},{4,5},{5,4},{6,7},{7,6},{8,9},{9,8},{10,11... | collective-permute-start | bytes 4718600 | tf_op jit(solution)/shard_map/weight_exchange/ppermute | solution.py:26
  18.9 29.4 %collective-permute-start.14 = (bf16[512,768]{1,0:T(8,128)(2,1)}, bf16[512,768]{1,0:T(8,128)(2,1)}, u32[]{:S(2)}, u32[]{:S(2)}) collective-permute-start(bf16[512,768]{1,0:T(8,128)(2,1)} %get-tuple-element.58), channel_id=1, source_target_pairs={{0,3},{1,2},{2,1},{3,0},{4,7},{5,6},{6,5},{7,4},{8,11},{9,10},{10,... | collective-permute-start | bytes 2359304 | tf_op jit(solution)/shard_map/weight_exchange/ppermute | solution.py:26
  19.7 7.4 %collective-permute-start.1 = (bf16[512,256]{1,0:T(8,128)(2,1)S(1)}, bf16[512,256]{1,0:T(8,128)(2,1)S(1)}, u32[]{:S(2)}, u32[]{:S(2)}) collective-permute-start(bf16[512,256]{1,0:T(8,128)(2,1)S(1)} %collective-permute-done.kv1.refs_2_), channel_id=1, source_target_pairs={{0,4},{4,8},{8,12},{1,5},{5,9},{9,13},{2,6},{6,10},{10,14},{3,7},{... | collective-permute-start | bytes 786440 | tf_op jit(solution)/shard_map/kv_forward/ppermute | solution.py:22
  21.1 1.0 %copy-start.3 = (bf16[512,512]{1,0:T(8,128)(2,1)S(1)}, bf16[512,512]{1,0:T(8,128)(2,1)}, u32[]{:S(2)}) copy-start(bf16[512,512]{1,0:T(8,128)(2,1)} %query_ref) | copy-start | bytes 1572868
  22.1 1.0 %copy-start.4 = (bf16[512,512]{1,0:T(8,128)(2,1)S(1)}, bf16[512,512]{1,0:T(8,128)(2,1)}, u32[]{:S(2)}) copy-start(bf16[512,512]{1,0:T(8,128)(2,1)} %grad_ref.1) | copy-start | bytes 1572868
  32.5 25.3 %collective-permute-start.10 = (bf16[512,768]{1,0:T(8,128)(2,1)S(1)}, bf16[512,768]{1,0:T(8,128)(2,1)S(1)}, u32[]{:S(2)}, u32[]{:S(2)}) collective-permute-start(bf16[512,768]{1,0:T(8,128)(2,1)S(1)} %collective-permute-done.6.refs_5_.refs_6_), channel_id=1, source_target_pairs={{0,16},{16,0},{1,17},{17,1},{2,18},{18,2},{3,19},{19,3},{4,20},{20... | collective-permute-start | bytes 2359304 | tf_op jit(solution)/shard_map/weight_exchange/ppermute | solution.py:476
  34.1 12.8 %collective-permute-start.8 = (bf16[512,256]{1,0:T(8,128)(2,1)S(1)}, bf16[512,256]{1,0:T(8,128)(2,1)S(1)}, u32[]{:S(2)}, u32[]{:S(2)}) collective-permute-start(bf16[512,256]{1,0:T(8,128)(2,1)S(1)} %get-tuple-element.52), channel_id=1, source_target_pairs={{4,0},{8,4},{12,8},{5,1},{9,5},{13,9},{6,2},{10,6},{14,10},{7,3},{... | collective-permute-start | bytes 786440 | tf_op jit(solution)/shard_map/kv_return/ppermute | solution.py:22
  37.9 14.5 %collective-permute-start.7 = (bf16[512,256]{1,0:T(8,128)(2,1)S(1)}, bf16[512,256]{1,0:T(8,128)(2,1)S(1)}, u32[]{:S(2)}, u32[]{:S(2)}) collective-permute-start(bf16[512,256]{1,0:T(8,128)(2,1)S(1)} %get-tuple-element.50), channel_id=1, source_target_pairs={{12,0},{13,1},{14,2},{15,3},{28,16},{29,17},{30,18},{31,19}} | collective-permute-start | bytes 786440 | tf_op jit(solution)/shard_map/kv_return/ppermute | solution.py:22
  44.6 21.0 %copy-start = (bf16[1024,768]{1,0:T(8,128)(2,1)S(1)}, bf16[1024,768]{1,0:T(8,128)(2,1)}, u32[]{:S(2)}) copy-start(bf16[1024,768]{1,0:T(8,128)(2,1)} %get-tuple-element.48.refs_1_.refs_2_) | copy-start | bytes 4718596
  47.0 10.8 %collective-permute-start.9 = (bf16[512,256]{1,0:T(8,128)(2,1)S(1)}, bf16[512,256]{1,0:T(8,128)(2,1)S(1)}, u32[]{:S(2)}, u32[]{:S(2)}) collective-permute-start(bf16[512,256]{1,0:T(8,128)(2,1)S(1)} %add_convert_fusion.1), channel_id=1, source_target_pairs={{4,0},{8,4},{12,8},{5,1},{9,5},{13,9},{6,2},{10,6},{14,10},{7,3},{... | collective-permute-start | bytes 786440 | tf_op jit(solution)/shard_map/kv_return/ppermute | solution.py:22
  48.3 20.4 %collective-permute-start.15 = (bf16[512,768]{1,0:T(8,128)(2,1)}, bf16[512,768]{1,0:T(8,128)(2,1)S(1)}, u32[]{:S(2)}, u32[]{:S(2)}) collective-permute-start(bf16[512,768]{1,0:T(8,128)(2,1)} %collective-permute-done.14.refs_10_), channel_id=1, source_target_pairs={{0,16},{16,0},{1,17},{17,1},{2,18},{18,2},{3,19},{19,3},{4,20},{20... | collective-permute-start | bytes 2359304 | tf_op jit(solution)/shard_map/weight_exchange/ppermute | solution.py:476
  52.4 12.6 %collective-permute-start.5 = (bf16[512,512]{1,0:T(8,128)(2,1)S(1)}, bf16[512,512]{1,0:T(8,128)(2,1)S(1)}, u32[]{:S(2)}, u32[]{:S(2)}) collective-permute-start(bf16[512,512]{1,0:T(8,128)(2,1)S(1)} %get-tuple-element.47.refs_0_), channel_id=1, source_target_pairs={{0,2},{1,3},{2,0},{3,1},{4,6},{5,7},{6,4},{7,5},{8,10},{9,11},{10,... | collective-permute-start | bytes 1572872 | tf_op jit(solution)/shard_map/query_grad_gather/ppermute | solution.py:26
  57.8 7.3 %collective-permute-start.3 = (bf16[512,512]{1,0:T(8,128)(2,1)S(1)}, bf16[512,512]{1,0:T(8,128)(2,1)S(1)}, u32[]{:S(2)}, u32[]{:S(2)}) collective-permute-start(bf16[512,512]{1,0:T(8,128)(2,1)S(1)} %get-tuple-element.47.refs_0_), channel_id=1, source_target_pairs={{0,1},{1,0},{2,3},{3,2},{4,5},{5,4},{6,7},{7,6},{8,9},{9,8},{10,11... | collective-permute-start | bytes 1572872 | tf_op jit(solution)/shard_map/query_grad_gather/ppermute | solution.py:26
  57.9 10.9 %collective-permute-start.12 = (bf16[512,256]{1,0:T(8,128)(2,1)S(1)}, bf16[512,256]{1,0:T(8,128)(2,1)S(1)}, u32[]{:S(2)}, u32[]{:S(2)}) collective-permute-start(bf16[512,256]{1,0:T(8,128)(2,1)S(1)} %add_convert_fusion.refs_1_), channel_id=1, source_target_pairs={{0,2},{1,3},{2,0},{3,1},{4,6},{5,7},{6,4},{7,5},{8,10},{9,11},{10,... | collective-permute-start | bytes 786440 | tf_op jit(solution)/shard_map/kv_grad_gather/ppermute | solution.py:26
  65.1 3.7 %collective-permute-start.13 = (bf16[512,512]{1,0:T(8,128)(2,1)S(1)}, bf16[512,512]{1,0:T(8,128)(2,1)S(1)}, u32[]{:S(2)}, u32[]{:S(2)}) collective-permute-start(bf16[512,512]{1,0:T(8,128)(2,1)S(1)} %collective-permute-done.5.refs_4_), channel_id=1, source_target_pairs={{0,1},{1,0},{2,3},{3,2},{4,5},{5,4},{6,7},{7,6},{8,9},{9,8},{10,11... | collective-permute-start | bytes 1572872 | tf_op jit(solution)/shard_map/query_grad_gather/ppermute | solution.py:26
  65.1 3.7 %collective-permute-start.11 = (bf16[512,256]{1,0:T(8,128)(2,1)S(1)}, bf16[512,256]{1,0:T(8,128)(2,1)S(1)}, u32[]{:S(2)}, u32[]{:S(2)}) collective-permute-start(bf16[512,256]{1,0:T(8,128)(2,1)S(1)} %add_convert_fusion.refs_1_), channel_id=1, source_target_pairs={{0,1},{1,0},{2,3},{3,2},{4,5},{5,4},{6,7},{7,6},{8,9},{9,8},{10,11... | collective-permute-start | bytes 786440 | tf_op jit(solution)/shard_map/kv_grad_gather/ppermute | solution.py:26
  68.7 1.5 %collective-permute-start.16 = (bf16[512,256]{1,0:T(8,128)(2,1)S(1)}, bf16[512,256]{1,0:T(8,128)(2,1)S(1)}, u32[]{:S(2)}, u32[]{:S(2)}) collective-permute-start(bf16[512,256]{1,0:T(8,128)(2,1)S(1)} %collective-permute-done.12.refs_5_), channel_id=1, source_target_pairs={{0,1},{1,0},{2,3},{3,2},{4,5},{5,4},{6,7},{7,6},{8,9},{9,8},{10,11... | collective-permute-start | bytes 786440 | tf_op jit(solution)/shard_map/kv_grad_gather/ppermute | solution.py:26

commit v6 on v5

--- a/solution.py
+++ b/solution.py
@@ -351,6 +351,13 @@
         columns = slice(parts[0][1], parts[-1][1] + refs[parts[-1][0]].shape[1])
         weights = refs[low:high]
         share = rows_out // len(weights)
+        if n == 0:
+            start, column = pl.multiple_of(place_ref[1] * rows_out, rows_out), columns.start
+            for array in weights:
+                width = array.shape[1]
+                moves.append((array.at[pl.ds(start, rows_out), :], right.at[n, :, column : column + width]))
+                column += width
+            weights = ()
         for step, array in enumerate(weights):
             source = lax.rem(place_ref[0] - step + group_count, group_count) if len(weights) > 1 else 0
             span = pl.ds(pl.multiple_of(source * share, share), share)
@@ -415,12 +422,12 @@
         far = tuple(range(2, reach + 1))
     with jax.named_scope("pack_rest"):
         held, _ = lax.optimization_barrier((weights, key_value))
-        pair_weights, own_weights, *more = packed(
-            [(held, (tp_place ^ 1) * rows_out, rows_out), (held, tp_place * rows_out, rows_out)]
+        pair_weights, *more = packed(
+            [(held, (tp_place ^ 1) * rows_out, rows_out)]
             + [(held, *share_of(bits)) for bits in late]
         )
     with jax.named_scope("weight_exchange"):
-        whole = [own_weights, swapped(pair_weights, "tp", 1)]
+        pair = swapped(pair_weights, "tp", 1)
         sent = [swapped(piece, "tp", bits) for bits, piece in zip([*early, *late], sent + more)]
 
     with jax.named_scope("flags"):
@@ -524,7 +531,7 @@
         q_pieces = gathered(query_grad)
     width = query.shape[1]
     total_width = width + 2 * HEAD_WIDTH
-    place_ids = jnp.full((1,), group_place, jnp.int32)
+    place_ids = jnp.stack([group_place, tp_place]).astype(jnp.int32)
 
     def product(scope, before, entries, out_type):
         arrays = [] if before is None else [before]
@@ -556,13 +563,14 @@
             )
         return result
 
-    sets = [[whole[0]], [whole[1]]]
+    sets = [[w_query], [pair]]
     sets += [shares[at : at + group_count] for at in range(0, len(shares), group_count)]
     acc = product(
         "query_product", None, [([(q_pieces[bits], 0)], sets[bits]) for bits in range(tp_count - 1)], f32
     )
     with jax.named_scope("kv_grad_gather"):
         kv_pieces = gathered(key_value_grad, [acc] + shares[-1:])
+    sets[0] = [key_weight, value_weight]
     entries = [([(kv_pieces[bits], width)], sets[bits]) for bits in range(tp_count - 1)]
     entries.append(([(q_pieces[-1], 0), (kv_pieces[-1], width)], sets[-1]))
     return product("last_product", acc, entries, bf16)

time: 74.4 us -> 76 us (1.022)
  waiting for transfers between devices: 17.9 us -> 19.1 us
    ppermute x9, waiting for transfers between devices: 7.17 us -> 10.3 us  [swapped(): lax.ppermute(block, axis, [(i, i ^ bits) for i in range(lax.axis_size(axi...]
    pallas_call x6, Pallas kernels: 22.8 us -> 24 us  [kernel_call(): pl.pallas_call(kernel, out_shape=outs, in_specs=[pl.BlockSpec(memory_spac...]
    ppermute x6, waiting for transfers between devices: 9.93 us -> 8.78 us  [shifted(): return lax.ppermute(block, axis, route)]
    pallas_call x2, Pallas kernels: 7.72 us -> 6.71 us  [packed(): pl.pallas_call(functools.partial(pack_kernel, plan), out_shape=outs, in_s...]
    unnamed x12 -> x16, local copies, waits for them, and re-layouts: 2.1 us -> 2.1 us
  transfers between devices with their start and end apart: 17 -> 17, of which waited for: 7 -> 7; matrix products, arithmetic and copies ran while one was open for 1% -> 1% of each run, Pallas kernels for 32% -> 31%
where the time goes in v6:
time: 76 us; the launch traced here: 75.6 us
  Pallas kernels  30.7 us (40%)
  starting transfers between devices  21.7 us (29%)
  waiting for transfers between devices  19.1 us (25%)
  local copies, waits for them, and re-layouts  2.1 us (3%)
  other arithmetic  1.63 us (2%)
    pallas_call x6, Pallas kernels, kernel_call(): pl.pallas_call(kernel, out_shape=outs, in_specs=[pl.BlockSpec(memory_spac...  24 us
    ppermute x6, starting transfers between devices, shifted(): return lax.ppermute(block, axis, route)  13.6 us
    ppermute x9, waiting for transfers between devices, swapped(): lax.ppermute(block, axis, [(i, i ^ bits) for i in range(lax.axis_size(axi...  10.3 us
    ppermute x6, waiting for transfers between devices, shifted(): return lax.ppermute(block, axis, route)  8.78 us
    pallas_call x2, Pallas kernels, packed(): pl.pallas_call(functools.partial(pack_kernel, plan), out_shape=outs, in_s...  6.71 us
    ppermute x9, starting transfers between devices, swapped(): lax.ppermute(block, axis, [(i, i ^ bits) for i in range(lax.axis_size(axi...  6 us
    unnamed x16, local copies, waits for them, and re-layouts  2.1 us
    ppermute x2, starting transfers between devices, passed_on(): moved.append(lax.ppermute(held, 'groups', route))  2.08 us
  transfers between devices with their start and end apart: 17, of which 7 were waited for; matrix products, arithmetic and copies ran while one was open for 1% of the time, Pallas kernels for 31%

profile of v6, /device:TPU:0, one launch (start us, length us, event | category | flops | bytes accessed | tf_op | source)
XLA Modules:
  0.0 75.6 jit_solution(7169023478494232290)
XLA Ops:
  0.7 2.9 %pack_first.1 = (bf16[512,256]{1,0:T(8,128)(2,1)}, bf16[512,768]{1,0:T(8,128)(2,1)}) custom-call(s32[2]{0:T(128)} %pad_add_fusion.2.rows_ref, bf16[512,128]{1,0:T(8,128)(2,1)} %refs_0_.4, bf16[512,128]{1,0:T(8,128)(2,1)} %refs_1_.5, bf16[4096,512]{1,0:T(8,128)(2,1)} %refs_1_.6, bf16[4096,128]{1,0:T(8,128)(2,1)} %refs_2_.4, bf16[4096,128]{1,0:T(8,128)(2,1)} %refs_3_.3), custom_call_target="tpu_custom_call" | custom-call | bytes 2097152 | tf_op jit(solution)/shard_map/pack_first/pallas_call | solution.py:328
  3.6 4.9 %collective-permute-start = (bf16[512,256]{1,0:T(8,128)(2,1)}, bf16[512,256]{1,0:T(8,128)(2,1)S(1)}, u32[]{:S(2)}, u32[]{:S(2)}) collective-permute-start(bf16[512,256]{1,0:T(8,128)(2,1)} %get-tuple-element.32), channel_id=1, source_target_pairs={{0,4},{4,8},{8,12},{1,5},{5,9},{9,13},{2,6},{6,10},{10,14},{3,7},{... | collective-permute-start | bytes 786440 | tf_op jit(solution)/shard_map/kv_forward/ppermute | solution.py:22
  8.5 3.3 %collective-permute-start.2 = (bf16[512,256]{1,0:T(8,128)(2,1)}, bf16[512,256]{1,0:T(8,128)(2,1)S(1)}, u32[]{:S(2)}, u32[]{:S(2)}) collective-permute-start(bf16[512,256]{1,0:T(8,128)(2,1)} %get-tuple-element.32), channel_id=1, source_target_pairs={{0,12},{1,13},{2,14},{3,15},{16,28},{17,29},{18,30},{19,31}} | collective-permute-start | bytes 786440 | tf_op jit(solution)/shard_map/kv_forward/ppermute | solution.py:22
  11.9 1.6 %collective-permute-start.6 = (bf16[512,768]{1,0:T(8,128)(2,1)}, bf16[512,768]{1,0:T(8,128)(2,1)S(1)}, u32[]{:S(2)}, u32[]{:S(2)}) collective-permute-start(bf16[512,768]{1,0:T(8,128)(2,1)} %get-tuple-element.47), channel_id=1, source_target_pairs={{0,2},{1,3},{2,0},{3,1},{4,6},{5,7},{6,4},{7,5},{8,10},{9,11},{10,... | collective-permute-start | bytes 2359304 | tf_op jit(solution)/shard_map/weight_exchange/ppermute | solution.py:26
  14.0 3.8 %pack_rest.1 = (bf16[1024,768]{1,0:T(8,128)(2,1)}, bf16[512,768]{1,0:T(8,128)(2,1)}) custom-call(s32[2]{0:T(128)} %pad_add_fusion.1.rows_ref, bf16[4096,512]{1,0:T(8,128)(2,1)} %refs_1_.6, bf16[4096,128]{1,0:T(8,128)(2,1)} %refs_2_.4, bf16[4096,128]{1,0:T(8,128)(2,1)} %refs_3_.3), custom_call_target="tpu_custom_call" | custom-call | bytes 4718592 | tf_op jit(solution)/shard_map/pack_rest/pallas_call | solution.py:328
  18.6 1.3 %collective-permute-start.1 = (bf16[512,256]{1,0:T(8,128)(2,1)S(1)}, bf16[512,256]{1,0:T(8,128)(2,1)S(1)}, u32[]{:S(2)}, u32[]{:S(2)}) collective-permute-start(bf16[512,256]{1,0:T(8,128)(2,1)S(1)} %collective-permute-done.kv1.refs_2_), channel_id=1, source_target_pairs={{0,4},{4,8},{8,12},{1,5},{5,9},{9,13},{2,6},{6,10},{10,14},{3,7},{... | collective-permute-start | bytes 786440 | tf_op jit(solution)/shard_map/kv_forward/ppermute | solution.py:22
  22.1 3.6 %near_stats.1 = (f32[4,512]{1,0:T(4,128)S(1)}, f32[4,512]{1,0:T(4,128)S(1)}, f32[4,512]{1,0:T(4,128)S(1)}, bf16[2048,128]{1,0:T(8,128)(2,1)S(1)}, bf16[2048,128]{1,0:T(8,128)(2,1)S(1)}) custom-call(s32[4,16]{1,0:T(4,128)S(1)} %fusion.4.flag_ref.refs_0_, bf16[512,512]{1,0:T(8,128)(2,1)S(1)} %copy-done.5, bf16[512,512]{1,0:T(8,128)(2,1)S(1)} %copy-done.6, ...), custom_call_target="tpu_custom_call" | custom-call | tf_op jit(solution)/shard_map/near_stats/pallas_call | solution.py:269
  26.0 5.5 %far_stats.1 = (f32[3,4,512]{2,1,0:T(4,128)S(1)}, f32[4,128,512]{2,1,0:T(8,128)S(1)}, bf16[512,256]{1,0:T(8,128)(2,1)S(1)}) custom-call(s32[4,16]{1,0:T(4,128)S(1)} %fusion.4.flag_ref.refs_0_, bf16[2048,128]{1,0:T(8,128)(2,1)S(1)} %get-tuple-element.38.refs_1_.qs, bf16[2048,128]{1,0:T(8,128)(2,1)S(1)} %get-tuple-element.39.refs_2_.gs, ...), custom_call_target="tpu_custom_call" | custom-call | tf_op jit(solution)/shard_map/far_stats/pallas_call | solution.py:269
  31.5 1.1 %collective-permute-done.6.refs_5_.refs_7_ = bf16[512,768]{1,0:T(8,128)(2,1)S(1)} collective-permute-done((bf16[512,768]{1,0:T(8,128)(2,1)}, bf16[512,768]{1,0:T(8,128)(2,1)S(1)}, u32[]{:S(2)}, u32[]{:S(2)}) %collective-permute-start.6) | collective-permute-done | bytes 786464 | tf_op jit(solution)/shard_map/weight_exchange/ppermute | solution.py:26
  32.6 1.5 %collective-permute-start.10 = (bf16[512,768]{1,0:T(8,128)(2,1)S(1)}, bf16[512,768]{1,0:T(8,128)(2,1)S(1)}, u32[]{:S(2)}, u32[]{:S(2)}) collective-permute-start(bf16[512,768]{1,0:T(8,128)(2,1)S(1)} %collective-permute-done.6.refs_5_.refs_7_), channel_id=1, source_target_pairs={{0,16},{16,0},{1,17},{17,1},{2,18},{18,2},{3,19},{19,3},{4,20},{20... | collective-permute-start | bytes 2359304 | tf_op jit(solution)/shard_map/weight_exchange/ppermute | solution.py:483
  34.1 1.3 %collective-permute-start.8 = (bf16[512,256]{1,0:T(8,128)(2,1)S(1)}, bf16[512,256]{1,0:T(8,128)(2,1)S(1)}, u32[]{:S(2)}, u32[]{:S(2)}) collective-permute-start(bf16[512,256]{1,0:T(8,128)(2,1)S(1)} %get-tuple-element.50), channel_id=1, source_target_pairs={{4,0},{8,4},{12,8},{5,1},{9,5},{13,9},{6,2},{10,6},{14,10},{7,3},{... | collective-permute-start | bytes 786440 | tf_op jit(solution)/shard_map/kv_return/ppermute | solution.py:22
  35.4 2.5 %longest_gradients.1 = (bf16[512,256]{1,0:T(8,128)(2,1)S(1)}, f32[4,128,512]{2,1,0:T(8,128)S(1)}) custom-call(s32[4,16]{1,0:T(4,128)S(1)} %fusion.4.flag_ref.refs_0_, bf16[2048,128]{1,0:T(8,128)(2,1)S(1)} %get-tuple-element.38.refs_1_.qs, bf16[2048,128]{1,0:T(8,128)(2,1)S(1)} %get-tuple-element.39.refs_2_.gs, f32[3,4,512]{2,1,0:T(4,128)S(1)} %get-tuple-element.43.stat_ref, ...), custom_call_target="tpu_custom_call" | custom-call | tf_op jit(solution)/shard_map/longest_gradients/pallas_call | solution.py:269
  37.9 1.5 %collective-permute-start.7 = (bf16[512,256]{1,0:T(8,128)(2,1)S(1)}, bf16[512,256]{1,0:T(8,128)(2,1)S(1)}, u32[]{:S(2)}, u32[]{:S(2)}) collective-permute-start(bf16[512,256]{1,0:T(8,128)(2,1)S(1)} %get-tuple-element.48), channel_id=1, source_target_pairs={{12,0},{13,1},{14,2},{15,3},{28,16},{29,17},{30,18},{31,19}} | collective-permute-start | bytes 786440 | tf_op jit(solution)/shard_map/kv_return/ppermute | solution.py:22
  39.4 5.3 %near_gradients.1 = (f32[512,256]{1,0:T(8,128)S(1)}, f32[512,256]{1,0:T(8,128)S(1)}, bf16[512,512]{1,0:T(8,128)(2,1)S(1)}) custom-call(s32[4,16]{1,0:T(4,128)S(1)} %fusion.4.flag_ref.refs_0_, bf16[2048,128]{1,0:T(8,128)(2,1)S(1)} %get-tuple-element.38.refs_1_.qs, bf16[2048,128]{1,0:T(8,128)(2,1)S(1)} %get-tuple-element.39.refs_2_.gs, ...), custom_call_target="tpu_custom_call" | custom-call | tf_op jit(solution)/shard_map/near_gradients/pallas_call | solution.py:269
  44.6 3.2 %collective-permute-done.8 = bf16[512,256]{1,0:T(8,128)(2,1)S(1)} collective-permute-done((bf16[512,256]{1,0:T(8,128)(2,1)S(1)}, bf16[512,256]{1,0:T(8,128)(2,1)S(1)}, u32[]{:S(2)}, u32[]{:S(2)}) %collective-permute-start.8) | collective-permute-done | bytes 262176 | tf_op jit(solution)/shard_map/kv_return/ppermute | solution.py:22
  47.9 1.3 %collective-permute-start.9 = (bf16[512,256]{1,0:T(8,128)(2,1)S(1)}, bf16[512,256]{1,0:T(8,128)(2,1)S(1)}, u32[]{:S(2)}, u32[]{:S(2)}) collective-permute-start(bf16[512,256]{1,0:T(8,128)(2,1)S(1)} %add_convert_fusion.1), channel_id=1, source_target_pairs={{4,0},{8,4},{12,8},{5,1},{9,5},{13,9},{6,2},{10,6},{14,10},{7,3},{... | collective-permute-start | bytes 786440 | tf_op jit(solution)/shard_map/kv_return/ppermute | solution.py:22
  49.8 2.2 %collective-permute-done.7 = bf16[512,256]{1,0:T(8,128)(2,1)S(1)} collective-permute-done((bf16[512,256]{1,0:T(8,128)(2,1)S(1)}, bf16[512,256]{1,0:T(8,128)(2,1)S(1)}, u32[]{:S(2)}, u32[]{:S(2)}) %collective-permute-start.7) | collective-permute-done | bytes 262176 | tf_op jit(solution)/shard_map/kv_return/ppermute | solution.py:22
  52.0 1.5 %collective-permute-start.5 = (bf16[512,512]{1,0:T(8,128)(2,1)S(1)}, bf16[512,512]{1,0:T(8,128)(2,1)S(1)}, u32[]{:S(2)}, u32[]{:S(2)}) collective-permute-start(bf16[512,512]{1,0:T(8,128)(2,1)S(1)} %get-tuple-element.46.refs_0_), channel_id=1, source_target_pairs={{0,2},{1,3},{2,0},{3,1},{4,6},{5,7},{6,4},{7,5},{8,10},{9,11},{10,... | collective-permute-start | bytes 1572872 | tf_op jit(solution)/shard_map/query_grad_gather/ppermute | solution.py:26
  53.5 3.2 %collective-permute-done.9 = bf16[512,256]{1,0:T(8,128)(2,1)S(1)} collective-permute-done((bf16[512,256]{1,0:T(8,128)(2,1)S(1)}, bf16[512,256]{1,0:T(8,128)(2,1)S(1)}, u32[]{:S(2)}, u32[]{:S(2)}) %collective-permute-start.9) | collective-permute-done | bytes 262176 | tf_op jit(solution)/shard_map/kv_return/ppermute | solution.py:22
  56.7 1.6 %collective-permute-start.12 = (bf16[512,256]{1,0:T(8,128)(2,1)S(1)}, bf16[512,256]{1,0:T(8,128)(2,1)S(1)}, u32[]{:S(2)}, u32[]{:S(2)}) collective-permute-start(bf16[512,256]{1,0:T(8,128)(2,1)S(1)} %add_convert_fusion.refs_1_), channel_id=1, source_target_pairs={{0,2},{1,3},{2,0},{3,1},{4,6},{5,7},{6,4},{7,5},{8,10},{9,11},{10,... | collective-permute-start | bytes 786440 | tf_op jit(solution)/shard_map/kv_grad_gather/ppermute | solution.py:26
  58.3 7.7 %collective-permute-done.5.refs_4_ = bf16[512,512]{1,0:T(8,128)(2,1)S(1)} collective-permute-done((bf16[512,512]{1,0:T(8,128)(2,1)S(1)}, bf16[512,512]{1,0:T(8,128)(2,1)S(1)}, u32[]{:S(2)}, u32[]{:S(2)}) %collective-permute-start.5) | collective-permute-done | bytes 524320 | tf_op jit(solution)/shard_map/query_grad_gather/ppermute | solution.py:26
  66.6 2.9 %query_product.1.refs_0_ = f32[512,1024]{1,0:T(8,128)S(1)} custom-call(s32[2]{0:T(128)S(1)} %pad_add_fusion.place_ref, bf16[512,512]{1,0:T(8,128)(2,1)S(1)} %get-tuple-element.46.refs_0_, bf16[4096,512]{1,0:T(8,128)(2,1)S(1)} %copy-done, bf16[512,512]{1,0:T(8,128)(2,1)S(1)} %collective-permute-done.3.refs_2_, ...), custom_call_target="tpu_custom_call" | custom-call | bytes 2097152 | tf_op jit(solution)/shard_map/query_product/pallas_call | solution.py:269
  69.7 1.5 %collective-permute-done.16.refs_10_ = bf16[512,256]{1,0:T(8,128)(2,1)S(1)} collective-permute-done((bf16[512,256]{1,0:T(8,128)(2,1)S(1)}, bf16[512,256]{1,0:T(8,128)(2,1)S(1)}, u32[]{:S(2)}, u32[]{:S(2)}) %collective-permute-start.16) | collective-permute-done | bytes 262176 | tf_op jit(solution)/shard_map/kv_grad_gather/ppermute | solution.py:26
  71.2 4.2 %last_product.1 = bf16[512,1024]{1,0:T(8,128)(2,1)} custom-call(s32[2]{0:T(128)S(1)} %pad_add_fusion.place_ref, f32[512,1024]{1,0:T(8,128)S(1)} %query_product.1.refs_0_, bf16[512,256]{1,0:T(8,128)(2,1)S(1)} %add_convert_fusion.refs_1_, bf16[4096,128]{1,0:T(8,128)(2,1)S(1)} %copy-done.1, bf16[4096,128]{1,0:T(8,128)(2,1)S(1)} %copy-done.2, ...), custom_call_target="tpu_custom_call" | custom-call | bytes 1048576 | tf_op jit(solution)/shard_map/last_product/pallas_call | solution.py:269
  (44 shorter events, 5.9 us)
Async XLA Ops:
  3.6 15.1 %collective-permute-start = (bf16[512,256]{1,0:T(8,128)(2,1)}, bf16[512,256]{1,0:T(8,128)(2,1)S(1)}, u32[]{:S(2)}, u32[]{:S(2)}) collective-permute-start(bf16[512,256]{1,0:T(8,128)(2,1)} %get-tuple-element.32), channel_id=1, source_target_pairs={{0,4},{4,8},{8,12},{1,5},{5,9},{9,13},{2,6},{6,10},{10,14},{3,7},{... | collective-permute-start | bytes 786440 | tf_op jit(solution)/shard_map/kv_forward/ppermute | solution.py:22
  8.5 17.2 %collective-permute-start.2 = (bf16[512,256]{1,0:T(8,128)(2,1)}, bf16[512,256]{1,0:T(8,128)(2,1)S(1)}, u32[]{:S(2)}, u32[]{:S(2)}) collective-permute-start(bf16[512,256]{1,0:T(8,128)(2,1)} %get-tuple-element.32), channel_id=1, source_target_pairs={{0,12},{1,13},{2,14},{3,15},{16,28},{17,29},{18,30},{19,31}} | collective-permute-start | bytes 786440 | tf_op jit(solution)/shard_map/kv_forward/ppermute | solution.py:22
  11.9 20.7 %collective-permute-start.6 = (bf16[512,768]{1,0:T(8,128)(2,1)}, bf16[512,768]{1,0:T(8,128)(2,1)S(1)}, u32[]{:S(2)}, u32[]{:S(2)}) collective-permute-start(bf16[512,768]{1,0:T(8,128)(2,1)} %get-tuple-element.47), channel_id=1, source_target_pairs={{0,2},{1,3},{2,0},{3,1},{4,6},{5,7},{6,4},{7,5},{8,10},{9,11},{10,... | collective-permute-start | bytes 2359304 | tf_op jit(solution)/shard_map/weight_exchange/ppermute | solution.py:26
  14.0 4.6 %copy-start.7 = (s32[4,8]{1,0:T(4,128)S(1)}, s32[4,8]{1,0:T(4,128)}, u32[]{:S(2)}) copy-start(s32[4,8]{1,0:T(4,128)} %param.12) | copy-start | bytes 388
  14.0 6.1 %copy-start.3 = (bf16[512,128]{1,0:T(8,128)(2,1)S(1)}, bf16[512,128]{1,0:T(8,128)(2,1)}, u32[]{:S(2)}) copy-start(bf16[512,128]{1,0:T(8,128)(2,1)} %refs_0_.4) | copy-start | bytes 393220
  14.0 6.1 %copy-start.4 = (bf16[512,128]{1,0:T(8,128)(2,1)S(1)}, bf16[512,128]{1,0:T(8,128)(2,1)}, u32[]{:S(2)}) copy-start(bf16[512,128]{1,0:T(8,128)(2,1)} %refs_1_.5) | copy-start | bytes 393220
  17.8 48.8 %collective-permute-start.4 = (bf16[1024,768]{1,0:T(8,128)(2,1)}, bf16[1024,768]{1,0:T(8,128)(2,1)S(1)}, u32[]{:S(2)}, u32[]{:S(2)}) collective-permute-start(bf16[1024,768]{1,0:T(8,128)(2,1)} %get-tuple-element.36), channel_id=1, source_target_pairs={{0,1},{1,0},{2,3},{3,2},{4,5},{5,4},{6,7},{7,6},{8,9},{9,8},{10,11... | collective-permute-start | bytes 4718600 | tf_op jit(solution)/shard_map/weight_exchange/ppermute | solution.py:26
  17.9 31.3 %collective-permute-start.14 = (bf16[512,768]{1,0:T(8,128)(2,1)}, bf16[512,768]{1,0:T(8,128)(2,1)}, u32[]{:S(2)}, u32[]{:S(2)}) collective-permute-start(bf16[512,768]{1,0:T(8,128)(2,1)} %get-tuple-element.56), channel_id=1, source_target_pairs={{0,3},{1,2},{2,1},{3,0},{4,7},{5,6},{6,5},{7,4},{8,11},{9,10},{10,... | collective-permute-start | bytes 2359304 | tf_op jit(solution)/shard_map/weight_exchange/ppermute | solution.py:26
  18.6 7.4 %collective-permute-start.1 = (bf16[512,256]{1,0:T(8,128)(2,1)S(1)}, bf16[512,256]{1,0:T(8,128)(2,1)S(1)}, u32[]{:S(2)}, u32[]{:S(2)}) collective-permute-start(bf16[512,256]{1,0:T(8,128)(2,1)S(1)} %collective-permute-done.kv1.refs_2_), channel_id=1, source_target_pairs={{0,4},{4,8},{8,12},{1,5},{5,9},{9,13},{2,6},{6,10},{10,14},{3,7},{... | collective-permute-start | bytes 786440 | tf_op jit(solution)/shard_map/kv_forward/ppermute | solution.py:22
  20.0 1.0 %copy-start.5 = (bf16[512,512]{1,0:T(8,128)(2,1)S(1)}, bf16[512,512]{1,0:T(8,128)(2,1)}, u32[]{:S(2)}) copy-start(bf16[512,512]{1,0:T(8,128)(2,1)} %query_ref) | copy-start | bytes 1572868
  32.6 24.0 %collective-permute-start.10 = (bf16[512,768]{1,0:T(8,128)(2,1)S(1)}, bf16[512,768]{1,0:T(8,128)(2,1)S(1)}, u32[]{:S(2)}, u32[]{:S(2)}) collective-permute-start(bf16[512,768]{1,0:T(8,128)(2,1)S(1)} %collective-permute-done.6.refs_5_.refs_7_), channel_id=1, source_target_pairs={{0,16},{16,0},{1,17},{17,1},{2,18},{18,2},{3,19},{19,3},{4,20},{20... | collective-permute-start | bytes 2359304 | tf_op jit(solution)/shard_map/weight_exchange/ppermute | solution.py:483
  34.1 13.7 %collective-permute-start.8 = (bf16[512,256]{1,0:T(8,128)(2,1)S(1)}, bf16[512,256]{1,0:T(8,128)(2,1)S(1)}, u32[]{:S(2)}, u32[]{:S(2)}) collective-permute-start(bf16[512,256]{1,0:T(8,128)(2,1)S(1)} %get-tuple-element.50), channel_id=1, source_target_pairs={{4,0},{8,4},{12,8},{5,1},{9,5},{13,9},{6,2},{10,6},{14,10},{7,3},{... | collective-permute-start | bytes 786440 | tf_op jit(solution)/shard_map/kv_return/ppermute | solution.py:22
  37.9 14.1 %collective-permute-start.7 = (bf16[512,256]{1,0:T(8,128)(2,1)S(1)}, bf16[512,256]{1,0:T(8,128)(2,1)S(1)}, u32[]{:S(2)}, u32[]{:S(2)}) collective-permute-start(bf16[512,256]{1,0:T(8,128)(2,1)S(1)} %get-tuple-element.48), channel_id=1, source_target_pairs={{12,0},{13,1},{14,2},{15,3},{28,16},{29,17},{30,18},{31,19}} | collective-permute-start | bytes 786440 | tf_op jit(solution)/shard_map/kv_return/ppermute | solution.py:22
  39.4 27.3 %copy-start = (bf16[4096,512]{1,0:T(8,128)(2,1)S(1)}, bf16[4096,512]{1,0:T(8,128)(2,1)}, u32[]{:S(2)}) copy-start(bf16[4096,512]{1,0:T(8,128)(2,1)} %refs_1_.6) | copy-start | bytes 12582916
  47.9 8.7 %collective-permute-start.9 = (bf16[512,256]{1,0:T(8,128)(2,1)S(1)}, bf16[512,256]{1,0:T(8,128)(2,1)S(1)}, u32[]{:S(2)}, u32[]{:S(2)}) collective-permute-start(bf16[512,256]{1,0:T(8,128)(2,1)S(1)} %add_convert_fusion.1), channel_id=1, source_target_pairs={{4,0},{8,4},{12,8},{5,1},{9,5},{13,9},{6,2},{10,6},{14,10},{7,3},{... | collective-permute-start | bytes 786440 | tf_op jit(solution)/shard_map/kv_return/ppermute | solution.py:22
  49.2 20.4 %collective-permute-start.15 = (bf16[512,768]{1,0:T(8,128)(2,1)}, bf16[512,768]{1,0:T(8,128)(2,1)S(1)}, u32[]{:S(2)}, u32[]{:S(2)}) collective-permute-start(bf16[512,768]{1,0:T(8,128)(2,1)} %collective-permute-done.14.refs_11_), channel_id=1, source_target_pairs={{0,16},{16,0},{1,17},{17,1},{2,18},{18,2},{3,19},{19,3},{4,20},{20... | collective-permute-start | bytes 2359304 | tf_op jit(solution)/shard_map/weight_exchange/ppermute | solution.py:483
  52.0 14.0 %collective-permute-start.5 = (bf16[512,512]{1,0:T(8,128)(2,1)S(1)}, bf16[512,512]{1,0:T(8,128)(2,1)S(1)}, u32[]{:S(2)}, u32[]{:S(2)}) collective-permute-start(bf16[512,512]{1,0:T(8,128)(2,1)S(1)} %get-tuple-element.46.refs_0_), channel_id=1, source_target_pairs={{0,2},{1,3},{2,0},{3,1},{4,6},{5,7},{6,4},{7,5},{8,10},{9,11},{10,... | collective-permute-start | bytes 1572872 | tf_op jit(solution)/shard_map/query_grad_gather/ppermute | solution.py:26
  56.6 9.4 %collective-permute-start.3 = (bf16[512,512]{1,0:T(8,128)(2,1)S(1)}, bf16[512,512]{1,0:T(8,128)(2,1)S(1)}, u32[]{:S(2)}, u32[]{:S(2)}) collective-permute-start(bf16[512,512]{1,0:T(8,128)(2,1)S(1)} %get-tuple-element.46.refs_0_), channel_id=1, source_target_pairs={{0,1},{1,0},{2,3},{3,2},{4,5},{5,4},{6,7},{7,6},{8,9},{9,8},{10,11... | collective-permute-start | bytes 1572872 | tf_op jit(solution)/shard_map/query_grad_gather/ppermute | solution.py:26
  56.7 12.9 %collective-permute-start.12 = (bf16[512,256]{1,0:T(8,128)(2,1)S(1)}, bf16[512,256]{1,0:T(8,128)(2,1)S(1)}, u32[]{:S(2)}, u32[]{:S(2)}) collective-permute-start(bf16[512,256]{1,0:T(8,128)(2,1)S(1)} %add_convert_fusion.refs_1_), channel_id=1, source_target_pairs={{0,2},{1,3},{2,0},{3,1},{4,6},{5,7},{6,4},{7,5},{8,10},{9,11},{10,... | collective-permute-start | bytes 786440 | tf_op jit(solution)/shard_map/kv_grad_gather/ppermute | solution.py:26
  66.0 3.7 %collective-permute-start.13 = (bf16[512,512]{1,0:T(8,128)(2,1)S(1)}, bf16[512,512]{1,0:T(8,128)(2,1)S(1)}, u32[]{:S(2)}, u32[]{:S(2)}) collective-permute-start(bf16[512,512]{1,0:T(8,128)(2,1)S(1)} %collective-permute-done.5.refs_4_), channel_id=1, source_target_pairs={{0,1},{1,0},{2,3},{3,2},{4,5},{5,4},{6,7},{7,6},{8,9},{9,8},{10,11... | collective-permute-start | bytes 1572872 | tf_op jit(solution)/shard_map/query_grad_gather/ppermute | solution.py:26
  66.1 5.1 %copy-start.1 = (bf16[4096,128]{1,0:T(8,128)(2,1)S(1)}, bf16[4096,128]{1,0:T(8,128)(2,1)}, u32[]{:S(2)}) copy-start(bf16[4096,128]{1,0:T(8,128)(2,1)} %refs_2_.4) | copy-start | bytes 3145732
  66.1 5.1 %copy-start.2 = (bf16[4096,128]{1,0:T(8,128)(2,1)S(1)}, bf16[4096,128]{1,0:T(8,128)(2,1)}, u32[]{:S(2)}) copy-start(bf16[4096,128]{1,0:T(8,128)(2,1)} %refs_3_.3) | copy-start | bytes 3145732
  66.1 3.6 %collective-permute-start.11 = (bf16[512,256]{1,0:T(8,128)(2,1)S(1)}, bf16[512,256]{1,0:T(8,128)(2,1)S(1)}, u32[]{:S(2)}, u32[]{:S(2)}) collective-permute-start(bf16[512,256]{1,0:T(8,128)(2,1)S(1)} %add_convert_fusion.refs_1_), channel_id=1, source_target_pairs={{0,1},{1,0},{2,3},{3,2},{4,5},{5,4},{6,7},{7,6},{8,9},{9,8},{10,11... | collective-permute-start | bytes 786440 | tf_op jit(solution)/shard_map/kv_grad_gather/ppermute | solution.py:26
  69.6 1.6 %collective-permute-start.16 = (bf16[512,256]{1,0:T(8,128)(2,1)S(1)}, bf16[512,256]{1,0:T(8,128)(2,1)S(1)}, u32[]{:S(2)}, u32[]{:S(2)}) collective-permute-start(bf16[512,256]{1,0:T(8,128)(2,1)S(1)} %collective-permute-done.12.refs_6_), channel_id=1, source_target_pairs={{0,1},{1,0},{2,3},{3,2},{4,5},{5,4},{6,7},{7,6},{8,9},{9,8},{10,11... | collective-permute-start | bytes 786440 | tf_op jit(solution)/shard_map/kv_grad_gather/ppermute | solution.py:26
  (1 other events, 1.0 us)
